TPU v7x, 256 devices: a whole 4x4x8 slice. The times are simulated.
256 devices in a mesh: rep: 4 (over x), ep: 64 (over z, y, core).
Axes of the slice: x: 4, y: 4, z: 8, core: 2. Of those that a mesh axis runs over, the one named last changes fastest.
Arguments:
- out_grad: bfloat16 [4096, 128, 256], P(('rep', 'ep')), may hold values from -3 to 3
- routes: int32 [4096, 2], P(('rep', 'ep')), may hold values from 0 to 63, all different within a row; in each aligned block of 16 rows (0 to 15, 16 to 31, ...) at most 2 rows name the same one
- gates: bfloat16 [4096, 2], P(('rep', 'ep')), may hold values from 0.19921875 to 1
- stash: bfloat16 [4, 64, 64, 2, 128, 256], P('rep', 'ep'), may hold values from -6 to 6
- weights: bfloat16 [64, 9, 4, 32, 32], P('ep'), may hold values from -0.375 to 0.375
Outputs:
- in_grad: bfloat16 [4096, 128, 256], P(('rep', 'ep'))
- weight_grad: float32 [64, 9, 4, 32, 32], P('ep')
Inputs may be any that keep to these rules, and one draw needn't show every extreme that they name: Among the routes of the patches of one device, at most 2 name one expert, and some device reaches 2; the 2 experts of a patch differ.
All inputs are finite; a program needn't handle non-finite values.
Results may differ from a plain program's by a relative error of at most 0.014.
Values may be sent and summed in bfloat16 or wider, within the bound.
No kernel may reach another device: no remote copies, remote signals or barrier semaphores. Data moves between devices by JAX's collectives and lax.ppermute only.
A program may use at most 192 MiB of HBM per device.

v0:
```python
import jax
import jax.numpy as jnp
from jax import lax
from jax.sharding import PartitionSpec as P

SIDE = 16


tap_offsets = [(-1, -1), (-1, 0), (-1, 1), (0, -1), (0, 0), (0, 1), (1, -1), (1, 0), (1, 1)]
slot_block = 8


def shift_cells(values, row_step, col_step, side_cells):
    position = jnp.arange(side_cells * side_cells, dtype=jnp.int32)
    cell_row = position // side_cells
    cell_col = position % side_cells
    inside = (
        (cell_row + row_step >= 0)
        & (cell_row + row_step < side_cells)
        & (cell_col + col_step >= 0)
        & (cell_col + col_step < side_cells)
    )
    rolled = jnp.roll(values, -(row_step * side_cells + col_step), axis=-1)
    return jnp.where(inside, rolled, jnp.zeros_like(rolled))


def input_terms(grad_rows, kernel, einsum_form, groups, group_width):
    row_count, channels, positions = grad_rows.shape
    grouped_grad = grad_rows.reshape(row_count, groups, group_width, positions)
    summed = jnp.zeros((row_count, groups, group_width, positions), jnp.float32)
    for tap_index, (row_step, col_step) in enumerate(tap_offsets):
        tap_kernel = jnp.take(kernel, tap_index, axis=kernel.ndim - 4)
        mixed = jnp.einsum(
            einsum_form, tap_kernel, grouped_grad, preferred_element_type=jnp.float32
        )
        summed = summed + shift_cells(mixed, -row_step, -col_step, SIDE)
    return summed.reshape(row_count, channels, positions).astype(jnp.bfloat16)


def kernel_terms(grad_block, input_block, groups, group_width):
    row_count, channels, positions = grad_block.shape
    grouped_grad = grad_block.reshape(row_count, groups, group_width, positions)
    grouped_input = input_block.reshape(row_count, groups, group_width, positions)
    return jnp.stack(
        [
            jnp.einsum(
                "sgdp,sgcp->gdc",
                grouped_grad,
                shift_cells(grouped_input, row_step, col_step, SIDE),
                preferred_element_type=jnp.float32,
            )
            for row_step, col_step in tap_offsets
        ]
    )


def per_device(out_grad, routes, gates, stash, weights):
    n_ep = lax.axis_size("ep")
    token_rows, top_k = routes.shape
    capacity = stash.shape[3]
    channels = out_grad.shape[1]
    positions = out_grad.shape[2]
    groups = weights.shape[2]
    group_width = weights.shape[3]
    route_count = token_rows * top_k
    total_slots = n_ep * capacity
    route_experts = routes.reshape(route_count)
    onehot = (route_experts[:, None] == jnp.arange(n_ep, dtype=jnp.int32)[None, :]).astype(
        jnp.int32
    )
    earlier = jnp.cumsum(onehot, 0) - onehot
    slot_index = jnp.sum(earlier * onehot, 1)
    target = route_experts * capacity + slot_index
    scaled = (
        gates.astype(jnp.float32)[:, :, None, None] * out_grad.astype(jnp.float32)[:, None]
    ).astype(jnp.bfloat16)
    scaled = scaled.reshape(route_count, channels, positions)
    outgoing = jnp.zeros((total_slots, channels, positions), jnp.bfloat16).at[target].set(scaled)
    outgoing = outgoing.reshape(n_ep, capacity, channels, positions)
    inputs = stash.reshape(total_slots, channels, positions)
    kernel = weights[0]
    incoming = lax.all_to_all(outgoing, "ep", split_axis=0, concat_axis=0, tiled=True)
    incoming = incoming.reshape(total_slots, channels, positions)
    arrangement = jnp.arange(total_slots, dtype=jnp.int32)
    ordered_grad = incoming
    block_count = total_slots // slot_block
    slot_grads = jnp.zeros((total_slots, channels, positions), jnp.bfloat16)

    def step_fn(block_index, carried):
        weight_sum, grads_out = carried
        first_row = block_index * slot_block
        grad_block = lax.dynamic_slice_in_dim(ordered_grad, first_row, slot_block, 0)
        input_block = lax.dynamic_slice_in_dim(inputs, first_row, slot_block, 0)
        weight_sum = weight_sum + kernel_terms(grad_block, input_block, groups, group_width)
        block_grads = input_terms(grad_block, kernel, "gdc,sgdp->sgcp", groups, group_width)
        grads_out = lax.dynamic_update_slice_in_dim(grads_out, block_grads, first_row, 0)
        return (weight_sum, grads_out)

    weight_zero = jnp.zeros((9, groups, group_width, group_width), jnp.float32)
    weight_sum, slot_grads = lax.fori_loop(0, block_count, step_fn, (weight_zero, slot_grads))
    placed = (
        jnp.zeros((total_slots, channels, positions), jnp.bfloat16).at[arrangement].set(slot_grads)
    )
    placed = placed.reshape(n_ep, capacity, channels, positions)
    returned = lax.all_to_all(placed, "ep", split_axis=0, concat_axis=0, tiled=True)
    route_grad = returned.reshape(total_slots, channels, positions)[target]
    in_grad = jnp.sum(
        route_grad.reshape(token_rows, top_k, channels, positions).astype(jnp.float32), 1
    ).astype(jnp.bfloat16)
    weight_grad = lax.psum(weight_sum.astype(jnp.bfloat16), "rep").astype(jnp.float32)
    return (in_grad, weight_grad[None])


def solution(mesh):
    return jax.shard_map(
        per_device,
        mesh=mesh,
        in_specs=(
            P(("rep", "ep"), None, None),
            P(("rep", "ep"), None),
            P(("rep", "ep"), None),
            P("rep", "ep", None, None, None, None),
            P("ep", None, None, None, None),
        ),
        out_specs=(P(("rep", "ep"), None, None), P("ep", None, None, None, None)),
        check_vma=False,
    )
```

profile of v0, /device:TPU:1, one launch (start us, length us, event | category | flops | bytes accessed | tf_op | source)
XLA Modules:
  0.0 700.9 jit_solution(2004057411121918697)
XLA Ops:
  9.2 2.8 convert_element_type.31
  12.8 2.1 fusion.48
  15.0 4.3 broadcast.121.clone.1
  19.2 5.4 scatter_fusion
  24.7 13.4 %all-to-all-start = ((bf16[64,2,128,256]{3,2,1,0:T(8,128)(2,1)}), bf16[64,2,128,256]{3,2,1,0:T(8,128)(2,1)}, u32[]{:S(2)}, u32[]{:S(2)}) async-start(bf16[64,2,128,256]{3,2,1,0:T(8,128)(2,1)} %bitcast.293), calls=%async_computation | async-start | bytes 16777216 | tf_op jit(solution)/shard_map/all_to_all | solution.py:82
  38.4 182.2 %all-to-all-done = bf16[64,2,128,256]{3,2,1,0:T(8,128)(2,1)} async-done(((bf16[64,2,128,256]{3,2,1,0:T(8,128)(2,1)}), bf16[64,2,128,256]{3,2,1,0:T(8,128)(2,1)}, u32[]{:S(2)}, u32[]{:S(2)}) %all-to-all-start) | async-done | bytes 8388640 | tf_op jit(solution)/shard_map/all_to_all | solution.py:82
  220.6 4.3 broadcast.121.clone
  224.9 243.3 %while.27 = (s32[]{:T(128)}, f32[9,4,32,32]{3,2,1,0:T(8,128)S(1)}, bf16[128,128,256]{2,1,0:T(8,128)(2,1)}, bf16[128,128,256]{2,1,0:T(8,128)(2,1)}, bf16[128,128,...) while((s32[]{:T(128)}, f32[9,4,32,32]{3,2,1,0:T(8,128)S(1)}, ...), condition=%wide.region_4.14_spmd.clone, body=%wide.region_3.13_spmd.clone.sunk | while | flops 319674112 | bytes 60953620 | solution.py:100
  224.9 1.1 constant_dynamic-slice_fusion.3
  230.6 2.2 fusion.238
  232.9 1.9 constant_dynamic-update-slice_fusion.2
  240.1 1.1 constant_dynamic-slice_fusion.3
  245.8 2.2 fusion.238
  248.1 1.9 constant_dynamic-update-slice_fusion.2
  255.3 1.1 constant_dynamic-slice_fusion.3
  261.0 2.2 fusion.238
  263.3 1.9 constant_dynamic-update-slice_fusion.2
  270.5 1.1 constant_dynamic-slice_fusion.3
  276.2 2.2 fusion.238
  278.5 1.9 constant_dynamic-update-slice_fusion.2
  285.7 1.1 constant_dynamic-slice_fusion.3
  291.4 2.2 fusion.238
  293.7 1.9 constant_dynamic-update-slice_fusion.2
  300.9 1.1 constant_dynamic-slice_fusion.3
  306.6 2.2 fusion.238
  308.9 1.9 constant_dynamic-update-slice_fusion.2
  316.1 1.1 constant_dynamic-slice_fusion.3
  321.9 2.2 fusion.238
  324.1 1.9 constant_dynamic-update-slice_fusion.2
  331.3 1.1 constant_dynamic-slice_fusion.3
  337.1 2.2 fusion.238
  339.3 1.9 constant_dynamic-update-slice_fusion.2
  346.5 1.1 constant_dynamic-slice_fusion.3
  352.3 2.2 fusion.238
  354.5 1.9 constant_dynamic-update-slice_fusion.2
  361.7 1.1 constant_dynamic-slice_fusion.3
  367.5 2.2 fusion.238
  369.7 1.9 constant_dynamic-update-slice_fusion.2
  376.9 1.1 constant_dynamic-slice_fusion.3
  382.7 2.2 fusion.238
  385.0 1.9 constant_dynamic-update-slice_fusion.2
  392.1 1.1 constant_dynamic-slice_fusion.3
  397.9 2.2 fusion.238
  400.2 1.9 constant_dynamic-update-slice_fusion.2
  407.3 1.1 constant_dynamic-slice_fusion.3
  413.1 2.2 fusion.238
  415.4 1.9 constant_dynamic-update-slice_fusion.2
  422.6 1.1 constant_dynamic-slice_fusion.3
  428.3 2.2 fusion.238
  430.6 1.9 constant_dynamic-update-slice_fusion.2
  437.8 1.1 constant_dynamic-slice_fusion.3
  443.5 2.2 fusion.238
  445.8 1.9 constant_dynamic-update-slice_fusion.2
  453.0 1.1 constant_dynamic-slice_fusion.3
  458.7 2.2 fusion.238
  461.0 2.0 constant_dynamic-update-slice_fusion.2
  468.2 4.3 broadcast.121
  472.5 23.5 %scatter_fusion.1 = bf16[128,128,256]{2,1,0:T(8,128)(2,1)} fusion(bf16[128,128,256]{2,1,0:T(8,128)(2,1)} %broadcast.121, s32[128]{0:T(128)S(1)} %iota.70, bf16[128,128,256]{2,1,0:T(8,128)(2,1)} %get-tuple-element.211), kind=kCustom, calls=%fused_computation.2 | custom fusion | bytes 25166336 | tf_op jit(solution)/shard_map/scatter | solution.py:102
  496.0 10.2 %all-to-all-start.1 = ((bf16[64,2,128,256]{3,2,1,0:T(8,128)(2,1)}), bf16[64,2,128,256]{3,2,1,0:T(8,128)(2,1)}, u32[]{:S(2)}, u32[]{:S(2)}) async-start(bf16[64,2,128,256]{3,2,1,0:T(8,128)(2,1)} %bitcast.291), calls=%async_computation.1 | async-start | bytes 16777216 | tf_op jit(solution)/shard_map/all_to_all | solution.py:105
  507.0 49.6 %all-reduce.2.cloned.1.call-done = bf16[1,9,4,32,32]{4,3,2,1,0:T(8,128)(2,1)} async-done(((bf16[1,9,4,32,32]{4,3,2,1,0:T(8,128)(2,1)}), bf16[1,9,4,32,32]{4,3,2,1,0:T(8,128)(2,1)}) %all-reduce.2.cloned.1.call-update) | async-done | bytes 73744 | tf_op jit(solution)/shard_map/psum | solution.py:110
  556.5 1.8 broadcast_in_dim.163
  558.4 130.1 %all-to-all-done.1 = bf16[64,2,128,256]{3,2,1,0:T(8,128)(2,1)} async-done(((bf16[64,2,128,256]{3,2,1,0:T(8,128)(2,1)}), bf16[64,2,128,256]{3,2,1,0:T(8,128)(2,1)}, u32[]{:S(2)}, u32[]{:S(2)}) %all-to-all-start.1) | async-done | bytes 8388640 | tf_op jit(solution)/shard_map/all_to_all | solution.py:105
  688.5 4.1 gather_fusion
  692.6 1.4 bitcast_reduce_fusion
  (837 shorter events, 160.0 us)
Async XLA Ops:
  24.7 13.5 %copy-start.1 = (bf16[1,9,4,32,32]{4,3,2,1,0:T(8,128)(2,1)S(1)}, bf16[1,9,4,32,32]{4,3,2,1,0:T(8,128)(2,1)}, u32[]{:S(2)}) copy-start(bf16[1,9,4,32,32]{4,3,2,1,0:T(8,128)(2,1)} %param.29) | copy-start | bytes 221188
  24.7 195.9 %all-to-all-start = ((bf16[64,2,128,256]{3,2,1,0:T(8,128)(2,1)}), bf16[64,2,128,256]{3,2,1,0:T(8,128)(2,1)}, u32[]{:S(2)}, u32[]{:S(2)}) async-start(bf16[64,2,128,256]{3,2,1,0:T(8,128)(2,1)} %bitcast.293), calls=%async_computation | async-start | bytes 16777216 | tf_op jit(solution)/shard_map/all_to_all | solution.py:82
  226.2 2.3 copy-start
  228.6 2.1 slice-start
  241.4 2.3 copy-start
  243.8 2.1 slice-start
  256.6 2.3 copy-start
  259.0 2.1 slice-start
  271.8 2.3 copy-start
  274.2 2.1 slice-start
  287.0 2.3 copy-start
  289.4 2.1 slice-start
  302.2 2.3 copy-start
  304.6 2.1 slice-start
  317.4 2.3 copy-start
  319.8 2.1 slice-start
  332.7 2.3 copy-start
  335.0 2.1 slice-start
  347.9 2.3 copy-start
  350.2 2.1 slice-start
  363.1 2.3 copy-start
  365.4 2.1 slice-start
  378.3 2.3 copy-start
  380.6 2.1 slice-start
  393.5 2.3 copy-start
  395.8 2.1 slice-start
  408.7 2.3 copy-start
  411.0 2.1 slice-start
  423.9 2.3 copy-start
  426.3 2.1 slice-start
  439.1 2.3 copy-start
  441.5 2.1 slice-start
  454.3 2.3 copy-start
  456.7 2.1 slice-start
  496.0 192.6 %all-to-all-start.1 = ((bf16[64,2,128,256]{3,2,1,0:T(8,128)(2,1)}), bf16[64,2,128,256]{3,2,1,0:T(8,128)(2,1)}, u32[]{:S(2)}, u32[]{:S(2)}) async-start(bf16[64,2,128,256]{3,2,1,0:T(8,128)(2,1)} %bitcast.291), calls=%async_computation.1 | async-start | bytes 16777216 | tf_op jit(solution)/shard_map/all_to_all | solution.py:105
  506.1 50.4 %all-reduce.2.cloned.1.call-start = ((), (), s32[]{:S(2)}) async-start(), calls=%async_computation.2 | async-start | bytes 589824 | tf_op jit(solution)/shard_map/psum | solution.py:110
Sparse Core Ops, SparseCore 0:
  509.9 46.6 all-reduce.1
where the time goes:
time: 706 us; the launch traced here: 701 us
  waiting for transfers between devices  362 us (51%)
  local copies, waits for them, and re-layouts  161 us (23%)
  matrix products  122 us (17%)
  starting transfers between devices  23.7 us (3%)
  other arithmetic  14.7 us (2%)
  between operations  14.1 us (2%)
    all_to_all x1, waiting for transfers between devices, per_device(): lax.all_to_all(outgoing, 'ep', split_axis=0, concat_axis=0, tiled=True)  182 us
    all_to_all x1, waiting for transfers between devices, per_device(): lax.all_to_all(placed, 'ep', split_axis=0, concat_axis=0, tiled=True)  130 us
    dot_general x144, matrix products, input_terms(): jnp.einsum(einsum_form, tap_kernel, grouped_grad, preferred_element_type=...  70.4 us
    slice x336, local copies, waits for them, and re-layouts, shift_cells(): rolled = jnp.roll(values, -(row_step * side_cells + col_step), axis=-1)  64.3 us
    dot_general x144, matrix products, kernel_terms(): jnp.einsum('sgdp,sgcp->gdc', grouped_grad, shift_cells(grouped_input, row...  51.3 us
    psum x1, waiting for transfers between devices, per_device(): lax.psum(weight_sum.astype(jnp.bfloat16), 'rep').astype(jnp.float32)  49.6 us
    dynamic_update_slice x16, local copies, waits for them, and re-layouts, step_fn(): lax.dynamic_update_slice_in_dim(grads_out, block_grads, first_row, 0)  30.7 us
    scatter x1, local copies, waits for them, and re-layouts, per_device(): jnp.zeros((total_slots, channels, positions), jnp.bfloat16).at[arrangement]  23.5 us
  transfers between devices with their start and end apart: 3, of which 3 were waited for; matrix products, arithmetic and copies ran while one was open for 0% of the time, Pallas kernels for 0%

commit v1 on v0

v1 whole, which is shorter than its diff:
```python
import functools

import jax
import jax.numpy as jnp
from jax import lax
from jax.experimental import pallas as pl
from jax.experimental.pallas import tpu as pltpu
from jax.sharding import PartitionSpec as P

SIDE = 16
CELLS = 256
GROUPS = 4
WIDTH = 32
CHANNELS = 128
NZ, NY, NC, NX = 8, 4, 2, 4
PIECE = 80
DEPTH = 6


def ep_perm(dz, dy, dc):
    pairs = []
    for z in range(NZ):
        for y in range(NY):
            for c in range(NC):
                to = ((z + dz) % NZ, (y + dy) % NY, c ^ dc)
                pairs.append(((z * NY + y) * NC + c, (to[0] * NY + to[1]) * NC + to[2]))
    return pairs


def rep_perm(dx):
    return [(x, (x + dx) % NX) for x in range(NX)]


def shifted(values, row_step, col_step, cell):
    if row_step == 0 and col_step == 0:
        return values
    rolled = pltpu.roll(values, (-(row_step * SIDE + col_step)) % CELLS, 1)
    row, col = cell // SIDE + row_step, cell % SIDE + col_step
    inside = (row >= 0) & (row < SIDE) & (col >= 0) & (col < SIDE)
    return jnp.where(inside, rolled, 0.0)


def input_kernel(place_ref, gate_ref, grad_ref, weight_ref, out_ref, lhs_ref, rhs_ref, stage_ref):
    patch = pl.program_id(0)
    cell = lax.broadcasted_iota(jnp.int32, (1, CELLS), 1)
    lane_group = lax.broadcasted_iota(jnp.int32, (WIDTH, CHANNELS), 1) // WIDTH
    grad = grad_ref[0].astype(jnp.float32)
    for b in (-1, 0, 1):
        by_col = shifted(grad, 0, -b, cell)
        for a in (-1, 0, 1):
            tap = 3 * (a + 1) + (b + 1)
            rhs_ref[tap * CHANNELS : (tap + 1) * CHANNELS, :] = shifted(
                by_col, -a, 0, cell
            ).astype(jnp.bfloat16)
    for k in range(2):
        for quarter in range(NX):
            stage_ref[quarter * PIECE : (quarter + 1) * PIECE, :] = weight_ref[
                place_ref[(patch * 2 + k) * NX + quarter]
            ]
        for tap in range(9):
            kernel = stage_ref[tap * WIDTH : (tap + 1) * WIDTH, :]
            for group in range(GROUPS):
                row = k * CHANNELS + group * WIDTH
                lhs_ref[row : row + WIDTH, tap * CHANNELS : (tap + 1) * CHANNELS] = jnp.where(
                    lane_group == group, kernel, jnp.zeros_like(kernel)
                )
    both = jnp.dot(lhs_ref[...], rhs_ref[...], preferred_element_type=jnp.float32)
    total = (
        gate_ref[patch * 2] * both[:CHANNELS] + gate_ref[patch * 2 + 1] * both[CHANNELS:]
    )
    out_ref[0] = total.astype(jnp.bfloat16)


def input_grads(place, gate, grad, weight):
    count = grad.shape[0]
    return pl.pallas_call(
        input_kernel,
        out_shape=jax.ShapeDtypeStruct(grad.shape, jnp.bfloat16),
        grid=(count,),
        in_specs=[
            pl.BlockSpec(memory_space=pltpu.SMEM),
            pl.BlockSpec(memory_space=pltpu.SMEM),
            pl.BlockSpec((1, CHANNELS, CELLS), lambda i: (i, 0, 0)),
            pl.BlockSpec(memory_space=pltpu.VMEM),
        ],
        out_specs=pl.BlockSpec((1, CHANNELS, CELLS), lambda i: (i, 0, 0)),
        scratch_shapes=[
            pltpu.VMEM((2 * CHANNELS, 9 * CHANNELS), jnp.bfloat16),
            pltpu.VMEM((9 * CHANNELS, CELLS), jnp.bfloat16),
            pltpu.VMEM((NX * PIECE, CHANNELS), jnp.bfloat16),
        ],
        compiler_params=pltpu.CompilerParams(vmem_limit_bytes=24 << 20),
        cost_estimate=pl.CostEstimate(
            flops=1, bytes_accessed=1, transcendentals=0
        ),
    )(place, gate, grad, weight)


def weight_kernel(halves, chunks, continued, row_of, gate_of, *refs):
    grads, refs = refs[:halves], refs[halves:]
    stash, refs = refs[:chunks], refs[chunks:]
    if continued:
        begun, refs = refs[0], refs[1:]
    out_ref = refs[0]
    (list_grad, list_row, list_chunk, list_gate, ends, grad_buf, stash_buf, lhs, rhs, total, sems) = refs[1:]
    held = grads[0].shape[0]
    cell = lax.broadcasted_iota(jnp.int32, (1, CELLS), 1)

    filled = jnp.int32(0)
    for chunk in range(chunks):

        def note(slot, filled, chunk=chunk):
            row = row_of[chunk * 16 + slot]
            list_grad[filled] = jnp.maximum(row, 0)
            list_row[filled] = slot
            list_chunk[filled] = chunk
            list_gate[filled] = gate_of[chunk * 16 + slot]
            return filled + (row >= 0).astype(jnp.int32)

        filled = lax.fori_loop(0, 16, note, filled)
        list_grad[filled] = 0
        list_row[filled] = 0
        list_chunk[filled] = chunk
        list_gate[filled] = 0.0
        filled = filled + (filled & 1)
        ends[chunk] = filled // 2
    pairs = filled // 2

    def start(pair):
        for j in range(2):
            at = pair * 2 + j
            slot = (pair % DEPTH) * 2 + j
            row = list_grad[at]
            for half in range(halves):

                @pl.when((row >= half * held) & (row < (half + 1) * held))
                def _(half=half):
                    pltpu.make_async_copy(
                        grads[half].at[row - half * held], grad_buf.at[slot], sems.at[slot, 0]
                    ).start()

            for chunk in range(chunks):

                @pl.when(list_chunk[at] == chunk)
                def _(chunk=chunk):
                    pltpu.make_async_copy(
                        stash[chunk].at[list_row[at]], stash_buf.at[slot], sems.at[slot, 1]
                    ).start()

    def finish(pair):
        for j in range(2):
            slot = (pair % DEPTH) * 2 + j
            pltpu.make_async_copy(grads[0].at[0], grad_buf.at[slot], sems.at[slot, 0]).wait()
            pltpu.make_async_copy(stash[0].at[0], stash_buf.at[slot], sems.at[slot, 1]).wait()

    for pair in range(DEPTH):

        @pl.when(pair < pairs)
        def _(pair=pair):
            start(jnp.int32(pair))

    begin = jnp.int32(0)
    for chunk in range(chunks):
        total[...] = begun[chunk] if continued else jnp.zeros_like(total)

        def step(pair, carry):
            finish(pair)
            for j in range(2):
                slot = (pair % DEPTH) * 2 + j
                cells = slice(j * CELLS, (j + 1) * CELLS)
                grad = grad_buf[slot].astype(jnp.float32) * list_gate[pair * 2 + j]
                kept = stash_buf[slot].astype(jnp.float32)
                for i, step_by in enumerate((-1, 0, 1)):
                    left = shifted(grad, -step_by, 0, cell).astype(jnp.bfloat16)
                    right = shifted(kept, 0, step_by, cell).astype(jnp.bfloat16)
                    for group in range(GROUPS):
                        rows = slice(group * WIDTH, (group + 1) * WIDTH)
                        lhs[group, i * WIDTH : (i + 1) * WIDTH, cells] = left[rows]
                        rhs[group, i * WIDTH : (i + 1) * WIDTH, cells] = right[rows]
            for group in range(GROUPS):
                total[group] += lax.dot_general(
                    lhs[group],
                    rhs[group],
                    (((1,), (1,)), ((), ())),
                    preferred_element_type=jnp.float32,
                )

            @pl.when(pair + DEPTH < pairs)
            def _():
                start(pair + DEPTH)

            return carry

        lax.fori_loop(begin, ends[chunk], step, 0)
        begin = ends[chunk]
        out_ref[chunk] = total[...].astype(out_ref.dtype)


def weight_grads(row_of, gate_of, grads, stash, begun, dtype):
    chunks, halves, continued = len(stash), len(grads), begun is not None
    place = pl.BlockSpec(memory_space=pl.ANY)
    extra = [begun] if continued else []
    return pl.pallas_call(
        functools.partial(weight_kernel, halves, chunks, continued),
        out_shape=jax.ShapeDtypeStruct((chunks, GROUPS, 3 * WIDTH, 3 * WIDTH), dtype),
        in_specs=[pl.BlockSpec(memory_space=pltpu.SMEM)] * 2
        + [place] * (halves + chunks)
        + [pl.BlockSpec(memory_space=pltpu.VMEM)] * len(extra),
        out_specs=pl.BlockSpec(memory_space=pltpu.VMEM),
        scratch_shapes=[
            pltpu.SMEM((18 * chunks,), jnp.int32),
            pltpu.SMEM((18 * chunks,), jnp.int32),
            pltpu.SMEM((18 * chunks,), jnp.int32),
            pltpu.SMEM((18 * chunks,), jnp.float32),
            pltpu.SMEM((chunks,), jnp.int32),
            pltpu.VMEM((2 * DEPTH, CHANNELS, CELLS), jnp.bfloat16),
            pltpu.VMEM((2 * DEPTH, CHANNELS, CELLS), jnp.bfloat16),
            pltpu.VMEM((GROUPS, 3 * WIDTH, 2 * CELLS), jnp.bfloat16),
            pltpu.VMEM((GROUPS, 3 * WIDTH, 2 * CELLS), jnp.bfloat16),
            pltpu.VMEM((GROUPS, 3 * WIDTH, 3 * WIDTH), jnp.float32),
            pltpu.SemaphoreType.DMA((2 * DEPTH, 2)),
        ],
        compiler_params=pltpu.CompilerParams(vmem_limit_bytes=56 << 20),
        cost_estimate=pl.CostEstimate(
            flops=1, bytes_accessed=1, transcendentals=0
        ),
    )(row_of.reshape(-1), gate_of.reshape(-1), *grads, *stash, *extra)


def stack_of(first, others):
    return jnp.concatenate([first[None]] + [o[None] for o in others], 0)


def per_device(out_grad, routes, gates, stash, weights):
    x, e = lax.axis_index("rep"), lax.axis_index("ep")
    z, y, c = e // (NY * NC), e // NC % NY, e % NC
    rows, top = routes.shape
    groups = [[zz * NY * NC + r for zz in range(NZ)] for r in range(NY * NC)]
    grads = lax.all_gather(out_grad, "ep", axis=0, tiled=True, axis_index_groups=groups)

    kept = stash.reshape(NZ, NY, NC, 2, CHANNELS, CELLS)
    offsets = [(0, 0), (0, 1), (1, 0), (3, 0), (1, 1), (3, 1), (2, 0), (2, 1)]

    def sent(kept, d, dc):
        part = lax.dynamic_slice(
            kept, (0, (y + d) % NY, c ^ dc, 0, 0, 0), (NZ, 1, 1, 2, CHANNELS, CELLS)
        )
        return part.reshape(NZ * 2, CHANNELS, CELLS)

    first = [sent(kept, d, dc) for d, dc in offsets[2:4]]
    mixed = weights[0].transpose(0, 3, 1, 2).reshape(9 * WIDTH, CHANNELS)
    mixed = jnp.pad(mixed, ((0, NX * PIECE - 9 * WIDTH), (0, 0)))
    piece = lax.dynamic_slice_in_dim(mixed, x * PIECE, PIECE, 0)
    note = jnp.concatenate(
        [routes.reshape(1, -1).astype(jnp.bfloat16), gates.reshape(1, -1)], 1
    )
    note = jnp.pad(note, ((0, 15), (0, CHANNELS - 2 * rows * top)))
    held = jnp.concatenate([piece, note], 0)
    kept, held, *first = lax.optimization_barrier((kept, held, *first))
    own, *rest = [sent(kept, d, dc) for d, dc in offsets[:2] + offsets[4:]]
    experts = [e - y * NC - c + ((y - d) % NY) * NC + (c ^ dc) for d, dc in offsets]
    experts = jnp.stack(experts)

    up = down = held
    from_z = {0: held}
    for d in range(1, NZ // 2 + 1):
        up = lax.ppermute(up, "ep", ep_perm(1, 0, 0))
        from_z[d] = up
        if d < NZ // 2:
            down = lax.ppermute(down, "ep", ep_perm(-1, 0, 0))
            from_z[NZ - d] = down
    held = jnp.stack([from_z[d] for d in range(NZ)])
    notes = held[:, PIECE, : 2 * rows * top].astype(jnp.float32)
    held = held[:, :PIECE]
    held, *rest = lax.optimization_barrier((held, *rest))
    rest = rest[:1] + first + rest[1:]
    chunks = [own] + [
        lax.ppermute(part, "ep", ep_perm(0, d, dc)) for part, (d, dc) in zip(rest, offsets[1:])
    ]
    held = stack_of(held, [lax.ppermute(held, "ep", ep_perm(0, d, 0)) for d in range(1, NY)])
    held = held.reshape(NY * NZ, PIECE, CHANNELS)
    held, chunks[2], chunks[3] = lax.optimization_barrier((held, chunks[2], chunks[3]))
    held = stack_of(held, [lax.ppermute(held, "rep", rep_perm(d)) for d in range(1, NX)])
    held, chunks[4], chunks[5] = lax.optimization_barrier((held, chunks[4], chunks[5]))
    held = stack_of(held, [lax.ppermute(held, "ep", ep_perm(0, 0, 1))])
    held = held.reshape(NC * NX * NY * NZ, PIECE, CHANNELS)

    from_z = (z - jnp.arange(NZ, dtype=jnp.int32)) % NZ
    notes = jnp.sum(
        jnp.where((from_z[:, None] == jnp.arange(NZ)[None])[:, :, None], notes[:, None], 0.0), 0
    )
    named = notes[:, : rows * top].astype(jnp.int32)
    gate = notes[:, rows * top :]
    here = experts[:, None, None] == named[None]
    order = jnp.arange(rows * top, dtype=jnp.int32)
    before = (order[:, None] < order[None, :])[None, None] & here[:, :, :, None]
    earlier = jnp.sum(before.astype(jnp.int32), 2)
    chosen = here[:, :, None, :] & (earlier[:, :, None, :] == jnp.arange(2)[None, None, :, None])
    source_row = jnp.arange(NZ, dtype=jnp.int32)[:, None] * rows + (order // top)[None]
    row_of = jnp.max(jnp.where(chosen, source_row[None, :, None, :], -1), 3)
    gate_of = jnp.sum(jnp.where(chosen, gate[None, :, None, :], 0.0), 3)
    flat = routes.reshape(-1)
    at_z, at_y, at_c = flat // (NY * NC), flat // NC % NY, flat % NC
    block = ((y - at_y) % NY) * NZ + (z - at_z) % NZ
    quarter = (x - jnp.arange(NX, dtype=jnp.int32)) % NX
    place = ((at_c ^ c)[:, None] * NX + quarter[None]) * (NZ * NY) + block[:, None]
    in_grad = input_grads(
        place.reshape(-1), gates.reshape(-1).astype(jnp.float32), out_grad, held
    )

    in_grad, row_of = lax.optimization_barrier((in_grad, row_of))
    early = weight_grads(row_of[:6], gate_of[:6], [grads], chunks[:6], None, jnp.bfloat16)
    late = weight_grads(row_of[6:], gate_of[6:], [grads], chunks[6:], None, jnp.bfloat16)
    parts = [early[i] for i in range(6)] + [late[i] for i in range(2)]

    total = None
    for part, (d, dc) in zip(parts, offsets):
        if d or dc:
            part = lax.ppermute(part, "ep", ep_perm(0, -d, dc))
        part = part.astype(jnp.float32)
        total = part if total is None else total + part
    total = total.astype(jnp.bfloat16)
    summed = total.astype(jnp.float32)
    for d in range(1, NX):
        summed = summed + lax.ppermute(total, "rep", rep_perm(d)).astype(jnp.float32)
    weight_grad = summed.reshape(GROUPS, 3, WIDTH, 3, WIDTH).transpose(1, 3, 0, 2, 4)
    return in_grad, weight_grad.reshape(1, 9, GROUPS, WIDTH, WIDTH)


def solution(mesh):
    return jax.shard_map(
        per_device,
        mesh=mesh,
        in_specs=(
            P(("rep", "ep"), None, None),
            P(("rep", "ep"), None),
            P(("rep", "ep"), None),
            P("rep", "ep", None, None, None, None),
            P("ep", None, None, None, None),
        ),
        out_specs=(P(("rep", "ep"), None, None), P("ep", None, None, None, None)),
        check_vma=False,
    )
```

time: 706 us -> 176 us (0.25)
  waiting for transfers between devices: 362 us -> 64.7 us
  local copies, waits for them, and re-layouts: 161 us -> 18.2 us
  matrix products: 122 us -> 0 us
  starting transfers between devices: 23.7 us -> 49.5 us
  Pallas kernels: 0 us -> 21.6 us
  other arithmetic: 14.7 us -> 7.44 us
    all_to_all x2 -> x0, waiting for transfers between devices: 312 us -> none  [the longest x1 182 us: per_device(): lax.all_to_all(outgoing, 'ep', split_axis=0, concat_axis=0, tiled=True)]
    dot_general x288 -> x0, matrix products: 122 us -> none  [the longest x144 70.4 us: input_terms(): jnp.einsum(einsum_form, tap_kernel, grouped_grad, preferred_element_type=...]
    ppermute x0 -> x31, waiting for transfers between devices: none -> 64 us  [the longest x3 27.5 us: per_device(): lax.ppermute(held, 'rep', rep_perm(d))]
    slice x336 -> x9, local copies, waits for them, and re-layouts: 64.3 us -> 0.41 us  [the longest x2 0.11 us: per_device(): row_of[:6]]
    psum x1 -> x0, waiting for transfers between devices: 49.6 us -> none  [per_device(): lax.psum(weight_sum.astype(jnp.bfloat16), 'rep').astype(jnp.float32)]
    ppermute x0 -> x31, starting transfers between devices: none -> 49.4 us  [the longest x7 14 us: per_device(): lax.ppermute(part, 'ep', ep_perm(0, d, dc))]
    dynamic_update_slice x16 -> x0, local copies, waits for them, and re-layouts: 30.7 us -> none  [step_fn(): lax.dynamic_update_slice_in_dim(grads_out, block_grads, first_row, 0)]
    scatter x2 -> x0, local copies, waits for them, and re-layouts: 28.9 us -> none  [the longest x1 23.5 us: per_device(): jnp.zeros((total_slots, channels, positions), jnp.bfloat16).at[arrangement]]
  transfers between devices with their start and end apart: 3 -> 32, of which waited for: 3 -> 11; matrix products, arithmetic and copies ran while one was open for 0% -> 12% of each run, Pallas kernels for 0% -> 12%
where the time goes in v1:
time: 176 us
  waiting for transfers between devices  64.7 us (37%)
  starting transfers between devices  49.5 us (28%)
  Pallas kernels  21.6 us (12%)
  local copies, waits for them, and re-layouts  18.2 us (10%)
  between operations  14.4 us (8%)
  other arithmetic  7.44 us (4%)
    ppermute x3, waiting for transfers between devices, per_device(): lax.ppermute(held, 'rep', rep_perm(d))  27.5 us
    ppermute x7, waiting for transfers between devices, per_device(): lax.ppermute(part, 'ep', ep_perm(0, d, dc))  17.1 us
    ppermute x7, starting transfers between devices, per_device(): lax.ppermute(part, 'ep', ep_perm(0, d, dc))  14 us
    pallas_call x2, Pallas kernels, weight_grads(): pl.pallas_call(functools.partial(weight_kernel, halves, chunks, continued...  11.1 us
    pallas_call x1, Pallas kernels, input_grads(): pl.pallas_call(input_kernel, out_shape=jax.ShapeDtypeStruct(grad.shape, j...  10.5 us
    ppermute x3, starting transfers between devices, per_device(): down = lax.ppermute(down, 'ep', ep_perm(-1, 0, 0))  9.5 us
    ppermute x7, starting transfers between devices, per_device(): part = lax.ppermute(part, 'ep', ep_perm(0, -d, dc))  8.87 us
    ppermute x4, waiting for transfers between devices, per_device(): up = lax.ppermute(up, 'ep', ep_perm(1, 0, 0))  8.81 us
  transfers between devices with their start and end apart: 32, of which 11 were waited for; matrix products, arithmetic and copies ran while one was open for 12% of the time, Pallas kernels for 12%

profile of v1, /device:TPU:1, one launch (start us, length us, event | category | flops | bytes accessed | tf_op | source)
XLA Modules:
  0.0 175.8 jit_solution(4034356164014158189)
XLA Ops:
  7.2 0.7 all-gather.2.cloned.1.call-update
  8.0 1.2 copy.63
  9.1 0.2 reshape.304
  9.3 0.7 convert_element_type.75
  10.2 0.7 copy.65
  11.2 1.7 constant_dynamic-slice_fusion.6
  12.9 2.5 %collective-permute-start = (bf16[96,128]{1,0:T(8,128)(2,1)S(1)}, bf16[96,128]{1,0:T(8,128)(2,1)S(1)}, u32[]{:S(2)}, u32[]{:S(2)}) collective-permute-start(bf16[96,128]{1,0:T(8,128)(2,1)S(1)} %pad_maximum_fusion.3), channel_id=1, source_target_pairs={{0,8},{1,9},{2,10},{3,11},{4,12},{5,13},{6,14},{7,15},{8,16},{9,17... | collective-permute-start | bytes 73736 | tf_op jit(solution)/shard_map/ppermute | solution.py:267
  15.4 4.0 %collective-permute-start.4 = (bf16[96,128]{1,0:T(8,128)(2,1)S(1)}, bf16[96,128]{1,0:T(8,128)(2,1)S(1)}, u32[]{:S(2)}, u32[]{:S(2)}) collective-permute-start(bf16[96,128]{1,0:T(8,128)(2,1)S(1)} %pad_maximum_fusion.3), channel_id=1, source_target_pairs={{0,56},{1,57},{2,58},{3,59},{4,60},{5,61},{6,62},{7,63},{8,0},{9,1... | collective-permute-start | bytes 73736 | tf_op jit(solution)/shard_map/ppermute | solution.py:270
  19.5 1.3 collective-permute-start.10
  20.8 1.4 collective-permute-start.11
  22.2 5.1 %constant_dynamic-slice_fusion = (bf16[8,1,1,2,128,256]{5,4,3,0,2,1:T(8,128)(2,1)}, bf16[8,1,1,2,128,256]{5,4,3,0,2,1:T(8,128)(2,1)}, bf16[8,1,1,2,128,256]{5,4,...) fusion(s32[]{:T(128)S(6)} %select_n.202, ...), kind=kLoop, calls=%fused_computation.50 | loop fusion | bytes 12582936 | tf_op jit(solution)/shard_map/dynamic_slice | solution.py:245
  27.4 2.7 %collective-permute-start.5 = (bf16[96,128]{1,0:T(8,128)(2,1)S(1)}, bf16[96,128]{1,0:T(8,128)(2,1)S(1)}, u32[]{:S(2)}, u32[]{:S(2)}) collective-permute-start(bf16[96,128]{1,0:T(8,128)(2,1)S(1)} %collective-permute-done.4), channel_id=1, source_target_pairs={{0,56},{1,57},{2,58},{3,59},{4,60},{5,61},{6,62},{7,63},{8,0},{9,1... | collective-permute-start | bytes 73736 | tf_op jit(solution)/shard_map/ppermute | solution.py:270
  30.1 2.0 %collective-permute-done.1 = bf16[96,128]{1,0:T(8,128)(2,1)S(1)} collective-permute-done((bf16[96,128]{1,0:T(8,128)(2,1)S(1)}, bf16[96,128]{1,0:T(8,128)(2,1)S(1)}, u32[]{:S(2)}, u32[]{:S(2)}) %collective-permute-start.1) | collective-permute-done | bytes 24608 | tf_op jit(solution)/shard_map/ppermute | solution.py:267
  32.2 2.7 %collective-permute-start.6 = (bf16[96,128]{1,0:T(8,128)(2,1)S(1)}, bf16[96,128]{1,0:T(8,128)(2,1)S(1)}, u32[]{:S(2)}, u32[]{:S(2)}) collective-permute-start(bf16[96,128]{1,0:T(8,128)(2,1)S(1)} %collective-permute-done.5), channel_id=1, source_target_pairs={{0,56},{1,57},{2,58},{3,59},{4,60},{5,61},{6,62},{7,63},{8,0},{9,1... | collective-permute-start | bytes 73736 | tf_op jit(solution)/shard_map/ppermute | solution.py:270
  34.9 2.0 %collective-permute-done.2 = bf16[96,128]{1,0:T(8,128)(2,1)S(1)} collective-permute-done((bf16[96,128]{1,0:T(8,128)(2,1)S(1)}, bf16[96,128]{1,0:T(8,128)(2,1)S(1)}, u32[]{:S(2)}, u32[]{:S(2)}) %collective-permute-start.2) | collective-permute-done | bytes 24608 | tf_op jit(solution)/shard_map/ppermute | solution.py:267
  36.9 4.8 %collective-permute-done.3 = bf16[96,128]{1,0:T(8,128)(2,1)S(1)} collective-permute-done((bf16[96,128]{1,0:T(8,128)(2,1)S(1)}, bf16[96,128]{1,0:T(8,128)(2,1)S(1)}, u32[]{:S(2)}, u32[]{:S(2)}) %collective-permute-start.3) | collective-permute-done | bytes 24608 | tf_op jit(solution)/shard_map/ppermute | solution.py:267
  41.9 2.5 %collective-permute-start.8 = (bf16[8,80,128]{2,1,0:T(8,128)(2,1)S(1)}, bf16[8,80,128]{2,1,0:T(8,128)(2,1)S(1)}, u32[]{:S(2)}, u32[]{:S(2)}) collective-permute-start(bf16[8,80,128]{2,1,0:T(8,128)(2,1)S(1)} %slice.64), channel_id=1, source_target_pairs={{0,4},{1,5},{2,6},{3,7},{4,0},{5,1},{6,2},{7,3},{8,12},{9,13},{10,... | collective-permute-start | bytes 491528 | tf_op jit(solution)/shard_map/ppermute | solution.py:280
  44.4 1.0 collective-permute-start.9
  45.4 2.3 %collective-permute-done.7 = bf16[8,80,128]{2,1,0:T(8,128)(2,1)S(1)} collective-permute-done((bf16[8,80,128]{2,1,0:T(8,128)(2,1)S(1)}, bf16[8,80,128]{2,1,0:T(8,128)(2,1)S(1)}, u32[]{:S(2)}, u32[]{:S(2)}) %collective-permute-start.7) | collective-permute-done | bytes 163872 | tf_op jit(solution)/shard_map/ppermute | solution.py:280
  47.8 3.8 %collective-permute-start.15 = (bf16[16,128,256]{2,1,0:T(8,128)(2,1)S(1)}, bf16[16,128,256]{2,1,0:T(8,128)(2,1)S(1)}, u32[]{:S(2)}, u32[]{:S(2)}) collective-permute-start(bf16[16,128,256]{2,1,0:T(8,128)(2,1)S(1)} %bitcast.90), channel_id=1, source_target_pairs={{0,3},{1,2},{2,5},{3,4},{4,7},{5,6},{6,1},{7,0},{8,11},{9,10},{10,... | collective-permute-start | bytes 3145736 | tf_op jit(solution)/shard_map/ppermute | solution.py:278
  51.5 3.9 %collective-permute-start.16 = (bf16[16,128,256]{2,1,0:T(8,128)(2,1)S(1)}, bf16[16,128,256]{2,1,0:T(8,128)(2,1)S(1)}, u32[]{:S(2)}, u32[]{:S(2)}) collective-permute-start(bf16[16,128,256]{2,1,0:T(8,128)(2,1)S(1)} %bitcast.89), channel_id=1, source_target_pairs={{0,7},{1,6},{2,1},{3,0},{4,3},{5,2},{6,5},{7,4},{8,15},{9,14},{10,... | collective-permute-start | bytes 3145736 | tf_op jit(solution)/shard_map/ppermute | solution.py:278
  55.6 1.6 collective-permute-start.12
  57.1 2.5 %collective-permute-start.13 = (bf16[32,80,128]{2,1,0:T(8,128)(2,1)S(1)}, bf16[32,80,128]{2,1,0:T(8,128)(2,1)S(1)}, u32[]{:S(2)}, u32[]{:S(2)}) collective-permute-start(bf16[32,80,128]{2,1,0:T(8,128)(2,1)S(1)} %bitcast.81), channel_id=1, source_target_pairs={{0,128},{64,192},{128,0},{192,64},{1,129},{65,193},{129,1},{193,65... | collective-permute-start | bytes 1966088 | tf_op jit(solution)/shard_map/ppermute | solution.py:283
  59.6 1.1 collective-permute-start.14
  60.7 12.4 %collective-permute-done.12 = bf16[32,80,128]{2,1,0:T(8,128)(2,1)S(1)} collective-permute-done((bf16[32,80,128]{2,1,0:T(8,128)(2,1)S(1)}, bf16[32,80,128]{2,1,0:T(8,128)(2,1)S(1)}, u32[]{:S(2)}, u32[]{:S(2)}) %collective-permute-start.12) | collective-permute-done | bytes 655392 | tf_op jit(solution)/shard_map/ppermute | solution.py:283
  73.2 15.1 %collective-permute-done.13 = bf16[32,80,128]{2,1,0:T(8,128)(2,1)S(1)} collective-permute-done((bf16[32,80,128]{2,1,0:T(8,128)(2,1)S(1)}, bf16[32,80,128]{2,1,0:T(8,128)(2,1)S(1)}, u32[]{:S(2)}, u32[]{:S(2)}) %collective-permute-start.13) | collective-permute-done | bytes 655392 | tf_op jit(solution)/shard_map/ppermute | solution.py:283
  88.3 1.9 %pad_maximum_fusion.1 = bf16[4,32,80,128]{3,2,1,0:T(8,128)(2,1)} fusion(bf16[1,32,80,128]{3,2,1,0:T(8,128)(2,1)S(1)} %bitcast.93, bf16[1,32,80,128]{3,2,1,0:T(8,128)(2,1)S(1)} %bitcast.92, bf16[1,32,80,128]{3,2,1,0:T(8,128)(2,1)S(1)} %bitcast.91, bf16[1,32,80,128]{3,2,1,0:T(8,128)(2,1)S(1)} %bitcast.83), kind=kLoop, calls=%fused_computation.1 | loop fusion | flops 3932160 | bytes 5242880 | tf_op jit(solution)/shard_map/concatenate | solution.py:231
  90.2 1.0 copy-done.2
  91.2 1.0 copy-done.3
  92.2 1.0 collective-permute-start.17
  93.6 0.1 add.292.place_ref
  94.1 0.3 collective-permute-start.24
  94.5 3.3 %collective-permute-start.25 = (bf16[16,128,256]{2,1,0:T(8,128)(2,1)}, bf16[16,128,256]{2,1,0:T(8,128)(2,1)}, u32[]{:S(2)}, u32[]{:S(2)}) collective-permute-start(bf16[16,128,256]{2,1,0:T(8,128)(2,1)} %bitcast.86), channel_id=1, source_target_pairs={{0,5},{1,4},{2,7},{3,6},{4,1},{5,0},{6,3},{7,2},{8,13},{9,12},{10,... | collective-permute-start | bytes 3145736 | tf_op jit(solution)/shard_map/ppermute | solution.py:278
  98.0 0.4 convert_reduce_fusion
  98.4 0.1 select_reduce_fusion
  98.5 0.1 copy.74
  98.6 0.7 reshape.316.gate_of
  99.4 0.7 reshape.319.gate_of
  100.1 0.4 select_reduce_fusion.1
  100.5 2.3 %pad_maximum_fusion = bf16[2,4,32,80,128]{4,3,2,1,0:T(8,128)(2,1)S(1)} fusion(bf16[1,4,32,80,128]{4,3,2,1,0:T(8,128)(2,1)S(1)} %bitcast.79, bf16[1,4,32,80,128]{4,3,2,1,0:T(8,128)(2,1)} %bitcast.27), kind=kLoop, calls=%fused_computation | loop fusion | flops 2621440 | bytes 10485760 | tf_op jit(solution)/shard_map/concatenate | solution.py:231
  102.8 10.5 %shard_map.68 = bf16[16,128,256]{2,1,0:T(8,128)(2,1)} custom-call(s32[128]{0:T(128)S(1)} %add.292.place_ref, f32[32]{0:T(128)S(1)} %reshape.322.gate_ref, bf16[16,128,256]{2,1,0:T(8,128)(2,1)S(1)} %copy-done, bf16[256,80,128]{2,1,0:T(8,128)(2,1)S(1)} %bitcast.74), custom_call_target="tpu_custom_call" | custom-call | flops 1 | bytes 1 | tf_op jit(solution)/shard_map/pallas_call | solution.py:76
  113.3 0.1 copy.73
  113.4 0.7 reshape.315.row_of
  114.1 0.6 reshape.318.row_of
  114.8 7.5 %shard_map.69 = bf16[6,4,96,96]{3,2,1,0:T(8,128)(2,1)} custom-call(s32[96]{0:T(128)} %reshape.315.row_of, f32[96]{0:T(128)} %reshape.316.gate_of, bf16[128,128,256]{2,1,0:T(8,128)(2,1)} %all-gather.2.cloned.1.call-done.refs_0_, bf16[16,128,256]{2,1,0:T(8,128)(2,1)} %bitcast.77, bf16[16,128,256]{2,1,0:T(8,128)(2,1)} %collective-permute-done.18.refs_2_, ...), custom_call_target="tpu_custom_call" | custom-call | flops 1 | bytes 1 | tf_op jit(solution)/shard_map/pallas_call | solution.py:203
  122.3 1.1 slice_bitcast_fusion.6
  123.4 0.7 collective-permute-start.19
  124.2 1.5 collective-permute-start.21
  125.6 1.6 collective-permute-start.22
  127.2 17.1 %collective-permute-done.25.refs_2_ = bf16[16,128,256]{2,1,0:T(8,128)(2,1)} collective-permute-done((bf16[16,128,256]{2,1,0:T(8,128)(2,1)}, bf16[16,128,256]{2,1,0:T(8,128)(2,1)}, u32[]{:S(2)}, u32[]{:S(2)}) %collective-permute-start.25) | collective-permute-done | bytes 1048608 | tf_op jit(solution)/shard_map/ppermute | solution.py:278
  144.3 3.6 %shard_map.70 = bf16[2,4,96,96]{3,2,1,0:T(8,128)(2,1)} custom-call(s32[32]{0:T(128)} %reshape.318.row_of, f32[32]{0:T(128)} %reshape.319.gate_of, bf16[128,128,256]{2,1,0:T(8,128)(2,1)} %all-gather.2.cloned.1.call-done.refs_0_, bf16[16,128,256]{2,1,0:T(8,128)(2,1)} %collective-permute-done.24.refs_1_, bf16[16,128,256]{2,1,0:T(8,128)(2,1)} %collective-permute-done.25.refs_2_), custom_call_target="tpu_custom_call" | custom-call | flops 1 | bytes 1 | tf_op jit(solution)/shard_map/pallas_call | solution.py:203
  147.9 1.0 slice_bitcast_fusion.1
  148.8 1.6 collective-permute-start.26
  150.5 3.5 %collective-permute-start.27 = (bf16[4,96,96]{2,1,0:T(8,128)(2,1)S(1)}, bf16[4,96,96]{2,1,0:T(8,128)(2,1)S(1)}, u32[]{:S(2)}, u32[]{:S(2)}) collective-permute-start(bf16[4,96,96]{2,1,0:T(8,128)(2,1)S(1)} %get-tuple-element.52), channel_id=1, source_target_pairs={{0,5},{1,4},{2,7},{3,6},{4,1},{5,0},{6,3},{7,2},{8,13},{9,12},{10,... | collective-permute-start | bytes 221192 | tf_op jit(solution)/shard_map/ppermute | solution.py:319
  153.9 4.4 %collective-permute-done.27 = bf16[4,96,96]{2,1,0:T(8,128)(2,1)S(1)} collective-permute-done((bf16[4,96,96]{2,1,0:T(8,128)(2,1)S(1)}, bf16[4,96,96]{2,1,0:T(8,128)(2,1)S(1)}, u32[]{:S(2)}, u32[]{:S(2)}) %collective-permute-start.27) | collective-permute-done | bytes 73760 | tf_op jit(solution)/shard_map/ppermute | solution.py:319
  158.3 1.0 fusion.6
  159.3 0.8 collective-permute-start.28
  160.1 1.8 collective-permute-start.29
  161.9 1.9 %collective-permute-start.30 = (bf16[4,96,96]{2,1,0:T(8,128)(2,1)S(1)}, bf16[4,96,96]{2,1,0:T(8,128)(2,1)S(1)}, u32[]{:S(2)}, u32[]{:S(2)}) collective-permute-start(bf16[4,96,96]{2,1,0:T(8,128)(2,1)S(1)} %fusion.6), channel_id=1, source_target_pairs={{0,192},{64,0},{128,64},{192,128},{1,193},{65,1},{129,65},{193,129... | collective-permute-start | bytes 221192 | tf_op jit(solution)/shard_map/ppermute | solution.py:325
  163.8 1.4 collective-permute-done.28
  165.3 2.0 %collective-permute-done.29 = bf16[4,96,96]{2,1,0:T(8,128)(2,1)S(1)} collective-permute-done((bf16[4,96,96]{2,1,0:T(8,128)(2,1)S(1)}, bf16[4,96,96]{2,1,0:T(8,128)(2,1)S(1)}, u32[]{:S(2)}, u32[]{:S(2)}) %collective-permute-start.29) | collective-permute-done | bytes 73760 | tf_op jit(solution)/shard_map/ppermute | solution.py:325
  167.3 0.4 collective-permute-done.30
  167.7 0.3 reshape.320
  168.1 0.9 copy.78
  (79 shorter events, 2.0 us)
Async XLA Ops:
  7.2 107.6 %all-gather.2.cloned.1.call-start = ((), (), s32[]{:S(2)}) async-start(), calls=%async_computation | async-start | bytes 9437184 | tf_op jit(solution)/shard_map/all_gather | solution.py:239
  12.9 14.4 %collective-permute-start = (bf16[96,128]{1,0:T(8,128)(2,1)S(1)}, bf16[96,128]{1,0:T(8,128)(2,1)S(1)}, u32[]{:S(2)}, u32[]{:S(2)}) collective-permute-start(bf16[96,128]{1,0:T(8,128)(2,1)S(1)} %pad_maximum_fusion.3), channel_id=1, source_target_pairs={{0,8},{1,9},{2,10},{3,11},{4,12},{5,13},{6,14},{7,15},{8,16},{9,17... | collective-permute-start | bytes 73736 | tf_op jit(solution)/shard_map/ppermute | solution.py:267
  15.4 12.0 %collective-permute-start.4 = (bf16[96,128]{1,0:T(8,128)(2,1)S(1)}, bf16[96,128]{1,0:T(8,128)(2,1)S(1)}, u32[]{:S(2)}, u32[]{:S(2)}) collective-permute-start(bf16[96,128]{1,0:T(8,128)(2,1)S(1)} %pad_maximum_fusion.3), channel_id=1, source_target_pairs={{0,56},{1,57},{2,58},{3,59},{4,60},{5,61},{6,62},{7,63},{8,0},{9,1... | collective-permute-start | bytes 73736 | tf_op jit(solution)/shard_map/ppermute | solution.py:270
  19.5 36.1 %collective-permute-start.10 = (bf16[16,128,256]{2,1,0:T(8,128)(2,1)S(1)}, bf16[16,128,256]{2,1,0:T(8,128)(2,1)S(1)}, u32[]{:S(2)}, u32[]{:S(2)}) collective-permute-start(bf16[16,128,256]{2,1,0:T(8,128)(2,1)S(1)} %bitcast.85), channel_id=1, source_target_pairs={{0,2},{1,3},{2,4},{3,5},{4,6},{5,7},{6,0},{7,1},{8,10},{9,11},{10,... | collective-permute-start | bytes 3145736 | tf_op jit(solution)/shard_map/ppermute | solution.py:278
  20.8 34.8 %collective-permute-start.11 = (bf16[16,128,256]{2,1,0:T(8,128)(2,1)S(1)}, bf16[16,128,256]{2,1,0:T(8,128)(2,1)}, u32[]{:S(2)}, u32[]{:S(2)}) collective-permute-start(bf16[16,128,256]{2,1,0:T(8,128)(2,1)S(1)} %bitcast.84), channel_id=1, source_target_pairs={{0,6},{1,7},{2,0},{3,1},{4,2},{5,3},{6,4},{7,5},{8,14},{9,15},{10,... | collective-permute-start | bytes 3145736 | tf_op jit(solution)/shard_map/ppermute | solution.py:278
  27.3 66.0 %copy-start.5 = (s32[16,2]{0,1:T(2,128)S(1)}, s32[16,2]{0,1:T(2,128)}, u32[]{:S(2)}) copy-start(s32[16,2]{0,1:T(2,128)} %param.6) | copy-start | bytes 388
  27.3 66.1 %copy-start.4 = (bf16[16,2]{0,1:T(2,128)(2,1)S(1)}, bf16[16,2]{0,1:T(2,128)(2,1)}, u32[]{:S(2)}) copy-start(bf16[16,2]{0,1:T(2,128)(2,1)} %param.7) | copy-start | bytes 196
  27.3 4.9 %collective-permute-start.1 = (bf16[96,128]{1,0:T(8,128)(2,1)S(1)}, bf16[96,128]{1,0:T(8,128)(2,1)S(1)}, u32[]{:S(2)}, u32[]{:S(2)}) collective-permute-start(bf16[96,128]{1,0:T(8,128)(2,1)S(1)} %collective-permute-done), channel_id=1, source_target_pairs={{0,8},{1,9},{2,10},{3,11},{4,12},{5,13},{6,14},{7,15},{8,16},{9,17... | collective-permute-start | bytes 73736 | tf_op jit(solution)/shard_map/ppermute | solution.py:267
  27.4 4.8 %collective-permute-start.5 = (bf16[96,128]{1,0:T(8,128)(2,1)S(1)}, bf16[96,128]{1,0:T(8,128)(2,1)S(1)}, u32[]{:S(2)}, u32[]{:S(2)}) collective-permute-start(bf16[96,128]{1,0:T(8,128)(2,1)S(1)} %collective-permute-done.4), channel_id=1, source_target_pairs={{0,56},{1,57},{2,58},{3,59},{4,60},{5,61},{6,62},{7,63},{8,0},{9,1... | collective-permute-start | bytes 73736 | tf_op jit(solution)/shard_map/ppermute | solution.py:270
  32.1 4.8 %collective-permute-start.2 = (bf16[96,128]{1,0:T(8,128)(2,1)S(1)}, bf16[96,128]{1,0:T(8,128)(2,1)S(1)}, u32[]{:S(2)}, u32[]{:S(2)}) collective-permute-start(bf16[96,128]{1,0:T(8,128)(2,1)S(1)} %collective-permute-done.1), channel_id=1, source_target_pairs={{0,8},{1,9},{2,10},{3,11},{4,12},{5,13},{6,14},{7,15},{8,16},{9,17... | collective-permute-start | bytes 73736 | tf_op jit(solution)/shard_map/ppermute | solution.py:267
  32.2 9.6 %collective-permute-start.6 = (bf16[96,128]{1,0:T(8,128)(2,1)S(1)}, bf16[96,128]{1,0:T(8,128)(2,1)S(1)}, u32[]{:S(2)}, u32[]{:S(2)}) collective-permute-start(bf16[96,128]{1,0:T(8,128)(2,1)S(1)} %collective-permute-done.5), channel_id=1, source_target_pairs={{0,56},{1,57},{2,58},{3,59},{4,60},{5,61},{6,62},{7,63},{8,0},{9,1... | collective-permute-start | bytes 73736 | tf_op jit(solution)/shard_map/ppermute | solution.py:270
  36.9 4.8 %collective-permute-start.3 = (bf16[96,128]{1,0:T(8,128)(2,1)S(1)}, bf16[96,128]{1,0:T(8,128)(2,1)S(1)}, u32[]{:S(2)}, u32[]{:S(2)}) collective-permute-start(bf16[96,128]{1,0:T(8,128)(2,1)S(1)} %collective-permute-done.2), channel_id=1, source_target_pairs={{0,8},{1,9},{2,10},{3,11},{4,12},{5,13},{6,14},{7,15},{8,16},{9,17... | collective-permute-start | bytes 73736 | tf_op jit(solution)/shard_map/ppermute | solution.py:267
  41.8 6.0 %collective-permute-start.7 = (bf16[8,80,128]{2,1,0:T(8,128)(2,1)S(1)}, bf16[8,80,128]{2,1,0:T(8,128)(2,1)S(1)}, u32[]{:S(2)}, u32[]{:S(2)}) collective-permute-start(bf16[8,80,128]{2,1,0:T(8,128)(2,1)S(1)} %slice.64), channel_id=1, source_target_pairs={{0,2},{1,3},{2,4},{3,5},{4,6},{5,7},{6,0},{7,1},{8,10},{9,11},{10,... | collective-permute-start | bytes 491528 | tf_op jit(solution)/shard_map/ppermute | solution.py:280
  41.9 9.6 %collective-permute-start.8 = (bf16[8,80,128]{2,1,0:T(8,128)(2,1)S(1)}, bf16[8,80,128]{2,1,0:T(8,128)(2,1)S(1)}, u32[]{:S(2)}, u32[]{:S(2)}) collective-permute-start(bf16[8,80,128]{2,1,0:T(8,128)(2,1)S(1)} %slice.64), channel_id=1, source_target_pairs={{0,4},{1,5},{2,6},{3,7},{4,0},{5,1},{6,2},{7,3},{8,12},{9,13},{10,... | collective-permute-start | bytes 491528 | tf_op jit(solution)/shard_map/ppermute | solution.py:280
  44.4 11.0 %collective-permute-start.9 = (bf16[8,80,128]{2,1,0:T(8,128)(2,1)S(1)}, bf16[8,80,128]{2,1,0:T(8,128)(2,1)S(1)}, u32[]{:S(2)}, u32[]{:S(2)}) collective-permute-start(bf16[8,80,128]{2,1,0:T(8,128)(2,1)S(1)} %slice.64), channel_id=1, source_target_pairs={{0,6},{1,7},{2,0},{3,1},{4,2},{5,3},{6,4},{7,5},{8,14},{9,15},{10,... | collective-permute-start | bytes 491528 | tf_op jit(solution)/shard_map/ppermute | solution.py:280
  47.8 42.4 %collective-permute-start.15 = (bf16[16,128,256]{2,1,0:T(8,128)(2,1)S(1)}, bf16[16,128,256]{2,1,0:T(8,128)(2,1)S(1)}, u32[]{:S(2)}, u32[]{:S(2)}) collective-permute-start(bf16[16,128,256]{2,1,0:T(8,128)(2,1)S(1)} %bitcast.90), channel_id=1, source_target_pairs={{0,3},{1,2},{2,5},{3,4},{4,7},{5,6},{6,1},{7,0},{8,11},{9,10},{10,... | collective-permute-start | bytes 3145736 | tf_op jit(solution)/shard_map/ppermute | solution.py:278
  51.5 38.7 %collective-permute-start.16 = (bf16[16,128,256]{2,1,0:T(8,128)(2,1)S(1)}, bf16[16,128,256]{2,1,0:T(8,128)(2,1)S(1)}, u32[]{:S(2)}, u32[]{:S(2)}) collective-permute-start(bf16[16,128,256]{2,1,0:T(8,128)(2,1)S(1)} %bitcast.89), channel_id=1, source_target_pairs={{0,7},{1,6},{2,1},{3,0},{4,3},{5,2},{6,5},{7,4},{8,15},{9,14},{10,... | collective-permute-start | bytes 3145736 | tf_op jit(solution)/shard_map/ppermute | solution.py:278
  55.5 34.6 %copy-start.1 = (bf16[16,128,256]{2,1,0:T(8,128)(2,1)}, bf16[16,128,256]{2,1,0:T(8,128)(2,1)S(1)}, u32[]{:S(2)}) copy-start(bf16[16,128,256]{2,1,0:T(8,128)(2,1)S(1)} %collective-permute-done.10.refs_3_) | copy-start | bytes 3145732
  55.6 17.6 %collective-permute-start.12 = (bf16[32,80,128]{2,1,0:T(8,128)(2,1)S(1)}, bf16[32,80,128]{2,1,0:T(8,128)(2,1)S(1)}, u32[]{:S(2)}, u32[]{:S(2)}) collective-permute-start(bf16[32,80,128]{2,1,0:T(8,128)(2,1)S(1)} %bitcast.80), channel_id=1, source_target_pairs={{0,64},{64,128},{128,192},{192,0},{1,65},{65,129},{129,193},{193,1... | collective-permute-start | bytes 1966088 | tf_op jit(solution)/shard_map/ppermute | solution.py:283
  57.1 31.1 %collective-permute-start.13 = (bf16[32,80,128]{2,1,0:T(8,128)(2,1)S(1)}, bf16[32,80,128]{2,1,0:T(8,128)(2,1)S(1)}, u32[]{:S(2)}, u32[]{:S(2)}) collective-permute-start(bf16[32,80,128]{2,1,0:T(8,128)(2,1)S(1)} %bitcast.81), channel_id=1, source_target_pairs={{0,128},{64,192},{128,0},{192,64},{1,129},{65,193},{129,1},{193,65... | collective-permute-start | bytes 1966088 | tf_op jit(solution)/shard_map/ppermute | solution.py:283
  59.6 28.7 %collective-permute-start.14 = (bf16[32,80,128]{2,1,0:T(8,128)(2,1)S(1)}, bf16[32,80,128]{2,1,0:T(8,128)(2,1)S(1)}, u32[]{:S(2)}, u32[]{:S(2)}) collective-permute-start(bf16[32,80,128]{2,1,0:T(8,128)(2,1)S(1)} %bitcast.82), channel_id=1, source_target_pairs={{0,192},{64,0},{128,64},{192,128},{1,193},{65,1},{129,65},{193,129... | collective-permute-start | bytes 1966088 | tf_op jit(solution)/shard_map/ppermute | solution.py:283
  90.2 1.0 copy-start.2
  91.2 1.0 copy-start.3
  92.2 8.2 %collective-permute-start.17 = (bf16[4,32,80,128]{3,2,1,0:T(8,128)(2,1)}, bf16[4,32,80,128]{3,2,1,0:T(8,128)(2,1)S(1)}, u32[]{:S(2)}, u32[]{:S(2)}) collective-permute-start(bf16[4,32,80,128]{3,2,1,0:T(8,128)(2,1)} %pad_maximum_fusion.1), channel_id=1, source_target_pairs={{0,1},{1,0},{2,3},{3,2},{4,5},{5,4},{6,7},{7,6},{8,9},{9,8},{10,11... | collective-permute-start | bytes 7864328 | tf_op jit(solution)/shard_map/ppermute | solution.py:285
  94.1 20.7 %collective-permute-start.18 = (bf16[16,128,256]{2,1,0:T(8,128)(2,1)}, bf16[16,128,256]{2,1,0:T(8,128)(2,1)}, u32[]{:S(2)}, u32[]{:S(2)}) collective-permute-start(bf16[16,128,256]{2,1,0:T(8,128)(2,1)} %bitcast.88), channel_id=1, source_target_pairs={{0,1},{1,0},{2,3},{3,2},{4,5},{5,4},{6,7},{7,6},{8,9},{9,8},{10,11... | collective-permute-start | bytes 3145736 | tf_op jit(solution)/shard_map/ppermute | solution.py:278
  94.1 31.5 %collective-permute-start.24 = (bf16[16,128,256]{2,1,0:T(8,128)(2,1)}, bf16[16,128,256]{2,1,0:T(8,128)(2,1)}, u32[]{:S(2)}, u32[]{:S(2)}) collective-permute-start(bf16[16,128,256]{2,1,0:T(8,128)(2,1)} %bitcast.87), channel_id=1, source_target_pairs={{0,4},{1,5},{2,6},{3,7},{4,0},{5,1},{6,2},{7,3},{8,12},{9,13},{10,... | collective-permute-start | bytes 3145736 | tf_op jit(solution)/shard_map/ppermute | solution.py:278
  94.5 49.8 %collective-permute-start.25 = (bf16[16,128,256]{2,1,0:T(8,128)(2,1)}, bf16[16,128,256]{2,1,0:T(8,128)(2,1)}, u32[]{:S(2)}, u32[]{:S(2)}) collective-permute-start(bf16[16,128,256]{2,1,0:T(8,128)(2,1)} %bitcast.86), channel_id=1, source_target_pairs={{0,5},{1,4},{2,7},{3,6},{4,1},{5,0},{6,3},{7,2},{8,13},{9,12},{10,... | collective-permute-start | bytes 3145736 | tf_op jit(solution)/shard_map/ppermute | solution.py:278
  100.5 2.3 %copy-start = (bf16[16,128,256]{2,1,0:T(8,128)(2,1)S(1)}, bf16[16,128,256]{2,1,0:T(8,128)(2,1)}, u32[]{:S(2)}) copy-start(bf16[16,128,256]{2,1,0:T(8,128)(2,1)} %grad_ref.1) | copy-start | bytes 3145732
  123.4 25.4 %collective-permute-start.19 = (bf16[4,96,96]{2,1,0:T(8,128)(2,1)S(1)}, bf16[4,96,96]{2,1,0:T(8,128)(2,1)S(1)}, u32[]{:S(2)}, u32[]{:S(2)}) collective-permute-start(bf16[4,96,96]{2,1,0:T(8,128)(2,1)S(1)} %get-tuple-element.46), channel_id=1, source_target_pairs={{0,1},{1,0},{2,3},{3,2},{4,5},{5,4},{6,7},{7,6},{8,9},{9,8},{10,11... | collective-permute-start | bytes 221192 | tf_op jit(solution)/shard_map/ppermute | solution.py:319
  124.2 26.3 %collective-permute-start.20 = (bf16[4,96,96]{2,1,0:T(8,128)(2,1)S(1)}, bf16[4,96,96]{2,1,0:T(8,128)(2,1)S(1)}, u32[]{:S(2)}, u32[]{:S(2)}) collective-permute-start(bf16[4,96,96]{2,1,0:T(8,128)(2,1)S(1)} %get-tuple-element.50), channel_id=1, source_target_pairs={{0,6},{1,7},{2,0},{3,1},{4,2},{5,3},{6,4},{7,5},{8,14},{9,15},{10,... | collective-permute-start | bytes 221192 | tf_op jit(solution)/shard_map/ppermute | solution.py:319
  124.2 29.8 %collective-permute-start.21 = (bf16[4,96,96]{2,1,0:T(8,128)(2,1)S(1)}, bf16[4,96,96]{2,1,0:T(8,128)(2,1)S(1)}, u32[]{:S(2)}, u32[]{:S(2)}) collective-permute-start(bf16[4,96,96]{2,1,0:T(8,128)(2,1)S(1)} %get-tuple-element.49), channel_id=1, source_target_pairs={{0,2},{1,3},{2,4},{3,5},{4,6},{5,7},{6,0},{7,1},{8,10},{9,11},{10,... | collective-permute-start | bytes 221192 | tf_op jit(solution)/shard_map/ppermute | solution.py:319
  125.6 28.3 %collective-permute-start.22 = (bf16[4,96,96]{2,1,0:T(8,128)(2,1)S(1)}, bf16[4,96,96]{2,1,0:T(8,128)(2,1)S(1)}, u32[]{:S(2)}, u32[]{:S(2)}) collective-permute-start(bf16[4,96,96]{2,1,0:T(8,128)(2,1)S(1)} %get-tuple-element.48), channel_id=1, source_target_pairs={{0,7},{1,6},{2,1},{3,0},{4,3},{5,2},{6,5},{7,4},{8,15},{9,14},{10,... | collective-permute-start | bytes 221192 | tf_op jit(solution)/shard_map/ppermute | solution.py:319
  144.3 9.6 %collective-permute-start.23 = (bf16[4,96,96]{2,1,0:T(8,128)(2,1)S(1)}, bf16[4,96,96]{2,1,0:T(8,128)(2,1)S(1)}, u32[]{:S(2)}, u32[]{:S(2)}) collective-permute-start(bf16[4,96,96]{2,1,0:T(8,128)(2,1)S(1)} %get-tuple-element.47), channel_id=1, source_target_pairs={{0,3},{1,2},{2,5},{3,4},{4,7},{5,6},{6,1},{7,0},{8,11},{9,10},{10,... | collective-permute-start | bytes 221192 | tf_op jit(solution)/shard_map/ppermute | solution.py:319
  148.8 5.1 %collective-permute-start.26 = (bf16[4,96,96]{2,1,0:T(8,128)(2,1)S(1)}, bf16[4,96,96]{2,1,0:T(8,128)(2,1)S(1)}, u32[]{:S(2)}, u32[]{:S(2)}) collective-permute-start(bf16[4,96,96]{2,1,0:T(8,128)(2,1)S(1)} %get-tuple-element.51), channel_id=1, source_target_pairs={{0,4},{1,5},{2,6},{3,7},{4,0},{5,1},{6,2},{7,3},{8,12},{9,13},{10,... | collective-permute-start | bytes 221192 | tf_op jit(solution)/shard_map/ppermute | solution.py:319
  150.5 7.9 %collective-permute-start.27 = (bf16[4,96,96]{2,1,0:T(8,128)(2,1)S(1)}, bf16[4,96,96]{2,1,0:T(8,128)(2,1)S(1)}, u32[]{:S(2)}, u32[]{:S(2)}) collective-permute-start(bf16[4,96,96]{2,1,0:T(8,128)(2,1)S(1)} %get-tuple-element.52), channel_id=1, source_target_pairs={{0,5},{1,4},{2,7},{3,6},{4,1},{5,0},{6,3},{7,2},{8,13},{9,12},{10,... | collective-permute-start | bytes 221192 | tf_op jit(solution)/shard_map/ppermute | solution.py:319
  159.3 5.9 %collective-permute-start.28 = (bf16[4,96,96]{2,1,0:T(8,128)(2,1)S(1)}, bf16[4,96,96]{2,1,0:T(8,128)(2,1)S(1)}, u32[]{:S(2)}, u32[]{:S(2)}) collective-permute-start(bf16[4,96,96]{2,1,0:T(8,128)(2,1)S(1)} %fusion.6), channel_id=1, source_target_pairs={{0,64},{64,128},{128,192},{192,0},{1,65},{65,129},{129,193},{193,1... | collective-permute-start | bytes 221192 | tf_op jit(solution)/shard_map/ppermute | solution.py:325
  160.1 7.1 %collective-permute-start.29 = (bf16[4,96,96]{2,1,0:T(8,128)(2,1)S(1)}, bf16[4,96,96]{2,1,0:T(8,128)(2,1)S(1)}, u32[]{:S(2)}, u32[]{:S(2)}) collective-permute-start(bf16[4,96,96]{2,1,0:T(8,128)(2,1)S(1)} %fusion.6), channel_id=1, source_target_pairs={{0,128},{64,192},{128,0},{192,64},{1,129},{65,193},{129,1},{193,65... | collective-permute-start | bytes 221192 | tf_op jit(solution)/shard_map/ppermute | solution.py:325
  161.9 5.8 %collective-permute-start.30 = (bf16[4,96,96]{2,1,0:T(8,128)(2,1)S(1)}, bf16[4,96,96]{2,1,0:T(8,128)(2,1)S(1)}, u32[]{:S(2)}, u32[]{:S(2)}) collective-permute-start(bf16[4,96,96]{2,1,0:T(8,128)(2,1)S(1)} %fusion.6), channel_id=1, source_target_pairs={{0,192},{64,0},{128,64},{192,128},{1,193},{65,1},{129,65},{193,129... | collective-permute-start | bytes 221192 | tf_op jit(solution)/shard_map/ppermute | solution.py:325
Sparse Core Ops, SparseCore 0:
  9.8 99.5 all-gather.1

commit v2 on v1

v2 whole, which is shorter than its diff:
```python
import functools

import jax
import jax.numpy as jnp
from jax import lax
from jax.experimental import pallas as pl
from jax.experimental.pallas import tpu as pltpu
from jax.sharding import PartitionSpec as P

SIDE = 16
CELLS = 256
GROUPS = 4
WIDTH = 32
CHANNELS = 128
NZ, NY, NC, NX = 8, 4, 2, 4
PIECE = 80
DEPTH = 8
BATCH = 4


def ep_perm(dz, dy, dc):
    pairs = []
    for z in range(NZ):
        for y in range(NY):
            for c in range(NC):
                to = ((z + dz) % NZ, (y + dy) % NY, c ^ dc)
                pairs.append(((z * NY + y) * NC + c, (to[0] * NY + to[1]) * NC + to[2]))
    return pairs


def rep_perm(dx):
    return [(x, (x + dx) % NX) for x in range(NX)]


def shifted(values, row_step, col_step, cell):
    if row_step == 0 and col_step == 0:
        return values
    rolled = pltpu.roll(values, (-(row_step * SIDE + col_step)) % CELLS, 1)
    row, col = cell // SIDE + row_step, cell % SIDE + col_step
    inside = (row >= 0) & (row < SIDE) & (col >= 0) & (col < SIDE)
    return jnp.where(inside, rolled, jnp.zeros_like(rolled))


def input_kernel(place_ref, gate_ref, grad_ref, weight_ref, out_ref, lhs_ref, rhs_ref, stage_ref):
    cell = lax.broadcasted_iota(jnp.int32, (1, CELLS), 1)
    lane_group = lax.broadcasted_iota(jnp.int32, (WIDTH, CHANNELS), 1) // WIDTH
    for j in range(BATCH):
        patch = pl.program_id(0) * BATCH + j
        grad = grad_ref[j]
        for b in (-1, 0, 1):
            by_col = shifted(grad, 0, -b, cell)
            for a in (-1, 0, 1):
                tap = 3 * (a + 1) + (b + 1)
                rhs_ref[j, tap * CHANNELS : (tap + 1) * CHANNELS, :] = shifted(by_col, -a, 0, cell)
        for k in range(2):
            for quarter in range(NX):
                stage_ref[j, k, quarter * PIECE : (quarter + 1) * PIECE, :] = weight_ref[
                    place_ref[(patch * 2 + k) * NX + quarter]
                ]
            for tap in range(9):
                kernel = stage_ref[j, k, tap * WIDTH : (tap + 1) * WIDTH, :]
                for group in range(GROUPS):
                    row = k * CHANNELS + group * WIDTH
                    lhs_ref[
                        j, row : row + WIDTH, tap * CHANNELS : (tap + 1) * CHANNELS
                    ] = jnp.where(lane_group == group, kernel, jnp.zeros_like(kernel))
        both = jnp.dot(lhs_ref[j], rhs_ref[j], preferred_element_type=jnp.float32)
        total = (
            gate_ref[patch * 2] * both[:CHANNELS] + gate_ref[patch * 2 + 1] * both[CHANNELS:]
        )
        out_ref[j] = total.astype(jnp.bfloat16)


def input_grads(place, gate, grad, weight):
    count = grad.shape[0]
    return pl.pallas_call(
        input_kernel,
        out_shape=jax.ShapeDtypeStruct(grad.shape, jnp.bfloat16),
        grid=(count // BATCH,),
        in_specs=[
            pl.BlockSpec(memory_space=pltpu.SMEM),
            pl.BlockSpec(memory_space=pltpu.SMEM),
            pl.BlockSpec((BATCH, CHANNELS, CELLS), lambda i: (i, 0, 0)),
            pl.BlockSpec(memory_space=pltpu.VMEM),
        ],
        out_specs=pl.BlockSpec((BATCH, CHANNELS, CELLS), lambda i: (i, 0, 0)),
        scratch_shapes=[
            pltpu.VMEM((BATCH, 2 * CHANNELS, 9 * CHANNELS), jnp.bfloat16),
            pltpu.VMEM((BATCH, 9 * CHANNELS, CELLS), jnp.bfloat16),
            pltpu.VMEM((BATCH, 2, NX * PIECE, CHANNELS), jnp.bfloat16),
        ],
        compiler_params=pltpu.CompilerParams(vmem_limit_bytes=28 << 20),
        cost_estimate=pl.CostEstimate(flops=1, bytes_accessed=1, transcendentals=0),
    )(place, gate, grad, weight)


def weight_kernel(chunks, plan, gate_of, grads, *refs):
    stash, out_refs, refs = refs[:chunks], refs[chunks : 2 * chunks], refs[2 * chunks :]
    grad_buf, stash_buf, lhs_a, rhs_a, lhs_b, rhs_b, total, sems = refs
    cell = lax.broadcasted_iota(jnp.int32, (1, CELLS), 1)
    pairs = plan[0]

    def start(pair):
        for j in range(2):
            slot = (pair % DEPTH) * 2 + j
            pltpu.make_async_copy(
                grads.at[plan[pair * 5 + 2 + j]], grad_buf.at[slot], sems.at[slot, 0]
            ).start()
        for chunk in range(chunks):

            @pl.when(plan[pair * 5 + 1] == chunk)
            def _(chunk=chunk):
                for j in range(2):
                    slot = (pair % DEPTH) * 2 + j
                    pltpu.make_async_copy(
                        stash[chunk].at[plan[pair * 5 + 4 + j]], stash_buf.at[slot], sems.at[slot, 1]
                    ).start()

    def finish(pair):
        for j in range(2):
            slot = (pair % DEPTH) * 2 + j
            pltpu.make_async_copy(grads.at[0], grad_buf.at[slot], sems.at[slot, 0]).wait()
            pltpu.make_async_copy(stash[0].at[0], stash_buf.at[slot], sems.at[slot, 1]).wait()

    def prepare(pair, lhs, rhs):
        for j in range(2):
            slot = (pair % DEPTH) * 2 + j
            cells = slice(j * CELLS, (j + 1) * CELLS)
            grad = grad_buf[slot].astype(jnp.float32) * gate_of[pair * 2 + j]
            grad = grad.astype(jnp.bfloat16)
            kept = stash_buf[slot]
            for i, step_by in enumerate((-1, 0, 1)):
                left = shifted(grad, -step_by, 0, cell)
                right = shifted(kept, 0, step_by, cell)
                for group in range(GROUPS):
                    rows = slice(group * WIDTH, (group + 1) * WIDTH)
                    lhs[group, i * WIDTH : (i + 1) * WIDTH, cells] = left[rows]
                    rhs[group, i * WIDTH : (i + 1) * WIDTH, cells] = right[rows]

    def multiply(pair, lhs, rhs):
        chunk = plan[pair * 5 + 1]
        for group in range(GROUPS):
            total[chunk, group] += lax.dot_general(
                lhs[group],
                rhs[group],
                (((1,), (1,)), ((), ())),
                preferred_element_type=jnp.float32,
            )

    for pair in range(DEPTH):

        @pl.when(pair < pairs)
        def _(pair=pair):
            start(jnp.int32(pair))

    total[...] = jnp.zeros_like(total)

    @pl.when(pairs > 0)
    def _():
        finish(jnp.int32(0))
        prepare(jnp.int32(0), lhs_a, rhs_a)

        @pl.when(DEPTH < pairs)
        def _():
            start(jnp.int32(DEPTH))

    def step(twice, carry):
        pair = twice * 2 + 1
        finish(pair)
        multiply(pair - 1, lhs_a, rhs_a)
        prepare(pair, lhs_b, rhs_b)

        @pl.when(pair + DEPTH < pairs)
        def _():
            start(pair + DEPTH)

        @pl.when(pair + 1 < pairs)
        def _():
            finish(pair + 1)

        multiply(pair, lhs_b, rhs_b)
        prepare(pair + 1, lhs_a, rhs_a)

        @pl.when(pair + 1 + DEPTH < pairs)
        def _():
            start(pair + 1 + DEPTH)

        return carry

    lax.fori_loop(0, pairs // 2, step, 0)
    for chunk in range(chunks):
        out_refs[chunk][...] = total[chunk].astype(out_refs[chunk].dtype)


def compact(row_of, gate_of):
    chunks, slots = row_of.shape
    length = chunks * slots
    used = row_of >= 0
    order = jnp.arange(slots, dtype=jnp.int32)
    rank = jnp.sum((used[:, :, None] & (order[:, None] < order[None, :])[None]).astype(jnp.int32), 1)
    padded = (jnp.sum(used.astype(jnp.int32), 1) + 1) // 2 * 2
    index = jnp.arange(chunks, dtype=jnp.int32)
    ends = jnp.sum(jnp.where(index[:, None] <= index[None, :], padded[:, None], 0), 0)
    where = (ends - padded)[:, None] + rank
    place = jnp.arange(length + 4, dtype=jnp.int32)
    hit = (used[:, :, None] & (where[:, :, None] == place)).astype(jnp.int32)
    rows = jnp.sum(hit * jnp.maximum(row_of, 0)[:, :, None], (0, 1))
    slot = jnp.sum(hit * order[None, :, None], (0, 1))
    gate = jnp.sum(jnp.where(hit > 0, gate_of[:, :, None], 0.0), (0, 1))
    chunk = jnp.sum((place[None, ::2] >= ends[:, None]).astype(jnp.int32), 0)
    chunk = jnp.minimum(chunk, chunks - 1)
    count = (ends[-1:] // 2 + 1) // 2 * 2
    pairs = jnp.concatenate([chunk[:, None], rows.reshape(-1, 2), slot.reshape(-1, 2)], 1)
    return jnp.concatenate([count, pairs.reshape(-1)]), gate


def weight_grads(plan, gate_of, grads, stash):
    chunks = len(stash)
    place = pl.BlockSpec(memory_space=pl.ANY)
    operand = pltpu.VMEM((GROUPS, 3 * WIDTH, 2 * CELLS), jnp.bfloat16)
    return pl.pallas_call(
        functools.partial(weight_kernel, chunks),
        out_shape=[jax.ShapeDtypeStruct((GROUPS, 3 * WIDTH, 3 * WIDTH), jnp.bfloat16)] * chunks,
        in_specs=[pl.BlockSpec(memory_space=pltpu.SMEM)] * 2 + [place] * (1 + chunks),
        out_specs=[pl.BlockSpec(memory_space=pltpu.VMEM)] * chunks,
        scratch_shapes=[
            pltpu.VMEM((2 * DEPTH, CHANNELS, CELLS), jnp.bfloat16),
            pltpu.VMEM((2 * DEPTH, CHANNELS, CELLS), jnp.bfloat16),
            operand,
            operand,
            operand,
            operand,
            pltpu.VMEM((chunks, GROUPS, 3 * WIDTH, 3 * WIDTH), jnp.float32),
            pltpu.SemaphoreType.DMA((2 * DEPTH, 2)),
        ],
        compiler_params=pltpu.CompilerParams(vmem_limit_bytes=56 << 20),
        cost_estimate=pl.CostEstimate(flops=1, bytes_accessed=1, transcendentals=0),
    )(plan, gate_of, grads, *stash)


def stack_of(first, others):
    return jnp.concatenate([first[None]] + [o[None] for o in others], 0)


def per_device(out_grad, routes, gates, stash, weights):
    x, e = lax.axis_index("rep"), lax.axis_index("ep")
    z, y, c = e // (NY * NC), e // NC % NY, e % NC
    rows, top = routes.shape
    groups = [[zz * NY * NC + r for zz in range(NZ)] for r in range(NY * NC)]
    grads = lax.all_gather(out_grad, "ep", axis=0, tiled=True, axis_index_groups=groups)

    kept = stash.reshape(NZ, NY, NC, 2, CHANNELS, CELLS)
    offsets = [(0, 0), (0, 1), (1, 0), (3, 0), (1, 1), (3, 1), (2, 0), (2, 1)]

    def sent(kept, d, dc):
        part = lax.dynamic_slice(
            kept, (0, (y + d) % NY, c ^ dc, 0, 0, 0), (NZ, 1, 1, 2, CHANNELS, CELLS)
        )
        return part.reshape(NZ * 2, CHANNELS, CELLS)

    first = [sent(kept, d, dc) for d, dc in offsets[2:4]]
    weights, *first = lax.optimization_barrier((weights, *first))
    mixed = weights[0].transpose(0, 3, 1, 2).reshape(9 * WIDTH, CHANNELS)
    mixed = jnp.pad(mixed, ((0, NX * PIECE - 9 * WIDTH), (0, 0)))
    piece = lax.dynamic_slice_in_dim(mixed, x * PIECE, PIECE, 0)
    note = jnp.concatenate(
        [routes.reshape(1, -1).astype(jnp.bfloat16), gates.reshape(1, -1)], 1
    )
    note = jnp.pad(note, ((0, 15), (0, CHANNELS - 2 * rows * top)))
    held = jnp.concatenate([piece, note], 0)
    kept, held, *first = lax.optimization_barrier((kept, held, *first))
    own, *rest = [sent(kept, d, dc) for d, dc in offsets[:2] + offsets[4:]]
    experts = [e - y * NC - c + ((y - d) % NY) * NC + (c ^ dc) for d, dc in offsets]
    experts = jnp.stack(experts)

    up = down = held
    from_z = {0: held}
    for d in range(1, NZ // 2 + 1):
        up = lax.ppermute(up, "ep", ep_perm(1, 0, 0))
        from_z[d] = up
        if d < NZ // 2:
            down = lax.ppermute(down, "ep", ep_perm(-1, 0, 0))
            from_z[NZ - d] = down
    held = jnp.stack([from_z[d] for d in range(NZ)])
    notes = held[:, PIECE, : 2 * rows * top].astype(jnp.float32)
    held = held[:, :PIECE]
    held, *rest = lax.optimization_barrier((held, *rest))
    rest = rest[:1] + first + rest[1:]
    chunks = [own] + [
        lax.ppermute(part, "ep", ep_perm(0, d, dc)) for part, (d, dc) in zip(rest, offsets[1:])
    ]
    held = stack_of(held, [lax.ppermute(held, "ep", ep_perm(0, d, 0)) for d in range(1, NY)])
    held = held.reshape(NY * NZ, PIECE, CHANNELS)
    held, chunks[2], chunks[3] = lax.optimization_barrier((held, chunks[2], chunks[3]))
    quarters = [held] + [lax.ppermute(held, "rep", rep_perm(d)) for d in range(1, NX)]
    quarters[2], chunks[4], chunks[5] = lax.optimization_barrier(
        (quarters[2], chunks[4], chunks[5])
    )
    quarters += [lax.ppermute(quarter, "ep", ep_perm(0, 0, 1)) for quarter in quarters]
    held = jnp.concatenate(quarters, 0)
    held, chunks[6] = lax.optimization_barrier((held, chunks[6]))
    held = held.reshape(NC * NX * NY * NZ, PIECE, CHANNELS)

    from_z = (z - jnp.arange(NZ, dtype=jnp.int32)) % NZ
    notes = jnp.sum(
        jnp.where((from_z[:, None] == jnp.arange(NZ)[None])[:, :, None], notes[:, None], 0.0), 0
    )
    named = notes[:, : rows * top].astype(jnp.int32)
    gate = notes[:, rows * top :]
    here = experts[:, None, None] == named[None]
    order = jnp.arange(rows * top, dtype=jnp.int32)
    before = (order[:, None] < order[None, :])[None, None] & here[:, :, :, None]
    earlier = jnp.sum(before.astype(jnp.int32), 2)
    chosen = here[:, :, None, :] & (earlier[:, :, None, :] == jnp.arange(2)[None, None, :, None])
    source_row = jnp.arange(NZ, dtype=jnp.int32)[:, None] * rows + (order // top)[None]
    row_of = jnp.max(jnp.where(chosen, source_row[None, :, None, :], -1), 3)
    gate_of = jnp.sum(jnp.where(chosen, gate[None, :, None, :], 0.0), 3)
    row_of, gate_of = row_of.reshape(8, NZ * 2), gate_of.reshape(8, NZ * 2)
    early, late = compact(row_of[:7], gate_of[:7]), compact(row_of[7:], gate_of[7:])
    flat = routes.reshape(-1)
    at_z, at_y, at_c = flat // (NY * NC), flat // NC % NY, flat % NC
    block = ((y - at_y) % NY) * NZ + (z - at_z) % NZ
    quarter = (x - jnp.arange(NX, dtype=jnp.int32)) % NX
    place = ((at_c ^ c)[:, None] * NX + quarter[None]) * (NZ * NY) + block[:, None]
    parts = list(weight_grads(*early, grads, chunks[:7]))
    parts[0], place = lax.optimization_barrier((parts[0], place))
    in_grad = input_grads(
        place.reshape(-1), gates.reshape(-1).astype(jnp.float32), out_grad, held
    )

    def returned(part, d, dc):
        if d or dc:
            part = lax.ppermute(part, "ep", ep_perm(0, -d, dc))
        return part.astype(jnp.float32)

    total = sum(returned(part, *offset) for part, offset in zip(parts, offsets))
    in_grad, total, plan = lax.optimization_barrier((in_grad, total, late[0]))
    (last,) = weight_grads(plan, late[1], grads, chunks[7:])
    total = total + returned(last, *offsets[7])
    total = total.astype(jnp.bfloat16)
    summed = total.astype(jnp.float32)
    for d in range(1, NX):
        summed = summed + lax.ppermute(total, "rep", rep_perm(d)).astype(jnp.float32)
    weight_grad = summed.reshape(GROUPS, 3, WIDTH, 3, WIDTH).transpose(1, 3, 0, 2, 4)
    return in_grad, weight_grad.reshape(1, 9, GROUPS, WIDTH, WIDTH)


def solution(mesh):
    return jax.shard_map(
        per_device,
        mesh=mesh,
        in_specs=(
            P(("rep", "ep"), None, None),
            P(("rep", "ep"), None),
            P(("rep", "ep"), None),
            P("rep", "ep", None, None, None, None),
            P("ep", None, None, None, None),
        ),
        out_specs=(P(("rep", "ep"), None, None), P("ep", None, None, None, None)),
        check_vma=False,
    )
```

time: 176 us -> 176 us (level)
  waiting for transfers between devices: 64.7 us -> 48.9 us
  local copies, waits for them, and re-layouts: 18.2 us -> 28.7 us
  Pallas kernels: 21.6 us -> 16.7 us
  between operations: 14.4 us -> 18.1 us
  other arithmetic: 7.44 us -> 10.6 us
  starting transfers between devices: 49.5 us -> 52.2 us
    ppermute x3, waiting for transfers between devices: 27.5 us -> 6.1 us  [per_device(): lax.ppermute(held, 'rep', rep_perm(d))]
    unnamed x21 -> x50, local copies, waits for them, and re-layouts: 2.92 us -> 11.2 us
    ppermute x8 -> x11, waiting for transfers between devices: 4.39 us -> 11.4 us  [the longest x7 11.3 us: returned(): part = lax.ppermute(part, 'ep', ep_perm(0, -d, dc))]
    ppermute x8 -> x11, starting transfers between devices: 9.92 us -> 14.9 us  [the longest x7 13.5 us: returned(): part = lax.ppermute(part, 'ep', ep_perm(0, -d, dc))]
    pallas_call x1, Pallas kernels: 10.5 us -> 6.11 us  [input_grads(): pl.pallas_call(input_kernel, out_shape=jax.ShapeDtypeStruct(grad.shape, j...]
    concatenate x3 -> x1, other arithmetic: 4.27 us -> 0.08 us  [stack_of(): return jnp.concatenate([first[None]] + [o[None] for o in others], 0)]
    reduce_sum x0 -> x10, other arithmetic: none -> 3.48 us  [the longest x2 2.05 us: compact(): gate = jnp.sum(jnp.where(hit > 0, gate_of[:, :, None], 0.0), (0, 1))]
    ppermute x7, starting transfers between devices: 14 us -> 11 us  [per_device(): lax.ppermute(part, 'ep', ep_perm(0, d, dc))]
  transfers between devices with their start and end apart: 32 -> 35, of which waited for: 11 -> 12; matrix products, arithmetic and copies ran while one was open for 12% -> 18% of each run, Pallas kernels for 12% -> 8%
where the time goes in v2:
time: 176 us; the launch traced here: 175 us
  starting transfers between devices  52.2 us (30%)
  waiting for transfers between devices  48.9 us (28%)
  local copies, waits for them, and re-layouts  28.7 us (16%)
  between operations  18.1 us (10%)
  Pallas kernels  16.7 us (9%)
  other arithmetic  10.6 us (6%)
    ppermute x7, waiting for transfers between devices, per_device(): lax.ppermute(part, 'ep', ep_perm(0, d, dc))  15.5 us
    ppermute x7, starting transfers between devices, returned(): part = lax.ppermute(part, 'ep', ep_perm(0, -d, dc))  13.5 us
    ppermute x7, waiting for transfers between devices, returned(): part = lax.ppermute(part, 'ep', ep_perm(0, -d, dc))  11.3 us
    unnamed x50, local copies, waits for them, and re-layouts  11.2 us
    ppermute x7, starting transfers between devices, per_device(): lax.ppermute(part, 'ep', ep_perm(0, d, dc))  11 us
    pallas_call x2, Pallas kernels, weight_grads(): pl.pallas_call(functools.partial(weight_kernel, chunks), out_shape=[jax.S...  10.6 us
    ppermute x3, starting transfers between devices, per_device(): down = lax.ppermute(down, 'ep', ep_perm(-1, 0, 0))  9.5 us
    ppermute x4, waiting for transfers between devices, per_device(): up = lax.ppermute(up, 'ep', ep_perm(1, 0, 0))  8.81 us
  transfers between devices with their start and end apart: 35, of which 12 were waited for; matrix products, arithmetic and copies ran while one was open for 18% of the time, Pallas kernels for 8%

profile of v2, /device:TPU:1, one launch (start us, length us, event | category | flops | bytes accessed | tf_op | source)
XLA Modules:
  0.0 175.2 jit_solution(17578835822244439916)
XLA Ops:
  7.2 0.7 all-gather.2.cloned.1.call-update
  8.0 3.1 %constant_dynamic-slice_fusion.6 = (bf16[8,1,1,2,128,256]{5,4,3,2,1,0:T(8,128)(2,1)}, bf16[8,1,1,2,128,256]{5,4,3,2,1,0:T(8,128)(2,1)}) fusion(bf16[8,4,2,2,128,256]{5,4,3,2,1,0:T(8,128)(2,1)} %bitcast.58, s32[]{:T(128)S(6)} %select_n.248, s32[]{:T(128)S(6)} %select_n.246, s32[]{:T(128)S(6)} %select_n.245), kind=kLoop, calls=%fused_computation.73 | loop fusion | bytes 4194316 | tf_op jit(solution)/shard_map/dynamic_slice | solution.py:256
  12.0 2.5 %collective-permute-start = (bf16[96,128]{1,0:T(8,128)(2,1)S(1)}, bf16[96,128]{1,0:T(8,128)(2,1)S(1)}, u32[]{:S(2)}, u32[]{:S(2)}) collective-permute-start(bf16[96,128]{1,0:T(8,128)(2,1)S(1)} %pad_maximum_fusion.1), channel_id=1, source_target_pairs={{0,8},{1,9},{2,10},{3,11},{4,12},{5,13},{6,14},{7,15},{8,16},{9,17... | collective-permute-start | bytes 73736 | tf_op jit(solution)/shard_map/ppermute | solution.py:279
  14.6 4.0 %collective-permute-start.4 = (bf16[96,128]{1,0:T(8,128)(2,1)S(1)}, bf16[96,128]{1,0:T(8,128)(2,1)S(1)}, u32[]{:S(2)}, u32[]{:S(2)}) collective-permute-start(bf16[96,128]{1,0:T(8,128)(2,1)S(1)} %pad_maximum_fusion.1), channel_id=1, source_target_pairs={{0,56},{1,57},{2,58},{3,59},{4,60},{5,61},{6,62},{7,63},{8,0},{9,1... | collective-permute-start | bytes 73736 | tf_op jit(solution)/shard_map/ppermute | solution.py:282
  18.6 1.3 collective-permute-start.11
  19.9 1.4 collective-permute-start.12
  21.8 0.7 multiply_add_fusion
  22.5 5.6 %constant_dynamic-slice_fusion = (bf16[8,1,1,2,128,256]{5,4,3,0,2,1:T(8,128)(2,1)}, bf16[8,1,1,2,128,256]{5,4,3,0,2,1:T(8,128)(2,1)}, bf16[8,1,1,2,128,256]{5,4,...) fusion(s32[]{:T(128)S(6)} %select_n.262, ...), kind=kLoop, calls=%fused_computation.67 | loop fusion | bytes 12582936 | tf_op jit(solution)/shard_map/dynamic_slice | solution.py:256
  28.8 2.7 %collective-permute-start.5 = (bf16[96,128]{1,0:T(8,128)(2,1)S(1)}, bf16[96,128]{1,0:T(8,128)(2,1)S(1)}, u32[]{:S(2)}, u32[]{:S(2)}) collective-permute-start(bf16[96,128]{1,0:T(8,128)(2,1)S(1)} %collective-permute-done.4), channel_id=1, source_target_pairs={{0,56},{1,57},{2,58},{3,59},{4,60},{5,61},{6,62},{7,63},{8,0},{9,1... | collective-permute-start | bytes 73736 | tf_op jit(solution)/shard_map/ppermute | solution.py:282
  31.5 2.0 %collective-permute-done.1 = bf16[96,128]{1,0:T(8,128)(2,1)S(1)} collective-permute-done((bf16[96,128]{1,0:T(8,128)(2,1)S(1)}, bf16[96,128]{1,0:T(8,128)(2,1)S(1)}, u32[]{:S(2)}, u32[]{:S(2)}) %collective-permute-start.1) | collective-permute-done | bytes 24608 | tf_op jit(solution)/shard_map/ppermute | solution.py:279
  33.6 2.7 %collective-permute-start.6 = (bf16[96,128]{1,0:T(8,128)(2,1)S(1)}, bf16[96,128]{1,0:T(8,128)(2,1)S(1)}, u32[]{:S(2)}, u32[]{:S(2)}) collective-permute-start(bf16[96,128]{1,0:T(8,128)(2,1)S(1)} %collective-permute-done.5), channel_id=1, source_target_pairs={{0,56},{1,57},{2,58},{3,59},{4,60},{5,61},{6,62},{7,63},{8,0},{9,1... | collective-permute-start | bytes 73736 | tf_op jit(solution)/shard_map/ppermute | solution.py:282
  36.3 2.0 %collective-permute-done.2 = bf16[96,128]{1,0:T(8,128)(2,1)S(1)} collective-permute-done((bf16[96,128]{1,0:T(8,128)(2,1)S(1)}, bf16[96,128]{1,0:T(8,128)(2,1)S(1)}, u32[]{:S(2)}, u32[]{:S(2)}) %collective-permute-start.2) | collective-permute-done | bytes 24608 | tf_op jit(solution)/shard_map/ppermute | solution.py:279
  38.3 4.8 %collective-permute-done.3 = bf16[96,128]{1,0:T(8,128)(2,1)S(1)} collective-permute-done((bf16[96,128]{1,0:T(8,128)(2,1)S(1)}, bf16[96,128]{1,0:T(8,128)(2,1)S(1)}, u32[]{:S(2)}, u32[]{:S(2)}) %collective-permute-start.3) | collective-permute-done | bytes 24608 | tf_op jit(solution)/shard_map/ppermute | solution.py:279
  43.3 2.6 %collective-permute-start.9 = (bf16[8,80,128]{2,1,0:T(8,128)(2,1)S(1)}, bf16[8,80,128]{2,1,0:T(8,128)(2,1)S(1)}, u32[]{:S(2)}, u32[]{:S(2)}) collective-permute-start(bf16[8,80,128]{2,1,0:T(8,128)(2,1)S(1)} %slice.51), channel_id=1, source_target_pairs={{0,4},{1,5},{2,6},{3,7},{4,0},{5,1},{6,2},{7,3},{8,12},{9,13},{10,... | collective-permute-start | bytes 491528 | tf_op jit(solution)/shard_map/ppermute | solution.py:292
  45.9 5.0 %collective-permute-start.14 = (bf16[16,128,256]{2,1,0:T(8,128)(2,1)}, bf16[16,128,256]{2,1,0:T(8,128)(2,1)}, u32[]{:S(2)}, u32[]{:S(2)}) collective-permute-start(bf16[16,128,256]{2,1,0:T(8,128)(2,1)} %bitcast.27), channel_id=1, source_target_pairs={{0,3},{1,2},{2,5},{3,4},{4,7},{5,6},{6,1},{7,0},{8,11},{9,10},{10,... | collective-permute-start | bytes 3145736 | tf_op jit(solution)/shard_map/ppermute | solution.py:290
  51.0 0.7 fusion.23
  53.2 0.6 convert_reduce_fusion.5
  54.5 2.2 %collective-permute-start.10 = (bf16[8,80,128]{2,1,0:T(8,128)(2,1)S(1)}, bf16[8,80,128]{2,1,0:T(8,128)(2,1)S(1)}, u32[]{:S(2)}, u32[]{:S(2)}) collective-permute-start(bf16[8,80,128]{2,1,0:T(8,128)(2,1)S(1)} %slice.51), channel_id=1, source_target_pairs={{0,6},{1,7},{2,0},{3,1},{4,2},{5,3},{6,4},{7,5},{8,14},{9,15},{10,... | collective-permute-start | bytes 491528 | tf_op jit(solution)/shard_map/ppermute | solution.py:292
  57.2 0.7 copy.122
  58.0 2.8 %collective-permute-done.10 = bf16[8,80,128]{2,1,0:T(8,128)(2,1)S(1)} collective-permute-done((bf16[8,80,128]{2,1,0:T(8,128)(2,1)S(1)}, bf16[8,80,128]{2,1,0:T(8,128)(2,1)S(1)}, u32[]{:S(2)}, u32[]{:S(2)}) %collective-permute-start.10) | collective-permute-done | bytes 163872 | tf_op jit(solution)/shard_map/ppermute | solution.py:292
  60.9 1.3 collective-permute-start.16
  62.3 0.5 minimum_bitcast_fusion
  62.8 2.5 %collective-permute-start.13 = (bf16[32,80,128]{2,1,0:T(8,128)(2,1)S(1)}, bf16[32,80,128]{2,1,0:T(8,128)(2,1)}, u32[]{:S(2)}, u32[]{:S(2)}) collective-permute-start(bf16[32,80,128]{2,1,0:T(8,128)(2,1)S(1)} %bitcast.63), channel_id=1, source_target_pairs={{0,128},{64,192},{128,0},{192,64},{1,129},{65,193},{129,1},{193,65... | collective-permute-start | bytes 1966088 | tf_op jit(solution)/shard_map/ppermute | solution.py:295
  65.4 0.7 reshape.720
  66.1 0.7 reshape.721
  66.9 1.1 collective-permute-start.17
  68.4 1.3 copy.109
  69.8 7.8 %collective-permute-done.14.refs_4_ = bf16[16,128,256]{2,1,0:T(8,128)(2,1)} collective-permute-done((bf16[16,128,256]{2,1,0:T(8,128)(2,1)}, bf16[16,128,256]{2,1,0:T(8,128)(2,1)}, u32[]{:S(2)}, u32[]{:S(2)}) %collective-permute-start.14) | collective-permute-done | bytes 1048608 | tf_op jit(solution)/shard_map/ppermute | solution.py:290
  77.6 0.5 collective-permute-start.18
  78.1 0.8 pad_add_fusion
  79.0 0.8 select_reduce_fusion
  79.9 0.8 pad_add_fusion.1
  80.7 1.2 slice.40
  84.8 1.4 select_reduce_fusion.2.gate_of
  86.6 6.1 %collective-permute-done.13 = bf16[32,80,128]{2,1,0:T(8,128)(2,1)} collective-permute-done((bf16[32,80,128]{2,1,0:T(8,128)(2,1)S(1)}, bf16[32,80,128]{2,1,0:T(8,128)(2,1)}, u32[]{:S(2)}, u32[]{:S(2)}) %collective-permute-start.13) | collective-permute-done | bytes 655392 | tf_op jit(solution)/shard_map/ppermute | solution.py:295
  92.7 1.9 %collective-permute-start.7 = (bf16[16,128,256]{2,1,0:T(8,128)(2,1)}, bf16[16,128,256]{2,1,0:T(8,128)(2,1)}, u32[]{:S(2)}, u32[]{:S(2)}) collective-permute-start(bf16[16,128,256]{2,1,0:T(8,128)(2,1)} %bitcast.68), channel_id=1, source_target_pairs={{0,1},{1,0},{2,3},{3,2},{4,5},{5,4},{6,7},{7,6},{8,9},{9,8},{10,11... | collective-permute-start | bytes 3145736 | tf_op jit(solution)/shard_map/ppermute | solution.py:290
  94.6 0.7 pad_add_fusion.2.plan
  95.7 0.6 collective-permute-start.21
  96.3 1.2 constant_dynamic-update-slice_fusion.13
  97.5 0.9 collective-permute-start.29
  98.4 1.2 constant_dynamic-update-slice_fusion.12
  99.6 1.2 constant_dynamic-update-slice_fusion.11
  100.8 1.2 constant_dynamic-update-slice_fusion.10
  102.2 2.4 %copy-done = bf16[256,80,128]{2,1,0:T(8,128)(2,1)} copy-done((bf16[256,80,128]{2,1,0:T(8,128)(2,1)}, bf16[256,80,128]{2,1,0:T(8,128)(2,1)S(1)}, u32[]{:S(2)}) %copy-start) | copy-done | bytes 5242904
  104.6 7.7 %collective-permute-done.22.refs_6_ = bf16[16,128,256]{2,1,0:T(8,128)(2,1)} collective-permute-done((bf16[16,128,256]{2,1,0:T(8,128)(2,1)}, bf16[16,128,256]{2,1,0:T(8,128)(2,1)}, u32[]{:S(2)}, u32[]{:S(2)}) %collective-permute-start.22) | collective-permute-done | bytes 1048608 | tf_op jit(solution)/shard_map/ppermute | solution.py:290
  112.3 7.3 %shard_map.68 = (bf16[4,96,96]{2,1,0:T(8,128)(2,1)}, bf16[4,96,96]{2,1,0:T(8,128)(2,1)}, bf16[4,96,96]{2,1,0:T(8,128)(2,1)}, bf16[4,96,96]{2,1,0:T(8,128)(2,1)},...) custom-call(s32[291]{0:T(512)} %pad_add_fusion.2.plan, ...), custom_call_target="tpu_custom_call" | custom-call | flops 1 | bytes 1 | tf_op jit(solution)/shard_map/pallas_call | solution.py:221
  119.7 2.3 %collective-permute-start.23 = (bf16[4,96,96]{2,1,0:T(8,128)(2,1)}, bf16[4,96,96]{2,1,0:T(8,128)(2,1)S(1)}, u32[]{:S(2)}, u32[]{:S(2)}) collective-permute-start(bf16[4,96,96]{2,1,0:T(8,128)(2,1)} %get-tuple-element.58), channel_id=1, source_target_pairs={{0,1},{1,0},{2,3},{3,2},{4,5},{5,4},{6,7},{7,6},{8,9},{9,8},{10,11... | collective-permute-start | bytes 221192 | tf_op jit(solution)/shard_map/ppermute | solution.py:333
  122.0 2.5 %collective-permute-start.24 = (bf16[4,96,96]{2,1,0:T(8,128)(2,1)}, bf16[4,96,96]{2,1,0:T(8,128)(2,1)S(1)}, u32[]{:S(2)}, u32[]{:S(2)}) collective-permute-start(bf16[4,96,96]{2,1,0:T(8,128)(2,1)} %get-tuple-element.59), channel_id=1, source_target_pairs={{0,6},{1,7},{2,0},{3,1},{4,2},{5,3},{6,4},{7,5},{8,14},{9,15},{10,... | collective-permute-start | bytes 221192 | tf_op jit(solution)/shard_map/ppermute | solution.py:333
  124.5 0.7 select_reduce_fusion.6.gate_of
  125.1 3.2 %collective-permute-start.26 = (bf16[4,96,96]{2,1,0:T(8,128)(2,1)}, bf16[4,96,96]{2,1,0:T(8,128)(2,1)S(1)}, u32[]{:S(2)}, u32[]{:S(2)}) collective-permute-start(bf16[4,96,96]{2,1,0:T(8,128)(2,1)} %get-tuple-element.61), channel_id=1, source_target_pairs={{0,7},{1,6},{2,1},{3,0},{4,3},{5,2},{6,5},{7,4},{8,15},{9,14},{10,... | collective-permute-start | bytes 221192 | tf_op jit(solution)/shard_map/ppermute | solution.py:333
  128.3 7.8 %collective-permute-done.24 = bf16[4,96,96]{2,1,0:T(8,128)(2,1)S(1)} collective-permute-done((bf16[4,96,96]{2,1,0:T(8,128)(2,1)}, bf16[4,96,96]{2,1,0:T(8,128)(2,1)S(1)}, u32[]{:S(2)}, u32[]{:S(2)}) %collective-permute-start.24) | collective-permute-done | bytes 73760 | tf_op jit(solution)/shard_map/ppermute | solution.py:333
  136.1 1.8 %collective-permute-start.28 = (bf16[4,96,96]{2,1,0:T(8,128)(2,1)}, bf16[4,96,96]{2,1,0:T(8,128)(2,1)S(1)}, u32[]{:S(2)}, u32[]{:S(2)}) collective-permute-start(bf16[4,96,96]{2,1,0:T(8,128)(2,1)} %get-tuple-element.63), channel_id=1, source_target_pairs={{0,4},{1,5},{2,6},{3,7},{4,0},{5,1},{6,2},{7,3},{8,12},{9,13},{10,... | collective-permute-start | bytes 221192 | tf_op jit(solution)/shard_map/ppermute | solution.py:333
  138.0 0.6 pad_add_fusion.3.plan
  138.7 2.5 %copy-done.1 = bf16[256,80,128]{2,1,0:T(8,128)(2,1)S(1)} copy-done((bf16[256,80,128]{2,1,0:T(8,128)(2,1)S(1)}, bf16[256,80,128]{2,1,0:T(8,128)(2,1)}, u32[]{:S(2)}) %copy-start.1) | copy-done | bytes 5242904
  141.2 6.1 %shard_map.69 = bf16[16,128,256]{2,1,0:T(8,128)(2,1)} custom-call(s32[128]{0:T(128)S(1)} %reshape.719.place_ref, f32[32]{0:T(128)S(1)} %reshape.726.gate_ref, bf16[16,128,256]{2,1,0:T(8,128)(2,1)S(1)} %copy-done.2, bf16[256,80,128]{2,1,0:T(8,128)(2,1)S(1)} %copy-done.1), custom_call_target="tpu_custom_call" | custom-call | flops 1 | bytes 1 | tf_op jit(solution)/shard_map/pallas_call | solution.py:76
  147.4 1.1 copy-done.5
  148.5 3.3 %shard_map.70 = bf16[4,96,96]{2,1,0:T(8,128)(2,1)} custom-call(s32[51]{0:T(128)} %pad_add_fusion.3.plan, f32[20]{0:T(128)} %select_reduce_fusion.6.gate_of, bf16[128,128,256]{2,1,0:T(8,128)(2,1)} %all-gather.2.cloned.1.call-done.grads, bf16[16,128,256]{2,1,0:T(8,128)(2,1)} %copy-done.5), custom_call_target="tpu_custom_call" | custom-call | flops 1 | bytes 1 | tf_op jit(solution)/shard_map/pallas_call | solution.py:221
  151.8 3.7 %collective-permute-start.30 = (bf16[4,96,96]{2,1,0:T(8,128)(2,1)}, bf16[4,96,96]{2,1,0:T(8,128)(2,1)S(1)}, u32[]{:S(2)}, u32[]{:S(2)}) collective-permute-start(bf16[4,96,96]{2,1,0:T(8,128)(2,1)} %shard_map.70), channel_id=1, source_target_pairs={{0,5},{1,4},{2,7},{3,6},{4,1},{5,0},{6,3},{7,2},{8,13},{9,12},{10,... | collective-permute-start | bytes 221192 | tf_op jit(solution)/shard_map/ppermute | solution.py:333
  155.5 3.5 %collective-permute-done.30 = bf16[4,96,96]{2,1,0:T(8,128)(2,1)S(1)} collective-permute-done((bf16[4,96,96]{2,1,0:T(8,128)(2,1)}, bf16[4,96,96]{2,1,0:T(8,128)(2,1)S(1)}, u32[]{:S(2)}, u32[]{:S(2)}) %collective-permute-start.30) | collective-permute-done | bytes 73760 | tf_op jit(solution)/shard_map/ppermute | solution.py:333
  159.2 3.2 %collective-permute-start.32 = (bf16[4,96,96]{2,1,0:T(8,128)(2,1)S(1)}, bf16[4,96,96]{2,1,0:T(8,128)(2,1)S(1)}, u32[]{:S(2)}, u32[]{:S(2)}) collective-permute-start(bf16[4,96,96]{2,1,0:T(8,128)(2,1)S(1)} %add_convert_fusion), channel_id=1, source_target_pairs={{0,128},{64,192},{128,0},{192,64},{1,129},{65,193},{129,1},{193,65... | collective-permute-start | bytes 221192 | tf_op jit(solution)/shard_map/ppermute | solution.py:343
  162.3 1.1 collective-permute-start.33
  163.8 2.2 %collective-permute-done.32 = bf16[4,96,96]{2,1,0:T(8,128)(2,1)S(1)} collective-permute-done((bf16[4,96,96]{2,1,0:T(8,128)(2,1)S(1)}, bf16[4,96,96]{2,1,0:T(8,128)(2,1)S(1)}, u32[]{:S(2)}, u32[]{:S(2)}) %collective-permute-start.32) | collective-permute-done | bytes 73760 | tf_op jit(solution)/shard_map/ppermute | solution.py:343
  166.1 1.0 collective-permute-done.33
  167.5 0.9 copy.124
  (148 shorter events, 7.7 us)
Async XLA Ops:
  7.2 3.9 %copy-start.6 = (bf16[1,9,4,32,32]{4,3,2,1,0:T(8,128)(2,1)S(1)}, bf16[1,9,4,32,32]{4,3,2,1,0:T(8,128)(2,1)}, u32[]{:S(2)}) copy-start(bf16[1,9,4,32,32]{4,3,2,1,0:T(8,128)(2,1)} %param.9) | copy-start | bytes 221188
  7.2 4.3 %copy-start.15 = (s32[16,2]{0,1:T(2,128)S(1)}, s32[16,2]{0,1:T(2,128)}, u32[]{:S(2)}) copy-start(s32[16,2]{0,1:T(2,128)} %param.6) | copy-start | bytes 388
  7.2 4.5 %copy-start.10 = (bf16[16,2]{0,1:T(2,128)(2,1)S(1)}, bf16[16,2]{0,1:T(2,128)(2,1)}, u32[]{:S(2)}) copy-start(bf16[16,2]{0,1:T(2,128)(2,1)} %param.7) | copy-start | bytes 196
  7.2 105.1 %all-gather.2.cloned.1.call-start = ((), (), s32[]{:S(2)}) async-start(), calls=%async_computation | async-start | bytes 9437184 | tf_op jit(solution)/shard_map/all_gather | solution.py:250
  12.0 16.6 %collective-permute-start = (bf16[96,128]{1,0:T(8,128)(2,1)S(1)}, bf16[96,128]{1,0:T(8,128)(2,1)S(1)}, u32[]{:S(2)}, u32[]{:S(2)}) collective-permute-start(bf16[96,128]{1,0:T(8,128)(2,1)S(1)} %pad_maximum_fusion.1), channel_id=1, source_target_pairs={{0,8},{1,9},{2,10},{3,11},{4,12},{5,13},{6,14},{7,15},{8,16},{9,17... | collective-permute-start | bytes 73736 | tf_op jit(solution)/shard_map/ppermute | solution.py:279
  14.6 14.2 %collective-permute-start.4 = (bf16[96,128]{1,0:T(8,128)(2,1)S(1)}, bf16[96,128]{1,0:T(8,128)(2,1)S(1)}, u32[]{:S(2)}, u32[]{:S(2)}) collective-permute-start(bf16[96,128]{1,0:T(8,128)(2,1)S(1)} %pad_maximum_fusion.1), channel_id=1, source_target_pairs={{0,56},{1,57},{2,58},{3,59},{4,60},{5,61},{6,62},{7,63},{8,0},{9,1... | collective-permute-start | bytes 73736 | tf_op jit(solution)/shard_map/ppermute | solution.py:282
  18.6 42.3 %collective-permute-start.11 = (bf16[16,128,256]{2,1,0:T(8,128)(2,1)}, bf16[16,128,256]{2,1,0:T(8,128)(2,1)S(1)}, u32[]{:S(2)}, u32[]{:S(2)}) collective-permute-start(bf16[16,128,256]{2,1,0:T(8,128)(2,1)} %bitcast.9), channel_id=1, source_target_pairs={{0,2},{1,3},{2,4},{3,5},{4,6},{5,7},{6,0},{7,1},{8,10},{9,11},{10,... | collective-permute-start | bytes 3145736 | tf_op jit(solution)/shard_map/ppermute | solution.py:290
  19.9 41.0 %collective-permute-start.12 = (bf16[16,128,256]{2,1,0:T(8,128)(2,1)}, bf16[16,128,256]{2,1,0:T(8,128)(2,1)S(1)}, u32[]{:S(2)}, u32[]{:S(2)}) collective-permute-start(bf16[16,128,256]{2,1,0:T(8,128)(2,1)} %bitcast.10), channel_id=1, source_target_pairs={{0,6},{1,7},{2,0},{3,1},{4,2},{5,3},{6,4},{7,5},{8,14},{9,15},{10,... | collective-permute-start | bytes 3145736 | tf_op jit(solution)/shard_map/ppermute | solution.py:290
  28.7 4.9 %collective-permute-start.1 = (bf16[96,128]{1,0:T(8,128)(2,1)S(1)}, bf16[96,128]{1,0:T(8,128)(2,1)S(1)}, u32[]{:S(2)}, u32[]{:S(2)}) collective-permute-start(bf16[96,128]{1,0:T(8,128)(2,1)S(1)} %collective-permute-done), channel_id=1, source_target_pairs={{0,8},{1,9},{2,10},{3,11},{4,12},{5,13},{6,14},{7,15},{8,16},{9,17... | collective-permute-start | bytes 73736 | tf_op jit(solution)/shard_map/ppermute | solution.py:279
  28.8 4.8 %collective-permute-start.5 = (bf16[96,128]{1,0:T(8,128)(2,1)S(1)}, bf16[96,128]{1,0:T(8,128)(2,1)S(1)}, u32[]{:S(2)}, u32[]{:S(2)}) collective-permute-start(bf16[96,128]{1,0:T(8,128)(2,1)S(1)} %collective-permute-done.4), channel_id=1, source_target_pairs={{0,56},{1,57},{2,58},{3,59},{4,60},{5,61},{6,62},{7,63},{8,0},{9,1... | collective-permute-start | bytes 73736 | tf_op jit(solution)/shard_map/ppermute | solution.py:282
  33.5 4.8 %collective-permute-start.2 = (bf16[96,128]{1,0:T(8,128)(2,1)S(1)}, bf16[96,128]{1,0:T(8,128)(2,1)S(1)}, u32[]{:S(2)}, u32[]{:S(2)}) collective-permute-start(bf16[96,128]{1,0:T(8,128)(2,1)S(1)} %collective-permute-done.1), channel_id=1, source_target_pairs={{0,8},{1,9},{2,10},{3,11},{4,12},{5,13},{6,14},{7,15},{8,16},{9,17... | collective-permute-start | bytes 73736 | tf_op jit(solution)/shard_map/ppermute | solution.py:279
  33.6 9.6 %collective-permute-start.6 = (bf16[96,128]{1,0:T(8,128)(2,1)S(1)}, bf16[96,128]{1,0:T(8,128)(2,1)S(1)}, u32[]{:S(2)}, u32[]{:S(2)}) collective-permute-start(bf16[96,128]{1,0:T(8,128)(2,1)S(1)} %collective-permute-done.5), channel_id=1, source_target_pairs={{0,56},{1,57},{2,58},{3,59},{4,60},{5,61},{6,62},{7,63},{8,0},{9,1... | collective-permute-start | bytes 73736 | tf_op jit(solution)/shard_map/ppermute | solution.py:282
  38.3 4.8 %collective-permute-start.3 = (bf16[96,128]{1,0:T(8,128)(2,1)S(1)}, bf16[96,128]{1,0:T(8,128)(2,1)S(1)}, u32[]{:S(2)}, u32[]{:S(2)}) collective-permute-start(bf16[96,128]{1,0:T(8,128)(2,1)S(1)} %collective-permute-done.2), channel_id=1, source_target_pairs={{0,8},{1,9},{2,10},{3,11},{4,12},{5,13},{6,14},{7,15},{8,16},{9,17... | collective-permute-start | bytes 73736 | tf_op jit(solution)/shard_map/ppermute | solution.py:279
  43.2 11.4 %collective-permute-start.8 = (bf16[8,80,128]{2,1,0:T(8,128)(2,1)S(1)}, bf16[8,80,128]{2,1,0:T(8,128)(2,1)S(1)}, u32[]{:S(2)}, u32[]{:S(2)}) collective-permute-start(bf16[8,80,128]{2,1,0:T(8,128)(2,1)S(1)} %slice.51), channel_id=1, source_target_pairs={{0,2},{1,3},{2,4},{3,5},{4,6},{5,7},{6,0},{7,1},{8,10},{9,11},{10,... | collective-permute-start | bytes 491528 | tf_op jit(solution)/shard_map/ppermute | solution.py:292
  43.3 13.7 %collective-permute-start.9 = (bf16[8,80,128]{2,1,0:T(8,128)(2,1)S(1)}, bf16[8,80,128]{2,1,0:T(8,128)(2,1)S(1)}, u32[]{:S(2)}, u32[]{:S(2)}) collective-permute-start(bf16[8,80,128]{2,1,0:T(8,128)(2,1)S(1)} %slice.51), channel_id=1, source_target_pairs={{0,4},{1,5},{2,6},{3,7},{4,0},{5,1},{6,2},{7,3},{8,12},{9,13},{10,... | collective-permute-start | bytes 491528 | tf_op jit(solution)/shard_map/ppermute | solution.py:292
  45.9 31.7 %collective-permute-start.14 = (bf16[16,128,256]{2,1,0:T(8,128)(2,1)}, bf16[16,128,256]{2,1,0:T(8,128)(2,1)}, u32[]{:S(2)}, u32[]{:S(2)}) collective-permute-start(bf16[16,128,256]{2,1,0:T(8,128)(2,1)} %bitcast.27), channel_id=1, source_target_pairs={{0,3},{1,2},{2,5},{3,4},{4,7},{5,6},{6,1},{7,0},{8,11},{9,10},{10,... | collective-permute-start | bytes 3145736 | tf_op jit(solution)/shard_map/ppermute | solution.py:290
  52.9 24.7 %copy-start.9 = (pred[7,16]{1,0:T(8,128)(4,1)}, pred[7,16]{1,0:T(8,128)(4,1)S(1)}, u32[]{:S(2)}) copy-start(pred[7,16]{1,0:T(8,128)(4,1)S(1)} %copy.105) | copy-start | bytes 340
  53.0 15.2 %copy-start.16 = (s32[7]{0:T(128)}, s32[7]{0:T(128)S(1)}, u32[]{:S(2)}) copy-start(s32[7]{0:T(128)S(1)} %select_reduce_fusion.9) | copy-start | bytes 88
  54.5 6.3 %collective-permute-start.10 = (bf16[8,80,128]{2,1,0:T(8,128)(2,1)S(1)}, bf16[8,80,128]{2,1,0:T(8,128)(2,1)S(1)}, u32[]{:S(2)}, u32[]{:S(2)}) collective-permute-start(bf16[8,80,128]{2,1,0:T(8,128)(2,1)S(1)} %slice.51), channel_id=1, source_target_pairs={{0,6},{1,7},{2,0},{3,1},{4,2},{5,3},{6,4},{7,5},{8,14},{9,15},{10,... | collective-permute-start | bytes 491528 | tf_op jit(solution)/shard_map/ppermute | solution.py:292
  57.0 20.6 %copy-start.11 = (pred[16]{0:T(512)(128)(4,1)}, pred[16]{0:T(512)(128)(4,1)S(1)}, u32[]{:S(2)}) copy-start(pred[16]{0:T(512)(128)(4,1)S(1)} %ge.58) | copy-start | bytes 52
  57.0 29.2 %collective-permute-start.15 = (bf16[16,128,256]{2,1,0:T(8,128)(2,1)}, bf16[16,128,256]{2,1,0:T(8,128)(2,1)}, u32[]{:S(2)}, u32[]{:S(2)}) collective-permute-start(bf16[16,128,256]{2,1,0:T(8,128)(2,1)} %bitcast.28), channel_id=1, source_target_pairs={{0,7},{1,6},{2,1},{3,0},{4,3},{5,2},{6,5},{7,4},{8,15},{9,14},{10,... | collective-permute-start | bytes 3145736 | tf_op jit(solution)/shard_map/ppermute | solution.py:290
  57.2 20.4 %copy-start.13 = (s32[16]{0:T(128)}, s32[16]{0:T(128)S(1)}, u32[]{:S(2)}) copy-start(s32[16]{0:T(128)S(1)} %convert_reduce_fusion.2) | copy-start | bytes 196
  60.9 41.3 %copy-start.3 = (bf16[16,128,256]{2,1,0:T(8,128)(2,1)}, bf16[16,128,256]{2,1,0:T(8,128)(2,1)S(1)}, u32[]{:S(2)}) copy-start(bf16[16,128,256]{2,1,0:T(8,128)(2,1)S(1)} %collective-permute-done.11.refs_2_) | copy-start | bytes 3145732
  60.9 41.3 %copy-start.4 = (bf16[16,128,256]{2,1,0:T(8,128)(2,1)}, bf16[16,128,256]{2,1,0:T(8,128)(2,1)S(1)}, u32[]{:S(2)}) copy-start(bf16[16,128,256]{2,1,0:T(8,128)(2,1)S(1)} %collective-permute-done.12.refs_3_) | copy-start | bytes 3145732
  60.9 18.8 %collective-permute-start.16 = (bf16[32,80,128]{2,1,0:T(8,128)(2,1)S(1)}, bf16[32,80,128]{2,1,0:T(8,128)(2,1)S(1)}, u32[]{:S(2)}, u32[]{:S(2)}) collective-permute-start(bf16[32,80,128]{2,1,0:T(8,128)(2,1)S(1)} %bitcast.62), channel_id=1, source_target_pairs={{0,64},{64,128},{128,192},{192,0},{1,65},{65,129},{129,193},{193,1... | collective-permute-start | bytes 1966088 | tf_op jit(solution)/shard_map/ppermute | solution.py:295
  62.8 29.9 %collective-permute-start.13 = (bf16[32,80,128]{2,1,0:T(8,128)(2,1)S(1)}, bf16[32,80,128]{2,1,0:T(8,128)(2,1)}, u32[]{:S(2)}, u32[]{:S(2)}) collective-permute-start(bf16[32,80,128]{2,1,0:T(8,128)(2,1)S(1)} %bitcast.63), channel_id=1, source_target_pairs={{0,128},{64,192},{128,0},{192,64},{1,129},{65,193},{129,1},{193,65... | collective-permute-start | bytes 1966088 | tf_op jit(solution)/shard_map/ppermute | solution.py:295
  66.9 28.6 %collective-permute-start.17 = (bf16[32,80,128]{2,1,0:T(8,128)(2,1)S(1)}, bf16[32,80,128]{2,1,0:T(8,128)(2,1)}, u32[]{:S(2)}, u32[]{:S(2)}) collective-permute-start(bf16[32,80,128]{2,1,0:T(8,128)(2,1)S(1)} %bitcast.64), channel_id=1, source_target_pairs={{0,192},{64,0},{128,64},{192,128},{1,193},{65,1},{129,65},{193,129... | collective-permute-start | bytes 1966088 | tf_op jit(solution)/shard_map/ppermute | solution.py:295
  77.6 18.1 %collective-permute-start.18 = (bf16[32,80,128]{2,1,0:T(8,128)(2,1)S(1)}, bf16[32,80,128]{2,1,0:T(8,128)(2,1)}, u32[]{:S(2)}, u32[]{:S(2)}) collective-permute-start(bf16[32,80,128]{2,1,0:T(8,128)(2,1)S(1)} %bitcast.65), channel_id=1, source_target_pairs={{0,1},{1,0},{2,3},{3,2},{4,5},{5,4},{6,7},{7,6},{8,9},{9,8},{10,11... | collective-permute-start | bytes 1966088 | tf_op jit(solution)/shard_map/ppermute | solution.py:299
  79.8 17.8 %collective-permute-start.19 = (bf16[32,80,128]{2,1,0:T(8,128)(2,1)S(1)}, bf16[32,80,128]{2,1,0:T(8,128)(2,1)}, u32[]{:S(2)}, u32[]{:S(2)}) collective-permute-start(bf16[32,80,128]{2,1,0:T(8,128)(2,1)S(1)} %collective-permute-done.16), channel_id=1, source_target_pairs={{0,1},{1,0},{2,3},{3,2},{4,5},{5,4},{6,7},{7,6},{8,9},{9,8},{10,11... | collective-permute-start | bytes 1966088 | tf_op jit(solution)/shard_map/ppermute | solution.py:299
  86.2 26.1 %collective-permute-start.22 = (bf16[16,128,256]{2,1,0:T(8,128)(2,1)}, bf16[16,128,256]{2,1,0:T(8,128)(2,1)}, u32[]{:S(2)}, u32[]{:S(2)}) collective-permute-start(bf16[16,128,256]{2,1,0:T(8,128)(2,1)} %bitcast.69), channel_id=1, source_target_pairs={{0,4},{1,5},{2,6},{3,7},{4,0},{5,1},{6,2},{7,3},{8,12},{9,13},{10,... | collective-permute-start | bytes 3145736 | tf_op jit(solution)/shard_map/ppermute | solution.py:290
  92.7 19.6 %collective-permute-start.7 = (bf16[16,128,256]{2,1,0:T(8,128)(2,1)}, bf16[16,128,256]{2,1,0:T(8,128)(2,1)}, u32[]{:S(2)}, u32[]{:S(2)}) collective-permute-start(bf16[16,128,256]{2,1,0:T(8,128)(2,1)} %bitcast.68), channel_id=1, source_target_pairs={{0,1},{1,0},{2,3},{3,2},{4,5},{5,4},{6,7},{7,6},{8,9},{9,8},{10,11... | collective-permute-start | bytes 3145736 | tf_op jit(solution)/shard_map/ppermute | solution.py:290
  95.5 6.5 %collective-permute-start.20 = (bf16[32,80,128]{2,1,0:T(8,128)(2,1)}, bf16[32,80,128]{2,1,0:T(8,128)(2,1)S(1)}, u32[]{:S(2)}, u32[]{:S(2)}) collective-permute-start(bf16[32,80,128]{2,1,0:T(8,128)(2,1)} %collective-permute-done.13), channel_id=1, source_target_pairs={{0,1},{1,0},{2,3},{3,2},{4,5},{5,4},{6,7},{7,6},{8,9},{9,8},{10,11... | collective-permute-start | bytes 1966088 | tf_op jit(solution)/shard_map/ppermute | solution.py:299
  95.7 6.4 %collective-permute-start.21 = (bf16[32,80,128]{2,1,0:T(8,128)(2,1)}, bf16[32,80,128]{2,1,0:T(8,128)(2,1)S(1)}, u32[]{:S(2)}, u32[]{:S(2)}) collective-permute-start(bf16[32,80,128]{2,1,0:T(8,128)(2,1)} %collective-permute-done.17), channel_id=1, source_target_pairs={{0,1},{1,0},{2,3},{3,2},{4,5},{5,4},{6,7},{7,6},{8,9},{9,8},{10,11... | collective-permute-start | bytes 1966088 | tf_op jit(solution)/shard_map/ppermute | solution.py:299
  97.5 49.9 %collective-permute-start.29 = (bf16[16,128,256]{2,1,0:T(8,128)(2,1)}, bf16[16,128,256]{2,1,0:T(8,128)(2,1)S(1)}, u32[]{:S(2)}, u32[]{:S(2)}) collective-permute-start(bf16[16,128,256]{2,1,0:T(8,128)(2,1)} %bitcast.67), channel_id=1, source_target_pairs={{0,5},{1,4},{2,7},{3,6},{4,1},{5,0},{6,3},{7,2},{8,13},{9,12},{10,... | collective-permute-start | bytes 3145736 | tf_op jit(solution)/shard_map/ppermute | solution.py:290
  102.2 2.4 %copy-start = (bf16[256,80,128]{2,1,0:T(8,128)(2,1)}, bf16[256,80,128]{2,1,0:T(8,128)(2,1)S(1)}, u32[]{:S(2)}) copy-start(bf16[256,80,128]{2,1,0:T(8,128)(2,1)S(1)} %constant_dynamic-update-slice_fusion.8.weight_ref) | copy-start | bytes 15728644
  112.3 12.1 %copy-start.12 = (pred[16]{0:T(512)(128)(4,1)S(1)}, pred[16]{0:T(512)(128)(4,1)}, u32[]{:S(2)}) copy-start(pred[16]{0:T(512)(128)(4,1)} %copy-done.11) | copy-start | bytes 52
  112.3 12.1 %copy-start.14 = (s32[16]{0:T(128)S(1)}, s32[16]{0:T(128)}, u32[]{:S(2)}) copy-start(s32[16]{0:T(128)} %copy-done.13) | copy-start | bytes 196
  112.3 26.2 %copy-start.8 = (s32[32,4]{1,0:T(8,128)S(1)}, s32[32,4]{1,0:T(8,128)}, u32[]{:S(2)}) copy-start(s32[32,4]{1,0:T(8,128)} %multiply_add_fusion) | copy-start | bytes 1540
  112.3 26.3 %copy-start.2 = (bf16[16,128,256]{2,1,0:T(8,128)(2,1)S(1)}, bf16[16,128,256]{2,1,0:T(8,128)(2,1)}, u32[]{:S(2)}) copy-start(bf16[16,128,256]{2,1,0:T(8,128)(2,1)} %grad_ref.1) | copy-start | bytes 3145732
  119.7 8.7 %collective-permute-start.23 = (bf16[4,96,96]{2,1,0:T(8,128)(2,1)}, bf16[4,96,96]{2,1,0:T(8,128)(2,1)S(1)}, u32[]{:S(2)}, u32[]{:S(2)}) collective-permute-start(bf16[4,96,96]{2,1,0:T(8,128)(2,1)} %get-tuple-element.58), channel_id=1, source_target_pairs={{0,1},{1,0},{2,3},{3,2},{4,5},{5,4},{6,7},{7,6},{8,9},{9,8},{10,11... | collective-permute-start | bytes 221192 | tf_op jit(solution)/shard_map/ppermute | solution.py:333
  122.0 14.2 %collective-permute-start.24 = (bf16[4,96,96]{2,1,0:T(8,128)(2,1)}, bf16[4,96,96]{2,1,0:T(8,128)(2,1)S(1)}, u32[]{:S(2)}, u32[]{:S(2)}) collective-permute-start(bf16[4,96,96]{2,1,0:T(8,128)(2,1)} %get-tuple-element.59), channel_id=1, source_target_pairs={{0,6},{1,7},{2,0},{3,1},{4,2},{5,3},{6,4},{7,5},{8,14},{9,15},{10,... | collective-permute-start | bytes 221192 | tf_op jit(solution)/shard_map/ppermute | solution.py:333
  125.1 22.1 %collective-permute-start.25 = (bf16[4,96,96]{2,1,0:T(8,128)(2,1)}, bf16[4,96,96]{2,1,0:T(8,128)(2,1)S(1)}, u32[]{:S(2)}, u32[]{:S(2)}) collective-permute-start(bf16[4,96,96]{2,1,0:T(8,128)(2,1)} %get-tuple-element.60), channel_id=1, source_target_pairs={{0,2},{1,3},{2,4},{3,5},{4,6},{5,7},{6,0},{7,1},{8,10},{9,11},{10,... | collective-permute-start | bytes 221192 | tf_op jit(solution)/shard_map/ppermute | solution.py:333
  125.1 22.1 %collective-permute-start.26 = (bf16[4,96,96]{2,1,0:T(8,128)(2,1)}, bf16[4,96,96]{2,1,0:T(8,128)(2,1)S(1)}, u32[]{:S(2)}, u32[]{:S(2)}) collective-permute-start(bf16[4,96,96]{2,1,0:T(8,128)(2,1)} %get-tuple-element.61), channel_id=1, source_target_pairs={{0,7},{1,6},{2,1},{3,0},{4,3},{5,2},{6,5},{7,4},{8,15},{9,14},{10,... | collective-permute-start | bytes 221192 | tf_op jit(solution)/shard_map/ppermute | solution.py:333
  128.3 19.0 %collective-permute-start.27 = (bf16[4,96,96]{2,1,0:T(8,128)(2,1)}, bf16[4,96,96]{2,1,0:T(8,128)(2,1)S(1)}, u32[]{:S(2)}, u32[]{:S(2)}) collective-permute-start(bf16[4,96,96]{2,1,0:T(8,128)(2,1)} %get-tuple-element.62), channel_id=1, source_target_pairs={{0,3},{1,2},{2,5},{3,4},{4,7},{5,6},{6,1},{7,0},{8,11},{9,10},{10,... | collective-permute-start | bytes 221192 | tf_op jit(solution)/shard_map/ppermute | solution.py:333
  136.1 11.2 %collective-permute-start.28 = (bf16[4,96,96]{2,1,0:T(8,128)(2,1)}, bf16[4,96,96]{2,1,0:T(8,128)(2,1)S(1)}, u32[]{:S(2)}, u32[]{:S(2)}) collective-permute-start(bf16[4,96,96]{2,1,0:T(8,128)(2,1)} %get-tuple-element.63), channel_id=1, source_target_pairs={{0,4},{1,5},{2,6},{3,7},{4,0},{5,1},{6,2},{7,3},{8,12},{9,13},{10,... | collective-permute-start | bytes 221192 | tf_op jit(solution)/shard_map/ppermute | solution.py:333
  138.7 2.5 %copy-start.1 = (bf16[256,80,128]{2,1,0:T(8,128)(2,1)S(1)}, bf16[256,80,128]{2,1,0:T(8,128)(2,1)}, u32[]{:S(2)}) copy-start(bf16[256,80,128]{2,1,0:T(8,128)(2,1)} %copy-done) | copy-start | bytes 15728644
  141.2 6.1 %copy-start.7 = (bf16[4,96,96]{2,1,0:T(8,128)(2,1)S(1)}, bf16[4,96,96]{2,1,0:T(8,128)(2,1)}, u32[]{:S(2)}) copy-start(bf16[4,96,96]{2,1,0:T(8,128)(2,1)} %get-tuple-element.57) | copy-start | bytes 221188
  147.4 1.1 copy-start.5
  151.8 7.2 %collective-permute-start.30 = (bf16[4,96,96]{2,1,0:T(8,128)(2,1)}, bf16[4,96,96]{2,1,0:T(8,128)(2,1)S(1)}, u32[]{:S(2)}, u32[]{:S(2)}) collective-permute-start(bf16[4,96,96]{2,1,0:T(8,128)(2,1)} %shard_map.70), channel_id=1, source_target_pairs={{0,5},{1,4},{2,7},{3,6},{4,1},{5,0},{6,3},{7,2},{8,13},{9,12},{10,... | collective-permute-start | bytes 221192 | tf_op jit(solution)/shard_map/ppermute | solution.py:333
  159.1 4.8 %collective-permute-start.31 = (bf16[4,96,96]{2,1,0:T(8,128)(2,1)S(1)}, bf16[4,96,96]{2,1,0:T(8,128)(2,1)S(1)}, u32[]{:S(2)}, u32[]{:S(2)}) collective-permute-start(bf16[4,96,96]{2,1,0:T(8,128)(2,1)S(1)} %add_convert_fusion), channel_id=1, source_target_pairs={{0,64},{64,128},{128,192},{192,0},{1,65},{65,129},{129,193},{193,1... | collective-permute-start | bytes 221192 | tf_op jit(solution)/shard_map/ppermute | solution.py:343
  159.2 6.9 %collective-permute-start.32 = (bf16[4,96,96]{2,1,0:T(8,128)(2,1)S(1)}, bf16[4,96,96]{2,1,0:T(8,128)(2,1)S(1)}, u32[]{:S(2)}, u32[]{:S(2)}) collective-permute-start(bf16[4,96,96]{2,1,0:T(8,128)(2,1)S(1)} %add_convert_fusion), channel_id=1, source_target_pairs={{0,128},{64,192},{128,0},{192,64},{1,129},{65,193},{129,1},{193,65... | collective-permute-start | bytes 221192 | tf_op jit(solution)/shard_map/ppermute | solution.py:343
  162.3 4.8 %collective-permute-start.33 = (bf16[4,96,96]{2,1,0:T(8,128)(2,1)S(1)}, bf16[4,96,96]{2,1,0:T(8,128)(2,1)S(1)}, u32[]{:S(2)}, u32[]{:S(2)}) collective-permute-start(bf16[4,96,96]{2,1,0:T(8,128)(2,1)S(1)} %add_convert_fusion), channel_id=1, source_target_pairs={{0,192},{64,0},{128,64},{192,128},{1,193},{65,1},{129,65},{193,129... | collective-permute-start | bytes 221192 | tf_op jit(solution)/shard_map/ppermute | solution.py:343
Sparse Core Ops, SparseCore 0:
  9.8 99.5 all-gather.1

commit v3 on v2

--- a/solution.py
+++ b/solution.py
@@ -94,8 +94,9 @@
     )(place, gate, grad, weight)
 
 
-def weight_kernel(chunks, plan, gate_of, grads, *refs):
-    stash, out_refs, refs = refs[:chunks], refs[chunks : 2 * chunks], refs[2 * chunks :]
+def weight_kernel(lies, plan, gate_of, grads, *refs):
+    chunks, arrays = len(lies), max(array for array, _ in lies) + 1
+    stash, out_refs, refs = refs[:arrays], refs[arrays : arrays + chunks], refs[arrays + chunks :]
     grad_buf, stash_buf, lhs_a, rhs_a, lhs_b, rhs_b, total, sems = refs
     cell = lax.broadcasted_iota(jnp.int32, (1, CELLS), 1)
     pairs = plan[0]
@@ -113,7 +114,8 @@
                 for j in range(2):
                     slot = (pair % DEPTH) * 2 + j
                     pltpu.make_async_copy(
-                        stash[chunk].at[plan[pair * 5 + 4 + j]], stash_buf.at[slot], sems.at[slot, 1]
+                        stash[lies[chunk][0]].at[plan[pair * 5 + 4 + j] + lies[chunk][1]],
+                        stash_buf.at[slot], sems.at[slot, 1]
                     ).start()
 
     def finish(pair):
@@ -214,14 +216,14 @@
     return jnp.concatenate([count, pairs.reshape(-1)]), gate
 
 
-def weight_grads(plan, gate_of, grads, stash):
-    chunks = len(stash)
+def weight_grads(plan, gate_of, grads, stash, lies):
+    chunks = len(lies)
     place = pl.BlockSpec(memory_space=pl.ANY)
     operand = pltpu.VMEM((GROUPS, 3 * WIDTH, 2 * CELLS), jnp.bfloat16)
     return pl.pallas_call(
-        functools.partial(weight_kernel, chunks),
+        functools.partial(weight_kernel, lies),
         out_shape=[jax.ShapeDtypeStruct((GROUPS, 3 * WIDTH, 3 * WIDTH), jnp.bfloat16)] * chunks,
-        in_specs=[pl.BlockSpec(memory_space=pltpu.SMEM)] * 2 + [place] * (1 + chunks),
+        in_specs=[pl.BlockSpec(memory_space=pltpu.SMEM)] * 2 + [place] * (1 + len(stash)),
         out_specs=[pl.BlockSpec(memory_space=pltpu.VMEM)] * chunks,
         scratch_shapes=[
             pltpu.VMEM((2 * DEPTH, CHANNELS, CELLS), jnp.bfloat16),
@@ -258,20 +260,29 @@
         )
         return part.reshape(NZ * 2, CHANNELS, CELLS)
 
-    first = [sent(kept, d, dc) for d, dc in offsets[2:4]]
-    weights, *first = lax.optimization_barrier((weights, *first))
+    def along(part, d, dc):
+        return lax.ppermute(part, "ep", ep_perm(0, d, dc))
+
     mixed = weights[0].transpose(0, 3, 1, 2).reshape(9 * WIDTH, CHANNELS)
     mixed = jnp.pad(mixed, ((0, NX * PIECE - 9 * WIDTH), (0, 0)))
-    piece = lax.dynamic_slice_in_dim(mixed, x * PIECE, PIECE, 0)
+    held = lax.dynamic_slice_in_dim(mixed, x * PIECE, PIECE, 0)
+    next_to = [sent(kept, d, dc) for d, dc in offsets[2:4]]
+    kept, held, *next_to = lax.optimization_barrier((kept, held, *next_to))
+    next_to += [sent(kept, d, dc) for d, dc in offsets[4:6]]
+    next_to = [along(part, d, dc) for part, (d, dc) in zip(next_to, offsets[2:6])]
+    experts = [e - y * NC - c + ((y - d) % NY) * NC + (c ^ dc) for d, dc in offsets]
+    experts = jnp.stack(experts)
+
+    held = stack_of(held, [along(held, d, 0) for d in range(1, NY)])
     note = jnp.concatenate(
         [routes.reshape(1, -1).astype(jnp.bfloat16), gates.reshape(1, -1)], 1
     )
     note = jnp.pad(note, ((0, 15), (0, CHANNELS - 2 * rows * top)))
-    held = jnp.concatenate([piece, note], 0)
-    kept, held, *first = lax.optimization_barrier((kept, held, *first))
-    own, *rest = [sent(kept, d, dc) for d, dc in offsets[:2] + offsets[4:]]
-    experts = [e - y * NC - c + ((y - d) % NY) * NC + (c ^ dc) for d, dc in offsets]
-    experts = jnp.stack(experts)
+    held = jnp.concatenate([held.reshape(NY * PIECE, CHANNELS), note], 0)
+
+    kept, held = lax.optimization_barrier((kept, held))
+    swapped = along(jnp.concatenate([sent(kept, 0, 1), sent(kept, 2, 1)], 0), 0, 1)
+    across = along(jnp.concatenate([sent(kept, 2, 0), swapped[NZ * 2 :]], 0), 2, 0)
 
     up = down = held
     from_z = {0: held}
@@ -282,24 +293,12 @@
             down = lax.ppermute(down, "ep", ep_perm(-1, 0, 0))
             from_z[NZ - d] = down
     held = jnp.stack([from_z[d] for d in range(NZ)])
-    notes = held[:, PIECE, : 2 * rows * top].astype(jnp.float32)
-    held = held[:, :PIECE]
-    held, *rest = lax.optimization_barrier((held, *rest))
-    rest = rest[:1] + first + rest[1:]
-    chunks = [own] + [
-        lax.ppermute(part, "ep", ep_perm(0, d, dc)) for part, (d, dc) in zip(rest, offsets[1:])
-    ]
-    held = stack_of(held, [lax.ppermute(held, "ep", ep_perm(0, d, 0)) for d in range(1, NY)])
-    held = held.reshape(NY * NZ, PIECE, CHANNELS)
-    held, chunks[2], chunks[3] = lax.optimization_barrier((held, chunks[2], chunks[3]))
+    notes = held[:, NY * PIECE, : 2 * rows * top].astype(jnp.float32)
+    held = held[:, : NY * PIECE].reshape(NZ * NY, PIECE, CHANNELS)
+    held, *next_to = lax.optimization_barrier((held, *next_to))
     quarters = [held] + [lax.ppermute(held, "rep", rep_perm(d)) for d in range(1, NX)]
-    quarters[2], chunks[4], chunks[5] = lax.optimization_barrier(
-        (quarters[2], chunks[4], chunks[5])
-    )
-    quarters += [lax.ppermute(quarter, "ep", ep_perm(0, 0, 1)) for quarter in quarters]
-    held = jnp.concatenate(quarters, 0)
-    held, chunks[6] = lax.optimization_barrier((held, chunks[6]))
-    held = held.reshape(NC * NX * NY * NZ, PIECE, CHANNELS)
+    quarters += [along(quarter, 0, 1) for quarter in quarters]
+    held = jnp.concatenate(quarters, 0).reshape(NC * NX * NY * NZ, PIECE, CHANNELS)
 
     from_z = (z - jnp.arange(NZ, dtype=jnp.int32)) % NZ
     notes = jnp.sum(
@@ -316,27 +315,24 @@
     row_of = jnp.max(jnp.where(chosen, source_row[None, :, None, :], -1), 3)
     gate_of = jnp.sum(jnp.where(chosen, gate[None, :, None, :], 0.0), 3)
     row_of, gate_of = row_of.reshape(8, NZ * 2), gate_of.reshape(8, NZ * 2)
-    early, late = compact(row_of[:7], gate_of[:7]), compact(row_of[7:], gate_of[7:])
+    early, late = compact(row_of[:6], gate_of[:6]), compact(row_of[6:], gate_of[6:])
     flat = routes.reshape(-1)
     at_z, at_y, at_c = flat // (NY * NC), flat // NC % NY, flat % NC
-    block = ((y - at_y) % NY) * NZ + (z - at_z) % NZ
+    block = ((z - at_z) % NZ) * NY + (y - at_y) % NY
     quarter = (x - jnp.arange(NX, dtype=jnp.int32)) % NX
     place = ((at_c ^ c)[:, None] * NX + quarter[None]) * (NZ * NY) + block[:, None]
-    parts = list(weight_grads(*early, grads, chunks[:7]))
-    parts[0], place = lax.optimization_barrier((parts[0], place))
     in_grad = input_grads(
         place.reshape(-1), gates.reshape(-1).astype(jnp.float32), out_grad, held
     )
-
-    def returned(part, d, dc):
-        if d or dc:
-            part = lax.ppermute(part, "ep", ep_perm(0, -d, dc))
-        return part.astype(jnp.float32)
-
-    total = sum(returned(part, *offset) for part, offset in zip(parts, offsets))
-    in_grad, total, plan = lax.optimization_barrier((in_grad, total, late[0]))
-    (last,) = weight_grads(plan, late[1], grads, chunks[7:])
-    total = total + returned(last, *offsets[7])
+    in_grad, plan = lax.optimization_barrier((in_grad, early[0]))
+    first = [sent(kept, 0, 0), swapped, *next_to]
+    parts = weight_grads(plan, early[1], grads, first, tuple((i, 0) for i in range(6)))
+    parts += weight_grads(*late, grads, [across], ((0, 0), (0, NZ * 2)))
+
+    total = None
+    for part, (d, dc) in zip(parts, offsets):
+        part = (along(part, -d, dc) if d or dc else part).astype(jnp.float32)
+        total = part if total is None else total + part
     total = total.astype(jnp.bfloat16)
     summed = total.astype(jnp.float32)
     for d in range(1, NX):

time: 176 us -> 205 us (1.16)
  the two profiles are of different devices: /device:TPU:1 before, /device:TPU:102 now
where the time goes in v3:
time: 205 us; the launch traced here: 203 us
  waiting for transfers between devices  82.8 us (40%)
  starting transfers between devices  45.3 us (22%)
  local copies, waits for them, and re-layouts  28.7 us (14%)
  between operations  20 us (10%)
  Pallas kernels  18 us (9%)
  other arithmetic  8.7 us (4%)
    ppermute x20, waiting for transfers between devices, along(): return lax.ppermute(part, 'ep', ep_perm(0, d, dc))  53.4 us
    ppermute x20, starting transfers between devices, along(): return lax.ppermute(part, 'ep', ep_perm(0, d, dc))  24 us
    ppermute x4, starting transfers between devices, per_device(): up = lax.ppermute(up, 'ep', ep_perm(1, 0, 0))  13.8 us
    pallas_call x2, Pallas kernels, weight_grads(): pl.pallas_call(functools.partial(weight_kernel, lies), out_shape=[jax.Sha...  11.8 us
    unnamed x30, local copies, waits for them, and re-layouts  11 us
    dynamic_slice x3, local copies, waits for them, and re-layouts, sent(): lax.dynamic_slice(kept, (0, (y + d) % NY, c ^ dc, 0, 0, 0), (NZ, 1, 1, 2,...  9.89 us
    ppermute x4, waiting for transfers between devices, per_device(): up = lax.ppermute(up, 'ep', ep_perm(1, 0, 0))  8.11 us
    ppermute x3, waiting for transfers between devices, per_device(): down = lax.ppermute(down, 'ep', ep_perm(-1, 0, 0))  7.95 us
  transfers between devices with their start and end apart: 34, of which 13 were waited for; matrix products, arithmetic and copies ran while one was open for 15% of the time, Pallas kernels for 9%

profile of v3, /device:TPU:102, one launch (start us, length us, event | category | flops | bytes accessed | tf_op | source)
XLA Modules:
  0.0 203.5 jit_solution(18047959805808917034)
XLA Ops:
  7.2 0.7 all-gather.2.cloned.1.call-update
  8.0 1.2 copy.103
  9.2 0.2 reshape.478
  9.4 3.1 %constant_dynamic-slice_fusion.6 = (bf16[8,1,1,2,128,256]{5,4,3,2,1,0:T(8,128)(2,1)}, bf16[8,1,1,2,128,256]{5,4,3,2,1,0:T(8,128)(2,1)}) fusion(bf16[8,4,2,2,128,256]{5,4,3,2,1,0:T(8,128)(2,1)} %bitcast.55, s32[]{:T(128)S(6)} %select_n.254, s32[]{:T(128)S(6)} %select_n.252, s32[]{:T(128)S(6)} %select_n.251), kind=kLoop, calls=%fused_computation.72 | loop fusion | bytes 4194316 | tf_op jit(solution)/shard_map/dynamic_slice | solution.py:258
  12.5 1.6 collective-permute-start
  14.1 2.9 %collective-permute-start.1 = (bf16[80,128]{1,0:T(8,128)(2,1)S(1)}, bf16[80,128]{1,0:T(8,128)(2,1)S(1)}, u32[]{:S(2)}, u32[]{:S(2)}) collective-permute-start(bf16[80,128]{1,0:T(8,128)(2,1)S(1)} %pad_dynamic-slice_fusion), channel_id=1, source_target_pairs={{0,4},{1,5},{2,6},{3,7},{4,0},{5,1},{6,2},{7,3},{8,12},{9,13},{10,... | collective-permute-start | bytes 61448 | tf_op jit(solution)/shard_map/ppermute | solution.py:264
  17.0 1.3 collective-permute-start.2
  18.3 3.1 %constant_dynamic-slice_fusion.4 = (bf16[8,1,1,2,128,256]{5,4,3,0,2,1:T(8,128)(2,1)}, bf16[8,1,1,2,128,256]{5,4,3,0,2,1:T(8,128)(2,1)}) fusion(s32[]{:T(128)S(6)} %select_n.254, s32[]{:T(128)S(6)} %select_n.255, s32[]{:T(128)S(6)} %select_n.251, bf16[8,4,2,2,128,256]{5,4,3,2,1,0:T(8,128)(2,1)} %bitcast.56), kind=kLoop, calls=%fused_computation.70 | loop fusion | bytes 4194316 | tf_op jit(solution)/shard_map/dynamic_slice | solution.py:258
  21.4 3.0 %collective-permute-start.13 = (bf16[16,128,256]{2,1,0:T(8,128)(2,1)}, bf16[16,128,256]{2,1,0:T(8,128)(2,1)}, u32[]{:S(2)}, u32[]{:S(2)}) collective-permute-start(bf16[16,128,256]{2,1,0:T(8,128)(2,1)} %bitcast.20), channel_id=1, source_target_pairs={{0,7},{1,6},{2,1},{3,0},{4,3},{5,2},{6,5},{7,4},{8,15},{9,14},{10,... | collective-permute-start | bytes 3145736 | tf_op jit(solution)/shard_map/ppermute | solution.py:264
  25.5 0.1 slice.48
  26.3 3.2 %collective-permute-start.3 = (bf16[336,128]{1,0:T(8,128)(2,1)S(1)}, bf16[336,128]{1,0:T(8,128)(2,1)S(1)}, u32[]{:S(2)}, u32[]{:S(2)}) collective-permute-start(bf16[336,128]{1,0:T(8,128)(2,1)S(1)} %pad_maximum_fusion.2), channel_id=1, source_target_pairs={{0,8},{1,9},{2,10},{3,11},{4,12},{5,13},{6,14},{7,15},{8,16},{9,17... | collective-permute-start | bytes 258056 | tf_op jit(solution)/shard_map/ppermute | solution.py:290
  29.5 3.7 %constant_dynamic-slice_fusion.3 = (bf16[8,1,1,2,128,256]{5,4,3,0,2,1:T(8,128)(2,1)}, bf16[8,1,1,2,128,256]{5,4,3,0,2,1:T(8,128)(2,1)S(1)}, bf16[8,1,1,2,128,256...) fusion(s32[]{:T(128)S(6)} %select_n.270, s32[]{:T(128)S(6)} %select_n.252, s32[]{:T(128)S(6)} %select_n.272, ...), kind=kLoop, calls=%fused_computation.69 | loop fusion | bytes 8388624 | tf_op jit(solution)/shard_map/dynamic_slice | solution.py:258
  33.2 1.5 pad_maximum_fusion
  34.7 3.2 %collective-permute-start.4 = (bf16[336,128]{1,0:T(8,128)(2,1)S(1)}, bf16[336,128]{1,0:T(8,128)(2,1)S(1)}, u32[]{:S(2)}, u32[]{:S(2)}) collective-permute-start(bf16[336,128]{1,0:T(8,128)(2,1)S(1)} %collective-permute-done.3), channel_id=1, source_target_pairs={{0,8},{1,9},{2,10},{3,11},{4,12},{5,13},{6,14},{7,15},{8,16},{9,17... | collective-permute-start | bytes 258056 | tf_op jit(solution)/shard_map/ppermute | solution.py:290
  38.0 3.7 %collective-permute-done.4 = bf16[336,128]{1,0:T(8,128)(2,1)S(1)} collective-permute-done((bf16[336,128]{1,0:T(8,128)(2,1)S(1)}, bf16[336,128]{1,0:T(8,128)(2,1)S(1)}, u32[]{:S(2)}, u32[]{:S(2)}) %collective-permute-start.4) | collective-permute-done | bytes 86048 | tf_op jit(solution)/shard_map/ppermute | solution.py:290
  41.8 3.7 %collective-permute-start.5 = (bf16[336,128]{1,0:T(8,128)(2,1)S(1)}, bf16[336,128]{1,0:T(8,128)(2,1)S(1)}, u32[]{:S(2)}, u32[]{:S(2)}) collective-permute-start(bf16[336,128]{1,0:T(8,128)(2,1)S(1)} %collective-permute-done.4), channel_id=1, source_target_pairs={{0,8},{1,9},{2,10},{3,11},{4,12},{5,13},{6,14},{7,15},{8,16},{9,17... | collective-permute-start | bytes 258056 | tf_op jit(solution)/shard_map/ppermute | solution.py:290
  45.5 3.8 %collective-permute-done.5 = bf16[336,128]{1,0:T(8,128)(2,1)S(1)} collective-permute-done((bf16[336,128]{1,0:T(8,128)(2,1)S(1)}, bf16[336,128]{1,0:T(8,128)(2,1)S(1)}, u32[]{:S(2)}, u32[]{:S(2)}) %collective-permute-start.5) | collective-permute-done | bytes 86048 | tf_op jit(solution)/shard_map/ppermute | solution.py:290
  49.3 3.7 %collective-permute-start.6 = (bf16[336,128]{1,0:T(8,128)(2,1)S(1)}, bf16[336,128]{1,0:T(8,128)(2,1)S(1)}, u32[]{:S(2)}, u32[]{:S(2)}) collective-permute-start(bf16[336,128]{1,0:T(8,128)(2,1)S(1)} %collective-permute-done.5), channel_id=1, source_target_pairs={{0,8},{1,9},{2,10},{3,11},{4,12},{5,13},{6,14},{7,15},{8,16},{9,17... | collective-permute-start | bytes 258056 | tf_op jit(solution)/shard_map/ppermute | solution.py:290
  53.0 3.2 %collective-permute-start.11 = (bf16[16,128,256]{2,1,0:T(8,128)(2,1)}, bf16[16,128,256]{2,1,0:T(8,128)(2,1)}, u32[]{:S(2)}, u32[]{:S(2)}) collective-permute-start(bf16[16,128,256]{2,1,0:T(8,128)(2,1)} %bitcast.4), channel_id=1, source_target_pairs={{0,6},{1,7},{2,0},{3,1},{4,2},{5,3},{6,4},{7,5},{8,14},{9,15},{10,... | collective-permute-start | bytes 3145736 | tf_op jit(solution)/shard_map/ppermute | solution.py:264
  56.2 0.6 collective-permute-done.6
  56.8 7.9 %collective-permute-done.9 = bf16[336,128]{1,0:T(8,128)(2,1)S(1)} collective-permute-done((bf16[336,128]{1,0:T(8,128)(2,1)S(1)}, bf16[336,128]{1,0:T(8,128)(2,1)S(1)}, u32[]{:S(2)}, u32[]{:S(2)}) %collective-permute-start.9) | collective-permute-done | bytes 86048 | tf_op jit(solution)/shard_map/ppermute | solution.py:293
  64.8 0.9 slice.56
  66.0 0.4 convert_reduce_fusion
  66.3 0.4 select_reduce_fusion.1
  66.7 0.2 convert_reduce_fusion.3
  67.2 0.1 copy.127
  68.7 0.4 collective-permute-done.21.refs_1_
  69.2 1.7 pad_maximum_fusion.1
  70.9 2.1 %collective-permute-start.27 = (bf16[32,128,256]{2,1,0:T(8,128)(2,1)}, bf16[32,128,256]{2,1,0:T(8,128)(2,1)}, u32[]{:S(2)}, u32[]{:S(2)}) collective-permute-start(bf16[32,128,256]{2,1,0:T(8,128)(2,1)} %pad_maximum_fusion.1), channel_id=1, source_target_pairs={{0,4},{1,5},{2,6},{3,7},{4,0},{5,1},{6,2},{7,3},{8,12},{9,13},{10,... | collective-permute-start | bytes 6291464 | tf_op jit(solution)/shard_map/ppermute | solution.py:264
  73.0 47.4 %collective-permute-done.11.refs_3_ = bf16[16,128,256]{2,1,0:T(8,128)(2,1)} collective-permute-done((bf16[16,128,256]{2,1,0:T(8,128)(2,1)}, bf16[16,128,256]{2,1,0:T(8,128)(2,1)}, u32[]{:S(2)}, u32[]{:S(2)}) %collective-permute-start.11) | collective-permute-done | bytes 1048608 | tf_op jit(solution)/shard_map/ppermute | solution.py:264
  120.4 0.5 collective-permute-start.14
  121.7 2.4 %collective-permute-start.15 = (bf16[32,80,128]{2,1,0:T(8,128)(2,1)}, bf16[32,80,128]{2,1,0:T(8,128)(2,1)}, u32[]{:S(2)}, u32[]{:S(2)}) collective-permute-start(bf16[32,80,128]{2,1,0:T(8,128)(2,1)} %bitcast.18), channel_id=1, source_target_pairs={{0,128},{64,192},{128,0},{192,64},{1,129},{65,193},{129,1},{193,65... | collective-permute-start | bytes 1966088 | tf_op jit(solution)/shard_map/ppermute | solution.py:299
  124.6 0.6 select_reduce_fusion.6.gate_of
  125.2 0.7 select_reduce_fusion.2.gate_of
  126.0 0.6 slice.47
  129.3 2.0 collective-permute-done.14
  131.3 0.6 pad_add_fusion.2.plan
  132.0 0.6 slice.52
  135.2 0.6 collective-permute-start.19
  135.8 1.1 constant_dynamic-update-slice_fusion.7
  136.9 4.3 %collective-permute-done.16 = bf16[32,80,128]{2,1,0:T(8,128)(2,1)} collective-permute-done((bf16[32,80,128]{2,1,0:T(8,128)(2,1)}, bf16[32,80,128]{2,1,0:T(8,128)(2,1)}, u32[]{:S(2)}, u32[]{:S(2)}) %collective-permute-start.16) | collective-permute-done | bytes 655392 | tf_op jit(solution)/shard_map/ppermute | solution.py:299
  141.2 1.2 constant_dynamic-update-slice_fusion.6
  142.4 1.2 constant_dynamic-update-slice_fusion.5
  143.5 1.2 constant_dynamic-update-slice_fusion.4
  144.7 1.2 constant_dynamic-update-slice_fusion.3
  146.2 2.3 %copy-done = bf16[256,80,128]{2,1,0:T(8,128)(2,1)} copy-done((bf16[256,80,128]{2,1,0:T(8,128)(2,1)}, bf16[256,80,128]{2,1,0:T(8,128)(2,1)S(1)}, u32[]{:S(2)}) %copy-start) | copy-done | bytes 5242904
  148.6 2.5 %copy-done.1 = bf16[256,80,128]{2,1,0:T(8,128)(2,1)S(1)} copy-done((bf16[256,80,128]{2,1,0:T(8,128)(2,1)S(1)}, bf16[256,80,128]{2,1,0:T(8,128)(2,1)}, u32[]{:S(2)}) %copy-start.1) | copy-done | bytes 5242904
  151.1 6.2 %shard_map.68 = bf16[16,128,256]{2,1,0:T(8,128)(2,1)} custom-call(s32[128]{0:T(128)S(1)} %add.362.place_ref, f32[32]{0:T(128)S(1)} %reshape.498.gate_ref, bf16[16,128,256]{2,1,0:T(8,128)(2,1)S(1)} %copy-done.2, bf16[256,80,128]{2,1,0:T(8,128)(2,1)S(1)} %copy-done.1), custom_call_target="tpu_custom_call" | custom-call | flops 1 | bytes 1 | tf_op jit(solution)/shard_map/pallas_call | solution.py:76
  157.3 7.8 %shard_map.69 = (bf16[4,96,96]{2,1,0:T(8,128)(2,1)}, bf16[4,96,96]{2,1,0:T(8,128)(2,1)}, bf16[4,96,96]{2,1,0:T(8,128)(2,1)}, bf16[4,96,96]{2,1,0:T(8,128)(2,1)},...) custom-call(s32[251]{0:T(256)} %pad_add_fusion.2.plan, f32[100]{0:T(128)} %select_reduce_fusion.2.gate_of, ...), custom_call_target="tpu_custom_call" | custom-call | flops 1 | bytes 1 | tf_op jit(solution)/shard_map/pallas_call | solution.py:223
  165.2 2.8 %collective-permute-start.23 = (bf16[4,96,96]{2,1,0:T(8,128)(2,1)}, bf16[4,96,96]{2,1,0:T(8,128)(2,1)S(1)}, u32[]{:S(2)}, u32[]{:S(2)}) collective-permute-start(bf16[4,96,96]{2,1,0:T(8,128)(2,1)} %get-tuple-element.38), channel_id=1, source_target_pairs={{0,6},{1,7},{2,0},{3,1},{4,2},{5,3},{6,4},{7,5},{8,14},{9,15},{10,... | collective-permute-start | bytes 221192 | tf_op jit(solution)/shard_map/ppermute | solution.py:264
  168.0 0.6 pad_add_fusion.3.plan
  168.6 2.6 %collective-permute-start.25 = (bf16[4,96,96]{2,1,0:T(8,128)(2,1)}, bf16[4,96,96]{2,1,0:T(8,128)(2,1)S(1)}, u32[]{:S(2)}, u32[]{:S(2)}) collective-permute-start(bf16[4,96,96]{2,1,0:T(8,128)(2,1)} %get-tuple-element.40), channel_id=1, source_target_pairs={{0,7},{1,6},{2,1},{3,0},{4,3},{5,2},{6,5},{7,4},{8,15},{9,14},{10,... | collective-permute-start | bytes 221192 | tf_op jit(solution)/shard_map/ppermute | solution.py:264
  171.2 4.0 %shard_map.70 = (bf16[4,96,96]{2,1,0:T(8,128)(2,1)}, bf16[4,96,96]{2,1,0:T(8,128)(2,1)}) custom-call(s32[91]{0:T(128)} %pad_add_fusion.3.plan, f32[36]{0:T(128)} %select_reduce_fusion.6.gate_of, bf16[128,128,256]{2,1,0:T(8,128)(2,1)} %all-gather.2.cloned.1.call-done.grads, bf16[32,128,256]{2,1,0:T(8,128)(2,1)} %collective-permute-done.27.refs_0_), custom_call_target="tpu_custom_call" | custom-call | flops 1 | bytes 1 | tf_op jit(solution)/shard_map/pallas_call | solution.py:223
  175.3 0.9 collective-permute-start.28
  176.2 2.8 %collective-permute-start.29 = (bf16[4,96,96]{2,1,0:T(8,128)(2,1)}, bf16[4,96,96]{2,1,0:T(8,128)(2,1)S(1)}, u32[]{:S(2)}, u32[]{:S(2)}) collective-permute-start(bf16[4,96,96]{2,1,0:T(8,128)(2,1)} %get-tuple-element.43), channel_id=1, source_target_pairs={{0,5},{1,4},{2,7},{3,6},{4,1},{5,0},{6,3},{7,2},{8,13},{9,12},{10,... | collective-permute-start | bytes 221192 | tf_op jit(solution)/shard_map/ppermute | solution.py:264
  179.0 3.7 %collective-permute-done.28 = bf16[4,96,96]{2,1,0:T(8,128)(2,1)S(1)} collective-permute-done((bf16[4,96,96]{2,1,0:T(8,128)(2,1)}, bf16[4,96,96]{2,1,0:T(8,128)(2,1)S(1)}, u32[]{:S(2)}, u32[]{:S(2)}) %collective-permute-start.28) | collective-permute-done | bytes 73760 | tf_op jit(solution)/shard_map/ppermute | solution.py:264
  182.7 1.7 collective-permute-done.29
  184.5 2.4 %collective-permute-start.30 = (bf16[4,96,96]{2,1,0:T(8,128)(2,1)S(1)}, bf16[4,96,96]{2,1,0:T(8,128)(2,1)S(1)}, u32[]{:S(2)}, u32[]{:S(2)}) collective-permute-start(bf16[4,96,96]{2,1,0:T(8,128)(2,1)S(1)} %add_convert_fusion), channel_id=1, source_target_pairs={{0,64},{64,128},{128,192},{192,0},{1,65},{65,129},{129,193},{193,1... | collective-permute-start | bytes 221192 | tf_op jit(solution)/shard_map/ppermute | solution.py:339
  187.0 2.0 collective-permute-start.31
  189.0 1.5 collective-permute-done.30
  190.5 3.3 %collective-permute-done.31 = bf16[4,96,96]{2,1,0:T(8,128)(2,1)S(1)} collective-permute-done((bf16[4,96,96]{2,1,0:T(8,128)(2,1)S(1)}, bf16[4,96,96]{2,1,0:T(8,128)(2,1)S(1)}, u32[]{:S(2)}, u32[]{:S(2)}) %collective-permute-start.31) | collective-permute-done | bytes 73760 | tf_op jit(solution)/shard_map/ppermute | solution.py:339
  193.8 1.6 collective-permute-done.32
  195.4 0.3 reshape.496
  195.7 0.9 copy.126
  (134 shorter events, 5.8 us)
Async XLA Ops:
  7.2 17.2 %copy-start.6 = (s32[16,2]{0,1:T(2,128)S(1)}, s32[16,2]{0,1:T(2,128)}, u32[]{:S(2)}) copy-start(s32[16,2]{0,1:T(2,128)} %param.6) | copy-start | bytes 388
  7.2 17.5 %copy-start.5 = (bf16[16,2]{0,1:T(2,128)(2,1)S(1)}, bf16[16,2]{0,1:T(2,128)(2,1)}, u32[]{:S(2)}) copy-start(bf16[16,2]{0,1:T(2,128)(2,1)} %param.7) | copy-start | bytes 196
  7.2 150.1 %all-gather.2.cloned.1.call-start = ((), (), s32[]{:S(2)}) async-start(), calls=%async_computation | async-start | bytes 9437184 | tf_op jit(solution)/shard_map/all_gather | solution.py:252
  12.5 13.6 %collective-permute-start = (bf16[80,128]{1,0:T(8,128)(2,1)S(1)}, bf16[80,128]{1,0:T(8,128)(2,1)S(1)}, u32[]{:S(2)}, u32[]{:S(2)}) collective-permute-start(bf16[80,128]{1,0:T(8,128)(2,1)S(1)} %pad_dynamic-slice_fusion), channel_id=1, source_target_pairs={{0,2},{1,3},{2,4},{3,5},{4,6},{5,7},{6,0},{7,1},{8,10},{9,11},{10,... | collective-permute-start | bytes 61448 | tf_op jit(solution)/shard_map/ppermute | solution.py:264
  14.1 12.1 %collective-permute-start.1 = (bf16[80,128]{1,0:T(8,128)(2,1)S(1)}, bf16[80,128]{1,0:T(8,128)(2,1)S(1)}, u32[]{:S(2)}, u32[]{:S(2)}) collective-permute-start(bf16[80,128]{1,0:T(8,128)(2,1)S(1)} %pad_dynamic-slice_fusion), channel_id=1, source_target_pairs={{0,4},{1,5},{2,6},{3,7},{4,0},{5,1},{6,2},{7,3},{8,12},{9,13},{10,... | collective-permute-start | bytes 61448 | tf_op jit(solution)/shard_map/ppermute | solution.py:264
  17.0 9.2 %collective-permute-start.2 = (bf16[80,128]{1,0:T(8,128)(2,1)S(1)}, bf16[80,128]{1,0:T(8,128)(2,1)S(1)}, u32[]{:S(2)}, u32[]{:S(2)}) collective-permute-start(bf16[80,128]{1,0:T(8,128)(2,1)S(1)} %pad_dynamic-slice_fusion), channel_id=1, source_target_pairs={{0,6},{1,7},{2,0},{3,1},{4,2},{5,3},{6,4},{7,5},{8,14},{9,15},{10,... | collective-permute-start | bytes 61448 | tf_op jit(solution)/shard_map/ppermute | solution.py:264
  21.4 51.6 %collective-permute-start.12 = (bf16[16,128,256]{2,1,0:T(8,128)(2,1)}, bf16[16,128,256]{2,1,0:T(8,128)(2,1)}, u32[]{:S(2)}, u32[]{:S(2)}) collective-permute-start(bf16[16,128,256]{2,1,0:T(8,128)(2,1)} %bitcast.19), channel_id=1, source_target_pairs={{0,3},{1,2},{2,5},{3,4},{4,7},{5,6},{6,1},{7,0},{8,11},{9,10},{10,... | collective-permute-start | bytes 3145736 | tf_op jit(solution)/shard_map/ppermute | solution.py:264
  21.4 51.6 %collective-permute-start.13 = (bf16[16,128,256]{2,1,0:T(8,128)(2,1)}, bf16[16,128,256]{2,1,0:T(8,128)(2,1)}, u32[]{:S(2)}, u32[]{:S(2)}) collective-permute-start(bf16[16,128,256]{2,1,0:T(8,128)(2,1)} %bitcast.20), channel_id=1, source_target_pairs={{0,7},{1,6},{2,1},{3,0},{4,3},{5,2},{6,5},{7,4},{8,15},{9,14},{10,... | collective-permute-start | bytes 3145736 | tf_op jit(solution)/shard_map/ppermute | solution.py:264
  26.1 46.9 %collective-permute-start.10 = (bf16[16,128,256]{2,1,0:T(8,128)(2,1)}, bf16[16,128,256]{2,1,0:T(8,128)(2,1)}, u32[]{:S(2)}, u32[]{:S(2)}) collective-permute-start(bf16[16,128,256]{2,1,0:T(8,128)(2,1)} %bitcast.3), channel_id=1, source_target_pairs={{0,2},{1,3},{2,4},{3,5},{4,6},{5,7},{6,0},{7,1},{8,10},{9,11},{10,... | collective-permute-start | bytes 3145736 | tf_op jit(solution)/shard_map/ppermute | solution.py:264
  26.3 8.4 %collective-permute-start.3 = (bf16[336,128]{1,0:T(8,128)(2,1)S(1)}, bf16[336,128]{1,0:T(8,128)(2,1)S(1)}, u32[]{:S(2)}, u32[]{:S(2)}) collective-permute-start(bf16[336,128]{1,0:T(8,128)(2,1)S(1)} %pad_maximum_fusion.2), channel_id=1, source_target_pairs={{0,8},{1,9},{2,10},{3,11},{4,12},{5,13},{6,14},{7,15},{8,16},{9,17... | collective-permute-start | bytes 258056 | tf_op jit(solution)/shard_map/ppermute | solution.py:290
  29.5 8.5 %collective-permute-start.7 = (bf16[336,128]{1,0:T(8,128)(2,1)S(1)}, bf16[336,128]{1,0:T(8,128)(2,1)S(1)}, u32[]{:S(2)}, u32[]{:S(2)}) collective-permute-start(bf16[336,128]{1,0:T(8,128)(2,1)S(1)} %pad_maximum_fusion.2), channel_id=1, source_target_pairs={{0,56},{1,57},{2,58},{3,59},{4,60},{5,61},{6,62},{7,63},{8,0},{9,1... | collective-permute-start | bytes 258056 | tf_op jit(solution)/shard_map/ppermute | solution.py:293
  34.7 7.1 %collective-permute-start.4 = (bf16[336,128]{1,0:T(8,128)(2,1)S(1)}, bf16[336,128]{1,0:T(8,128)(2,1)S(1)}, u32[]{:S(2)}, u32[]{:S(2)}) collective-permute-start(bf16[336,128]{1,0:T(8,128)(2,1)S(1)} %collective-permute-done.3), channel_id=1, source_target_pairs={{0,8},{1,9},{2,10},{3,11},{4,12},{5,13},{6,14},{7,15},{8,16},{9,17... | collective-permute-start | bytes 258056 | tf_op jit(solution)/shard_map/ppermute | solution.py:290
  37.9 15.1 %collective-permute-start.8 = (bf16[336,128]{1,0:T(8,128)(2,1)S(1)}, bf16[336,128]{1,0:T(8,128)(2,1)S(1)}, u32[]{:S(2)}, u32[]{:S(2)}) collective-permute-start(bf16[336,128]{1,0:T(8,128)(2,1)S(1)} %collective-permute-done.7), channel_id=1, source_target_pairs={{0,56},{1,57},{2,58},{3,59},{4,60},{5,61},{6,62},{7,63},{8,0},{9,1... | collective-permute-start | bytes 258056 | tf_op jit(solution)/shard_map/ppermute | solution.py:293
  41.8 7.5 %collective-permute-start.5 = (bf16[336,128]{1,0:T(8,128)(2,1)S(1)}, bf16[336,128]{1,0:T(8,128)(2,1)S(1)}, u32[]{:S(2)}, u32[]{:S(2)}) collective-permute-start(bf16[336,128]{1,0:T(8,128)(2,1)S(1)} %collective-permute-done.4), channel_id=1, source_target_pairs={{0,8},{1,9},{2,10},{3,11},{4,12},{5,13},{6,14},{7,15},{8,16},{9,17... | collective-permute-start | bytes 258056 | tf_op jit(solution)/shard_map/ppermute | solution.py:290
  49.3 7.5 %collective-permute-start.6 = (bf16[336,128]{1,0:T(8,128)(2,1)S(1)}, bf16[336,128]{1,0:T(8,128)(2,1)S(1)}, u32[]{:S(2)}, u32[]{:S(2)}) collective-permute-start(bf16[336,128]{1,0:T(8,128)(2,1)S(1)} %collective-permute-done.5), channel_id=1, source_target_pairs={{0,8},{1,9},{2,10},{3,11},{4,12},{5,13},{6,14},{7,15},{8,16},{9,17... | collective-permute-start | bytes 258056 | tf_op jit(solution)/shard_map/ppermute | solution.py:290
  53.0 67.4 %collective-permute-start.11 = (bf16[16,128,256]{2,1,0:T(8,128)(2,1)}, bf16[16,128,256]{2,1,0:T(8,128)(2,1)}, u32[]{:S(2)}, u32[]{:S(2)}) collective-permute-start(bf16[16,128,256]{2,1,0:T(8,128)(2,1)} %bitcast.4), channel_id=1, source_target_pairs={{0,6},{1,7},{2,0},{3,1},{4,2},{5,3},{6,4},{7,5},{8,14},{9,15},{10,... | collective-permute-start | bytes 3145736 | tf_op jit(solution)/shard_map/ppermute | solution.py:264
  56.8 8.0 %collective-permute-start.9 = (bf16[336,128]{1,0:T(8,128)(2,1)S(1)}, bf16[336,128]{1,0:T(8,128)(2,1)S(1)}, u32[]{:S(2)}, u32[]{:S(2)}) collective-permute-start(bf16[336,128]{1,0:T(8,128)(2,1)S(1)} %collective-permute-done.8), channel_id=1, source_target_pairs={{0,56},{1,57},{2,58},{3,59},{4,60},{5,61},{6,62},{7,63},{8,0},{9,1... | collective-permute-start | bytes 258056 | tf_op jit(solution)/shard_map/ppermute | solution.py:293
  64.8 4.4 %collective-permute-start.21 = (bf16[32,128,256]{2,1,0:T(8,128)(2,1)}, bf16[32,128,256]{2,1,0:T(8,128)(2,1)S(1)}, u32[]{:S(2)}, u32[]{:S(2)}) collective-permute-start(bf16[32,128,256]{2,1,0:T(8,128)(2,1)} %pad_maximum_fusion), channel_id=1, source_target_pairs={{0,1},{1,0},{2,3},{3,2},{4,5},{5,4},{6,7},{7,6},{8,9},{9,8},{10,11... | collective-permute-start | bytes 6291464 | tf_op jit(solution)/shard_map/ppermute | solution.py:264
  69.1 74.4 %copy-start.3 = (bf16[32,128,256]{2,1,0:T(8,128)(2,1)}, bf16[32,128,256]{2,1,0:T(8,128)(2,1)S(1)}, u32[]{:S(2)}) copy-start(bf16[32,128,256]{2,1,0:T(8,128)(2,1)S(1)} %collective-permute-done.21.refs_1_) | copy-start | bytes 6291460
  70.9 100.3 %collective-permute-start.27 = (bf16[32,128,256]{2,1,0:T(8,128)(2,1)}, bf16[32,128,256]{2,1,0:T(8,128)(2,1)}, u32[]{:S(2)}, u32[]{:S(2)}) collective-permute-start(bf16[32,128,256]{2,1,0:T(8,128)(2,1)} %pad_maximum_fusion.1), channel_id=1, source_target_pairs={{0,4},{1,5},{2,6},{3,7},{4,0},{5,1},{6,2},{7,3},{8,12},{9,13},{10,... | collective-permute-start | bytes 6291464 | tf_op jit(solution)/shard_map/ppermute | solution.py:264
  120.4 10.9 %collective-permute-start.14 = (bf16[32,80,128]{2,1,0:T(8,128)(2,1)}, bf16[32,80,128]{2,1,0:T(8,128)(2,1)}, u32[]{:S(2)}, u32[]{:S(2)}) collective-permute-start(bf16[32,80,128]{2,1,0:T(8,128)(2,1)} %bitcast.18), channel_id=1, source_target_pairs={{0,64},{64,128},{128,192},{192,0},{1,65},{65,129},{129,193},{193,1... | collective-permute-start | bytes 1966088 | tf_op jit(solution)/shard_map/ppermute | solution.py:299
  121.7 13.5 %collective-permute-start.15 = (bf16[32,80,128]{2,1,0:T(8,128)(2,1)}, bf16[32,80,128]{2,1,0:T(8,128)(2,1)}, u32[]{:S(2)}, u32[]{:S(2)}) collective-permute-start(bf16[32,80,128]{2,1,0:T(8,128)(2,1)} %bitcast.18), channel_id=1, source_target_pairs={{0,128},{64,192},{128,0},{192,64},{1,129},{65,193},{129,1},{193,65... | collective-permute-start | bytes 1966088 | tf_op jit(solution)/shard_map/ppermute | solution.py:299
  124.5 16.6 %collective-permute-start.16 = (bf16[32,80,128]{2,1,0:T(8,128)(2,1)}, bf16[32,80,128]{2,1,0:T(8,128)(2,1)}, u32[]{:S(2)}, u32[]{:S(2)}) collective-permute-start(bf16[32,80,128]{2,1,0:T(8,128)(2,1)} %bitcast.18), channel_id=1, source_target_pairs={{0,192},{64,0},{128,64},{192,128},{1,193},{65,1},{129,65},{193,129... | collective-permute-start | bytes 1966088 | tf_op jit(solution)/shard_map/ppermute | solution.py:299
  125.9 18.8 %collective-permute-start.17 = (bf16[32,80,128]{2,1,0:T(8,128)(2,1)}, bf16[32,80,128]{2,1,0:T(8,128)(2,1)}, u32[]{:S(2)}, u32[]{:S(2)}) collective-permute-start(bf16[32,80,128]{2,1,0:T(8,128)(2,1)} %bitcast.18), channel_id=1, source_target_pairs={{0,1},{1,0},{2,3},{3,2},{4,5},{5,4},{6,7},{7,6},{8,9},{9,8},{10,11... | collective-permute-start | bytes 1966088 | tf_op jit(solution)/shard_map/ppermute | solution.py:264
  131.3 14.6 %collective-permute-start.18 = (bf16[32,80,128]{2,1,0:T(8,128)(2,1)}, bf16[32,80,128]{2,1,0:T(8,128)(2,1)S(1)}, u32[]{:S(2)}, u32[]{:S(2)}) collective-permute-start(bf16[32,80,128]{2,1,0:T(8,128)(2,1)} %collective-permute-done.14), channel_id=1, source_target_pairs={{0,1},{1,0},{2,3},{3,2},{4,5},{5,4},{6,7},{7,6},{8,9},{9,8},{10,11... | collective-permute-start | bytes 1966088 | tf_op jit(solution)/shard_map/ppermute | solution.py:264
  135.2 13.4 %copy-start.2 = (bf16[16,128,256]{2,1,0:T(8,128)(2,1)S(1)}, bf16[16,128,256]{2,1,0:T(8,128)(2,1)}, u32[]{:S(2)}) copy-start(bf16[16,128,256]{2,1,0:T(8,128)(2,1)} %grad_ref.1) | copy-start | bytes 3145732
  135.2 10.8 %collective-permute-start.19 = (bf16[32,80,128]{2,1,0:T(8,128)(2,1)}, bf16[32,80,128]{2,1,0:T(8,128)(2,1)S(1)}, u32[]{:S(2)}, u32[]{:S(2)}) collective-permute-start(bf16[32,80,128]{2,1,0:T(8,128)(2,1)} %collective-permute-done.15), channel_id=1, source_target_pairs={{0,1},{1,0},{2,3},{3,2},{4,5},{5,4},{6,7},{7,6},{8,9},{9,8},{10,11... | collective-permute-start | bytes 1966088 | tf_op jit(solution)/shard_map/ppermute | solution.py:264
  141.2 4.9 %collective-permute-start.20 = (bf16[32,80,128]{2,1,0:T(8,128)(2,1)}, bf16[32,80,128]{2,1,0:T(8,128)(2,1)S(1)}, u32[]{:S(2)}, u32[]{:S(2)}) collective-permute-start(bf16[32,80,128]{2,1,0:T(8,128)(2,1)} %collective-permute-done.16), channel_id=1, source_target_pairs={{0,1},{1,0},{2,3},{3,2},{4,5},{5,4},{6,7},{7,6},{8,9},{9,8},{10,11... | collective-permute-start | bytes 1966088 | tf_op jit(solution)/shard_map/ppermute | solution.py:264
  146.2 2.3 %copy-start = (bf16[256,80,128]{2,1,0:T(8,128)(2,1)}, bf16[256,80,128]{2,1,0:T(8,128)(2,1)S(1)}, u32[]{:S(2)}) copy-start(bf16[256,80,128]{2,1,0:T(8,128)(2,1)S(1)} %constant_dynamic-update-slice_fusion.weight_ref) | copy-start | bytes 15728644
  148.6 2.5 %copy-start.1 = (bf16[256,80,128]{2,1,0:T(8,128)(2,1)S(1)}, bf16[256,80,128]{2,1,0:T(8,128)(2,1)}, u32[]{:S(2)}) copy-start(bf16[256,80,128]{2,1,0:T(8,128)(2,1)} %copy-done) | copy-start | bytes 15728644
  165.1 10.2 %collective-permute-start.22 = (bf16[4,96,96]{2,1,0:T(8,128)(2,1)}, bf16[4,96,96]{2,1,0:T(8,128)(2,1)S(1)}, u32[]{:S(2)}, u32[]{:S(2)}) collective-permute-start(bf16[4,96,96]{2,1,0:T(8,128)(2,1)} %get-tuple-element.37), channel_id=1, source_target_pairs={{0,1},{1,0},{2,3},{3,2},{4,5},{5,4},{6,7},{7,6},{8,9},{9,8},{10,11... | collective-permute-start | bytes 221192 | tf_op jit(solution)/shard_map/ppermute | solution.py:264
  165.2 11.0 %collective-permute-start.23 = (bf16[4,96,96]{2,1,0:T(8,128)(2,1)}, bf16[4,96,96]{2,1,0:T(8,128)(2,1)S(1)}, u32[]{:S(2)}, u32[]{:S(2)}) collective-permute-start(bf16[4,96,96]{2,1,0:T(8,128)(2,1)} %get-tuple-element.38), channel_id=1, source_target_pairs={{0,6},{1,7},{2,0},{3,1},{4,2},{5,3},{6,4},{7,5},{8,14},{9,15},{10,... | collective-permute-start | bytes 221192 | tf_op jit(solution)/shard_map/ppermute | solution.py:264
  168.6 10.4 %collective-permute-start.24 = (bf16[4,96,96]{2,1,0:T(8,128)(2,1)}, bf16[4,96,96]{2,1,0:T(8,128)(2,1)S(1)}, u32[]{:S(2)}, u32[]{:S(2)}) collective-permute-start(bf16[4,96,96]{2,1,0:T(8,128)(2,1)} %get-tuple-element.39), channel_id=1, source_target_pairs={{0,2},{1,3},{2,4},{3,5},{4,6},{5,7},{6,0},{7,1},{8,10},{9,11},{10,... | collective-permute-start | bytes 221192 | tf_op jit(solution)/shard_map/ppermute | solution.py:264
  168.6 10.4 %collective-permute-start.25 = (bf16[4,96,96]{2,1,0:T(8,128)(2,1)}, bf16[4,96,96]{2,1,0:T(8,128)(2,1)S(1)}, u32[]{:S(2)}, u32[]{:S(2)}) collective-permute-start(bf16[4,96,96]{2,1,0:T(8,128)(2,1)} %get-tuple-element.40), channel_id=1, source_target_pairs={{0,7},{1,6},{2,1},{3,0},{4,3},{5,2},{6,5},{7,4},{8,15},{9,14},{10,... | collective-permute-start | bytes 221192 | tf_op jit(solution)/shard_map/ppermute | solution.py:264
  171.2 13.2 %copy-start.4 = (bf16[4,96,96]{2,1,0:T(8,128)(2,1)S(1)}, bf16[4,96,96]{2,1,0:T(8,128)(2,1)}, u32[]{:S(2)}) copy-start(bf16[4,96,96]{2,1,0:T(8,128)(2,1)} %get-tuple-element.36) | copy-start | bytes 221188
  171.2 7.8 %collective-permute-start.26 = (bf16[4,96,96]{2,1,0:T(8,128)(2,1)}, bf16[4,96,96]{2,1,0:T(8,128)(2,1)S(1)}, u32[]{:S(2)}, u32[]{:S(2)}) collective-permute-start(bf16[4,96,96]{2,1,0:T(8,128)(2,1)} %get-tuple-element.41), channel_id=1, source_target_pairs={{0,3},{1,2},{2,5},{3,4},{4,7},{5,6},{6,1},{7,0},{8,11},{9,10},{10,... | collective-permute-start | bytes 221192 | tf_op jit(solution)/shard_map/ppermute | solution.py:264
  175.3 7.5 %collective-permute-start.28 = (bf16[4,96,96]{2,1,0:T(8,128)(2,1)}, bf16[4,96,96]{2,1,0:T(8,128)(2,1)S(1)}, u32[]{:S(2)}, u32[]{:S(2)}) collective-permute-start(bf16[4,96,96]{2,1,0:T(8,128)(2,1)} %get-tuple-element.42), channel_id=1, source_target_pairs={{0,4},{1,5},{2,6},{3,7},{4,0},{5,1},{6,2},{7,3},{8,12},{9,13},{10,... | collective-permute-start | bytes 221192 | tf_op jit(solution)/shard_map/ppermute | solution.py:264
  176.2 8.2 %collective-permute-start.29 = (bf16[4,96,96]{2,1,0:T(8,128)(2,1)}, bf16[4,96,96]{2,1,0:T(8,128)(2,1)S(1)}, u32[]{:S(2)}, u32[]{:S(2)}) collective-permute-start(bf16[4,96,96]{2,1,0:T(8,128)(2,1)} %get-tuple-element.43), channel_id=1, source_target_pairs={{0,5},{1,4},{2,7},{3,6},{4,1},{5,0},{6,3},{7,2},{8,13},{9,12},{10,... | collective-permute-start | bytes 221192 | tf_op jit(solution)/shard_map/ppermute | solution.py:264
  184.5 5.9 %collective-permute-start.30 = (bf16[4,96,96]{2,1,0:T(8,128)(2,1)S(1)}, bf16[4,96,96]{2,1,0:T(8,128)(2,1)S(1)}, u32[]{:S(2)}, u32[]{:S(2)}) collective-permute-start(bf16[4,96,96]{2,1,0:T(8,128)(2,1)S(1)} %add_convert_fusion), channel_id=1, source_target_pairs={{0,64},{64,128},{128,192},{192,0},{1,65},{65,129},{129,193},{193,1... | collective-permute-start | bytes 221192 | tf_op jit(solution)/shard_map/ppermute | solution.py:339
  187.0 6.8 %collective-permute-start.31 = (bf16[4,96,96]{2,1,0:T(8,128)(2,1)S(1)}, bf16[4,96,96]{2,1,0:T(8,128)(2,1)S(1)}, u32[]{:S(2)}, u32[]{:S(2)}) collective-permute-start(bf16[4,96,96]{2,1,0:T(8,128)(2,1)S(1)} %add_convert_fusion), channel_id=1, source_target_pairs={{0,128},{64,192},{128,0},{192,64},{1,129},{65,193},{129,1},{193,65... | collective-permute-start | bytes 221192 | tf_op jit(solution)/shard_map/ppermute | solution.py:339
  189.0 6.4 %collective-permute-start.32 = (bf16[4,96,96]{2,1,0:T(8,128)(2,1)S(1)}, bf16[4,96,96]{2,1,0:T(8,128)(2,1)S(1)}, u32[]{:S(2)}, u32[]{:S(2)}) collective-permute-start(bf16[4,96,96]{2,1,0:T(8,128)(2,1)S(1)} %add_convert_fusion), channel_id=1, source_target_pairs={{0,192},{64,0},{128,64},{192,128},{1,193},{65,1},{129,65},{193,129... | collective-permute-start | bytes 221192 | tf_op jit(solution)/shard_map/ppermute | solution.py:339
Sparse Core Ops, SparseCore 0:
  9.8 100.8 all-gather.1

commit v4 on v2

--- a/solution.py
+++ b/solution.py
@@ -298,7 +298,6 @@
     )
     quarters += [lax.ppermute(quarter, "ep", ep_perm(0, 0, 1)) for quarter in quarters]
     held = jnp.concatenate(quarters, 0)
-    held, chunks[6] = lax.optimization_barrier((held, chunks[6]))
     held = held.reshape(NC * NX * NY * NZ, PIECE, CHANNELS)
 
     from_z = (z - jnp.arange(NZ, dtype=jnp.int32)) % NZ
@@ -322,21 +321,19 @@
     block = ((y - at_y) % NY) * NZ + (z - at_z) % NZ
     quarter = (x - jnp.arange(NX, dtype=jnp.int32)) % NX
     place = ((at_c ^ c)[:, None] * NX + quarter[None]) * (NZ * NY) + block[:, None]
-    parts = list(weight_grads(*early, grads, chunks[:7]))
-    parts[0], place = lax.optimization_barrier((parts[0], place))
     in_grad = input_grads(
         place.reshape(-1), gates.reshape(-1).astype(jnp.float32), out_grad, held
     )
-
-    def returned(part, d, dc):
+    in_grad, plan = lax.optimization_barrier((in_grad, early[0]))
+    parts = weight_grads(plan, early[1], grads, chunks[:7])
+    parts += weight_grads(*late, grads, chunks[7:])
+
+    total = None
+    for part, (d, dc) in zip(parts, offsets):
         if d or dc:
             part = lax.ppermute(part, "ep", ep_perm(0, -d, dc))
-        return part.astype(jnp.float32)
-
-    total = sum(returned(part, *offset) for part, offset in zip(parts, offsets))
-    in_grad, total, plan = lax.optimization_barrier((in_grad, total, late[0]))
-    (last,) = weight_grads(plan, late[1], grads, chunks[7:])
-    total = total + returned(last, *offsets[7])
+        part = part.astype(jnp.float32)
+        total = part if total is None else total + part
     total = total.astype(jnp.bfloat16)
     summed = total.astype(jnp.float32)
     for d in range(1, NX):

time: 176 us -> 173 us (0.983)
  other arithmetic: 10.6 us -> 7.88 us
    ppermute x7, waiting for transfers between devices: 11.3 us -> 4.94 us  [per_device(): part = lax.ppermute(part, 'ep', ep_perm(0, -d, dc))]
    ppermute x7, waiting for transfers between devices: 15.5 us -> 21.5 us  [per_device(): lax.ppermute(part, 'ep', ep_perm(0, d, dc))]
    ppermute x3, waiting for transfers between devices: 6.1 us -> 9.59 us  [per_device(): lax.ppermute(held, 'rep', rep_perm(d))]
    ppermute x3, waiting for transfers between devices: 2.8 us -> 0.01 us  [per_device(): lax.ppermute(held, 'ep', ep_perm(0, d, 0))]
    ppermute x7, starting transfers between devices: 13.5 us -> 10.8 us  [per_device(): part = lax.ppermute(part, 'ep', ep_perm(0, -d, dc))]
    unnamed x50 -> x36, local copies, waits for them, and re-layouts: 11.2 us -> 10 us
  transfers between devices with their start and end apart: 35 -> 35, of which waited for: 12 -> 12; matrix products, arithmetic and copies ran while one was open for 18% -> 17% of each run, Pallas kernels for 8% -> 10%
where the time goes in v4:
time: 173 us; the launch traced here: 172 us
  starting transfers between devices  51.3 us (30%)
  waiting for transfers between devices  50 us (29%)
  local copies, waits for them, and re-layouts  27.7 us (16%)
  between operations  17.7 us (10%)
  Pallas kernels  17.3 us (10%)
  other arithmetic  7.88 us (5%)
    ppermute x7, waiting for transfers between devices, per_device(): lax.ppermute(part, 'ep', ep_perm(0, d, dc))  21.5 us
    ppermute x7, starting transfers between devices, per_device(): lax.ppermute(part, 'ep', ep_perm(0, d, dc))  12 us
    pallas_call x2, Pallas kernels, weight_grads(): pl.pallas_call(functools.partial(weight_kernel, chunks), out_shape=[jax.S...  11.2 us
    ppermute x7, starting transfers between devices, per_device(): part = lax.ppermute(part, 'ep', ep_perm(0, -d, dc))  10.8 us
    unnamed x36, local copies, waits for them, and re-layouts  10 us
    ppermute x3, waiting for transfers between devices, per_device(): lax.ppermute(held, 'rep', rep_perm(d))  9.59 us
    ppermute x3, starting transfers between devices, per_device(): down = lax.ppermute(down, 'ep', ep_perm(-1, 0, 0))  9.5 us
    ppermute x4, waiting for transfers between devices, per_device(): up = lax.ppermute(up, 'ep', ep_perm(1, 0, 0))  8.81 us
  transfers between devices with their start and end apart: 35, of which 12 were waited for; matrix products, arithmetic and copies ran while one was open for 17% of the time, Pallas kernels for 10%

profile of v4, /device:TPU:1, one launch (start us, length us, event | category | flops | bytes accessed | tf_op | source)
XLA Modules:
  0.0 171.8 jit_solution(10323703144671942662)
XLA Ops:
  7.2 0.7 all-gather.2.cloned.1.call-update
  8.0 3.1 %constant_dynamic-slice_fusion.6 = (bf16[8,1,1,2,128,256]{5,4,3,2,1,0:T(8,128)(2,1)}, bf16[8,1,1,2,128,256]{5,4,3,2,1,0:T(8,128)(2,1)}) fusion(bf16[8,4,2,2,128,256]{5,4,3,2,1,0:T(8,128)(2,1)} %bitcast.58, s32[]{:T(128)S(6)} %select_n.250, s32[]{:T(128)S(6)} %select_n.248, s32[]{:T(128)S(6)} %select_n.247), kind=kLoop, calls=%fused_computation.72 | loop fusion | bytes 4194316 | tf_op jit(solution)/shard_map/dynamic_slice | solution.py:256
  12.0 2.5 %collective-permute-start = (bf16[96,128]{1,0:T(8,128)(2,1)S(1)}, bf16[96,128]{1,0:T(8,128)(2,1)S(1)}, u32[]{:S(2)}, u32[]{:S(2)}) collective-permute-start(bf16[96,128]{1,0:T(8,128)(2,1)S(1)} %pad_maximum_fusion.1), channel_id=1, source_target_pairs={{0,8},{1,9},{2,10},{3,11},{4,12},{5,13},{6,14},{7,15},{8,16},{9,17... | collective-permute-start | bytes 73736 | tf_op jit(solution)/shard_map/ppermute | solution.py:279
  14.6 4.0 %collective-permute-start.4 = (bf16[96,128]{1,0:T(8,128)(2,1)S(1)}, bf16[96,128]{1,0:T(8,128)(2,1)S(1)}, u32[]{:S(2)}, u32[]{:S(2)}) collective-permute-start(bf16[96,128]{1,0:T(8,128)(2,1)S(1)} %pad_maximum_fusion.1), channel_id=1, source_target_pairs={{0,56},{1,57},{2,58},{3,59},{4,60},{5,61},{6,62},{7,63},{8,0},{9,1... | collective-permute-start | bytes 73736 | tf_op jit(solution)/shard_map/ppermute | solution.py:282
  18.6 1.3 collective-permute-start.10
  19.9 1.4 collective-permute-start.11
  21.8 5.6 %constant_dynamic-slice_fusion = (bf16[8,1,1,2,128,256]{5,4,3,0,2,1:T(8,128)(2,1)}, bf16[8,1,1,2,128,256]{5,4,3,0,2,1:T(8,128)(2,1)}, bf16[8,1,1,2,128,256]{5,4,...) fusion(s32[]{:T(128)S(6)} %select_n.253, ...), kind=kLoop, calls=%fused_computation.66 | loop fusion | bytes 12582936 | tf_op jit(solution)/shard_map/dynamic_slice | solution.py:256
  28.3 2.7 %collective-permute-start.5 = (bf16[96,128]{1,0:T(8,128)(2,1)S(1)}, bf16[96,128]{1,0:T(8,128)(2,1)S(1)}, u32[]{:S(2)}, u32[]{:S(2)}) collective-permute-start(bf16[96,128]{1,0:T(8,128)(2,1)S(1)} %collective-permute-done.4), channel_id=1, source_target_pairs={{0,56},{1,57},{2,58},{3,59},{4,60},{5,61},{6,62},{7,63},{8,0},{9,1... | collective-permute-start | bytes 73736 | tf_op jit(solution)/shard_map/ppermute | solution.py:282
  31.0 2.0 %collective-permute-done.1 = bf16[96,128]{1,0:T(8,128)(2,1)S(1)} collective-permute-done((bf16[96,128]{1,0:T(8,128)(2,1)S(1)}, bf16[96,128]{1,0:T(8,128)(2,1)S(1)}, u32[]{:S(2)}, u32[]{:S(2)}) %collective-permute-start.1) | collective-permute-done | bytes 24608 | tf_op jit(solution)/shard_map/ppermute | solution.py:279
  33.0 2.7 %collective-permute-start.6 = (bf16[96,128]{1,0:T(8,128)(2,1)S(1)}, bf16[96,128]{1,0:T(8,128)(2,1)S(1)}, u32[]{:S(2)}, u32[]{:S(2)}) collective-permute-start(bf16[96,128]{1,0:T(8,128)(2,1)S(1)} %collective-permute-done.5), channel_id=1, source_target_pairs={{0,56},{1,57},{2,58},{3,59},{4,60},{5,61},{6,62},{7,63},{8,0},{9,1... | collective-permute-start | bytes 73736 | tf_op jit(solution)/shard_map/ppermute | solution.py:282
  35.8 2.0 %collective-permute-done.2 = bf16[96,128]{1,0:T(8,128)(2,1)S(1)} collective-permute-done((bf16[96,128]{1,0:T(8,128)(2,1)S(1)}, bf16[96,128]{1,0:T(8,128)(2,1)S(1)}, u32[]{:S(2)}, u32[]{:S(2)}) %collective-permute-start.2) | collective-permute-done | bytes 24608 | tf_op jit(solution)/shard_map/ppermute | solution.py:279
  37.8 4.8 %collective-permute-done.3 = bf16[96,128]{1,0:T(8,128)(2,1)S(1)} collective-permute-done((bf16[96,128]{1,0:T(8,128)(2,1)S(1)}, bf16[96,128]{1,0:T(8,128)(2,1)S(1)}, u32[]{:S(2)}, u32[]{:S(2)}) %collective-permute-start.3) | collective-permute-done | bytes 24608 | tf_op jit(solution)/shard_map/ppermute | solution.py:279
  42.8 2.6 %collective-permute-start.8 = (bf16[8,80,128]{2,1,0:T(8,128)(2,1)S(1)}, bf16[8,80,128]{2,1,0:T(8,128)(2,1)S(1)}, u32[]{:S(2)}, u32[]{:S(2)}) collective-permute-start(bf16[8,80,128]{2,1,0:T(8,128)(2,1)S(1)} %slice.48), channel_id=1, source_target_pairs={{0,4},{1,5},{2,6},{3,7},{4,0},{5,1},{6,2},{7,3},{8,12},{9,13},{10,... | collective-permute-start | bytes 491528 | tf_op jit(solution)/shard_map/ppermute | solution.py:292
  45.6 0.4 convert_reduce_fusion
  46.0 0.4 select_reduce_fusion.1
  47.0 4.8 %collective-permute-start.14 = (bf16[16,128,256]{2,1,0:T(8,128)(2,1)}, bf16[16,128,256]{2,1,0:T(8,128)(2,1)}, u32[]{:S(2)}, u32[]{:S(2)}) collective-permute-start(bf16[16,128,256]{2,1,0:T(8,128)(2,1)} %bitcast.14), channel_id=1, source_target_pairs={{0,3},{1,2},{2,5},{3,4},{4,7},{5,6},{6,1},{7,0},{8,11},{9,10},{10,... | collective-permute-start | bytes 3145736 | tf_op jit(solution)/shard_map/ppermute | solution.py:290
  51.9 1.2 convert_reduce_fusion.5
  53.5 2.4 %collective-permute-start.9 = (bf16[8,80,128]{2,1,0:T(8,128)(2,1)S(1)}, bf16[8,80,128]{2,1,0:T(8,128)(2,1)S(1)}, u32[]{:S(2)}, u32[]{:S(2)}) collective-permute-start(bf16[8,80,128]{2,1,0:T(8,128)(2,1)S(1)} %slice.48), channel_id=1, source_target_pairs={{0,6},{1,7},{2,0},{3,1},{4,2},{5,3},{6,4},{7,5},{8,14},{9,15},{10,... | collective-permute-start | bytes 491528 | tf_op jit(solution)/shard_map/ppermute | solution.py:292
  55.9 0.6 slice.41
  58.8 0.5 slice.53
  60.1 0.7 copy.118
  61.4 1.3 collective-permute-start.12
  62.8 0.5 fusion.16
  63.3 2.5 %collective-permute-start.13 = (bf16[32,80,128]{2,1,0:T(8,128)(2,1)S(1)}, bf16[32,80,128]{2,1,0:T(8,128)(2,1)}, u32[]{:S(2)}, u32[]{:S(2)}) collective-permute-start(bf16[32,80,128]{2,1,0:T(8,128)(2,1)S(1)} %bitcast.63), channel_id=1, source_target_pairs={{0,128},{64,192},{128,0},{192,64},{1,129},{65,193},{129,1},{193,65... | collective-permute-start | bytes 1966088 | tf_op jit(solution)/shard_map/ppermute | solution.py:295
  66.0 0.7 copy.123
  66.8 0.8 copy.120
  67.6 0.7 copy.122
  68.4 0.8 copy.121
  69.2 1.2 collective-permute-start.16
  70.4 5.6 %collective-permute-done.14.refs_4_ = bf16[16,128,256]{2,1,0:T(8,128)(2,1)} collective-permute-done((bf16[16,128,256]{2,1,0:T(8,128)(2,1)}, bf16[16,128,256]{2,1,0:T(8,128)(2,1)}, u32[]{:S(2)}, u32[]{:S(2)}) %collective-permute-start.14) | collective-permute-done | bytes 1048608 | tf_op jit(solution)/shard_map/ppermute | solution.py:290
  76.0 1.4 collective-permute-start.17
  77.4 1.3 collective-permute-done.12
  78.7 1.1 collective-permute-start.18
  80.1 0.7 select_reduce_fusion.6.gate_of
  80.8 1.4 select_reduce_fusion.2.gate_of
  82.2 3.2 %collective-permute-done.15.refs_5_ = bf16[16,128,256]{2,1,0:T(8,128)(2,1)} collective-permute-done((bf16[16,128,256]{2,1,0:T(8,128)(2,1)}, bf16[16,128,256]{2,1,0:T(8,128)(2,1)}, u32[]{:S(2)}, u32[]{:S(2)}) %collective-permute-start.15) | collective-permute-done | bytes 1048608 | tf_op jit(solution)/shard_map/ppermute | solution.py:290
  85.4 8.3 %collective-permute-done.13 = bf16[32,80,128]{2,1,0:T(8,128)(2,1)} collective-permute-done((bf16[32,80,128]{2,1,0:T(8,128)(2,1)S(1)}, bf16[32,80,128]{2,1,0:T(8,128)(2,1)}, u32[]{:S(2)}, u32[]{:S(2)}) %collective-permute-start.13) | collective-permute-done | bytes 655392 | tf_op jit(solution)/shard_map/ppermute | solution.py:295
  93.7 0.4 collective-permute-start.22
  94.1 0.7 pad_add_fusion.2.plan
  94.8 4.0 %collective-permute-start.29 = (bf16[16,128,256]{2,1,0:T(8,128)(2,1)}, bf16[16,128,256]{2,1,0:T(8,128)(2,1)}, u32[]{:S(2)}, u32[]{:S(2)}) collective-permute-start(bf16[16,128,256]{2,1,0:T(8,128)(2,1)} %bitcast.67), channel_id=1, source_target_pairs={{0,5},{1,4},{2,7},{3,6},{4,1},{5,0},{6,3},{7,2},{8,13},{9,12},{10,... | collective-permute-start | bytes 3145736 | tf_op jit(solution)/shard_map/ppermute | solution.py:290
  98.9 0.6 collective-permute-start.20
  99.6 1.2 constant_dynamic-update-slice_fusion.13
  100.7 1.2 constant_dynamic-update-slice_fusion.12
  101.9 1.2 constant_dynamic-update-slice_fusion.11
  103.1 1.2 constant_dynamic-update-slice_fusion.10
  104.5 2.4 %copy-done = bf16[256,80,128]{2,1,0:T(8,128)(2,1)} copy-done((bf16[256,80,128]{2,1,0:T(8,128)(2,1)}, bf16[256,80,128]{2,1,0:T(8,128)(2,1)S(1)}, u32[]{:S(2)}) %copy-start) | copy-done | bytes 5242904
  107.0 2.5 %copy-done.1 = bf16[256,80,128]{2,1,0:T(8,128)(2,1)S(1)} copy-done((bf16[256,80,128]{2,1,0:T(8,128)(2,1)S(1)}, bf16[256,80,128]{2,1,0:T(8,128)(2,1)}, u32[]{:S(2)}) %copy-start.1) | copy-done | bytes 5242904
  109.4 6.1 %shard_map.68 = bf16[16,128,256]{2,1,0:T(8,128)(2,1)} custom-call(s32[128]{0:T(128)S(1)} %add.346.place_ref, f32[32]{0:T(128)S(1)} %reshape.729.gate_ref, bf16[16,128,256]{2,1,0:T(8,128)(2,1)S(1)} %copy-done.2, bf16[256,80,128]{2,1,0:T(8,128)(2,1)S(1)} %copy-done.1), custom_call_target="tpu_custom_call" | custom-call | flops 1 | bytes 1 | tf_op jit(solution)/shard_map/pallas_call | solution.py:76
  115.6 3.4 %collective-permute-done.22.refs_6_ = bf16[16,128,256]{2,1,0:T(8,128)(2,1)} collective-permute-done((bf16[16,128,256]{2,1,0:T(8,128)(2,1)}, bf16[16,128,256]{2,1,0:T(8,128)(2,1)}, u32[]{:S(2)}, u32[]{:S(2)}) %collective-permute-start.22) | collective-permute-done | bytes 1048608 | tf_op jit(solution)/shard_map/ppermute | solution.py:290
  119.0 7.9 %shard_map.69 = (bf16[4,96,96]{2,1,0:T(8,128)(2,1)}, bf16[4,96,96]{2,1,0:T(8,128)(2,1)}, bf16[4,96,96]{2,1,0:T(8,128)(2,1)}, bf16[4,96,96]{2,1,0:T(8,128)(2,1)},...) custom-call(s32[291]{0:T(512)} %pad_add_fusion.2.plan, ...), custom_call_target="tpu_custom_call" | custom-call | flops 1 | bytes 1 | tf_op jit(solution)/shard_map/pallas_call | solution.py:221
  126.9 3.9 %collective-permute-start.23 = (bf16[4,96,96]{2,1,0:T(8,128)(2,1)}, bf16[4,96,96]{2,1,0:T(8,128)(2,1)S(1)}, u32[]{:S(2)}, u32[]{:S(2)}) collective-permute-start(bf16[4,96,96]{2,1,0:T(8,128)(2,1)} %get-tuple-element.51), channel_id=1, source_target_pairs={{0,1},{1,0},{2,3},{3,2},{4,5},{5,4},{6,7},{7,6},{8,9},{9,8},{10,11... | collective-permute-start | bytes 221192 | tf_op jit(solution)/shard_map/ppermute | solution.py:334
  130.9 0.7 pad_add_fusion.3.plan
  131.5 1.5 collective-permute-start.25
  133.0 1.7 %collective-permute-start.26 = (bf16[4,96,96]{2,1,0:T(8,128)(2,1)}, bf16[4,96,96]{2,1,0:T(8,128)(2,1)S(1)}, u32[]{:S(2)}, u32[]{:S(2)}) collective-permute-start(bf16[4,96,96]{2,1,0:T(8,128)(2,1)} %get-tuple-element.54), channel_id=1, source_target_pairs={{0,7},{1,6},{2,1},{3,0},{4,3},{5,2},{6,5},{7,4},{8,15},{9,14},{10,... | collective-permute-start | bytes 221192 | tf_op jit(solution)/shard_map/ppermute | solution.py:334
  134.7 9.3 %collective-permute-done.29.refs_0_ = bf16[16,128,256]{2,1,0:T(8,128)(2,1)} collective-permute-done((bf16[16,128,256]{2,1,0:T(8,128)(2,1)}, bf16[16,128,256]{2,1,0:T(8,128)(2,1)}, u32[]{:S(2)}, u32[]{:S(2)}) %collective-permute-start.29) | collective-permute-done | bytes 1048608 | tf_op jit(solution)/shard_map/ppermute | solution.py:290
  144.0 3.3 %shard_map.70 = bf16[4,96,96]{2,1,0:T(8,128)(2,1)} custom-call(s32[51]{0:T(128)} %pad_add_fusion.3.plan, f32[20]{0:T(128)} %select_reduce_fusion.6.gate_of, bf16[128,128,256]{2,1,0:T(8,128)(2,1)} %all-gather.2.cloned.1.call-done.grads, bf16[16,128,256]{2,1,0:T(8,128)(2,1)} %collective-permute-done.29.refs_0_), custom_call_target="tpu_custom_call" | custom-call | flops 1 | bytes 1 | tf_op jit(solution)/shard_map/pallas_call | solution.py:221
  147.4 1.9 %collective-permute-start.28 = (bf16[4,96,96]{2,1,0:T(8,128)(2,1)S(1)}, bf16[4,96,96]{2,1,0:T(8,128)(2,1)S(1)}, u32[]{:S(2)}, u32[]{:S(2)}) collective-permute-start(bf16[4,96,96]{2,1,0:T(8,128)(2,1)S(1)} %copy-done.9), channel_id=1, source_target_pairs={{0,4},{1,5},{2,6},{3,7},{4,0},{5,1},{6,2},{7,3},{8,12},{9,13},{10,... | collective-permute-start | bytes 221192 | tf_op jit(solution)/shard_map/ppermute | solution.py:334
  149.3 1.8 %collective-permute-start.30 = (bf16[4,96,96]{2,1,0:T(8,128)(2,1)}, bf16[4,96,96]{2,1,0:T(8,128)(2,1)S(1)}, u32[]{:S(2)}, u32[]{:S(2)}) collective-permute-start(bf16[4,96,96]{2,1,0:T(8,128)(2,1)} %shard_map.70), channel_id=1, source_target_pairs={{0,5},{1,4},{2,7},{3,6},{4,1},{5,0},{6,3},{7,2},{8,13},{9,12},{10,... | collective-permute-start | bytes 221192 | tf_op jit(solution)/shard_map/ppermute | solution.py:334
  151.1 1.9 %collective-permute-done.28 = bf16[4,96,96]{2,1,0:T(8,128)(2,1)S(1)} collective-permute-done((bf16[4,96,96]{2,1,0:T(8,128)(2,1)S(1)}, bf16[4,96,96]{2,1,0:T(8,128)(2,1)S(1)}, u32[]{:S(2)}, u32[]{:S(2)}) %collective-permute-start.28) | collective-permute-done | bytes 73760 | tf_op jit(solution)/shard_map/ppermute | solution.py:334
  152.9 3.0 %collective-permute-done.30 = bf16[4,96,96]{2,1,0:T(8,128)(2,1)S(1)} collective-permute-done((bf16[4,96,96]{2,1,0:T(8,128)(2,1)}, bf16[4,96,96]{2,1,0:T(8,128)(2,1)S(1)}, u32[]{:S(2)}, u32[]{:S(2)}) %collective-permute-start.30) | collective-permute-done | bytes 73760 | tf_op jit(solution)/shard_map/ppermute | solution.py:334
  156.2 1.1 collective-permute-start.32
  157.3 2.0 %collective-permute-start.33 = (bf16[4,96,96]{2,1,0:T(8,128)(2,1)S(1)}, bf16[4,96,96]{2,1,0:T(8,128)(2,1)S(1)}, u32[]{:S(2)}, u32[]{:S(2)}) collective-permute-start(bf16[4,96,96]{2,1,0:T(8,128)(2,1)S(1)} %add_convert_fusion), channel_id=1, source_target_pairs={{0,192},{64,0},{128,64},{192,128},{1,193},{65,1},{129,65},{193,129... | collective-permute-start | bytes 221192 | tf_op jit(solution)/shard_map/ppermute | solution.py:340
  159.3 4.4 %collective-permute-done.31 = bf16[4,96,96]{2,1,0:T(8,128)(2,1)S(1)} collective-permute-done((bf16[4,96,96]{2,1,0:T(8,128)(2,1)S(1)}, bf16[4,96,96]{2,1,0:T(8,128)(2,1)S(1)}, u32[]{:S(2)}, u32[]{:S(2)}) %collective-permute-start.31) | collective-permute-done | bytes 73760 | tf_op jit(solution)/shard_map/ppermute | solution.py:340
  164.1 0.9 copy.124
  (133 shorter events, 6.3 us)
Async XLA Ops:
  7.2 3.9 %copy-start.5 = (bf16[1,9,4,32,32]{4,3,2,1,0:T(8,128)(2,1)S(1)}, bf16[1,9,4,32,32]{4,3,2,1,0:T(8,128)(2,1)}, u32[]{:S(2)}) copy-start(bf16[1,9,4,32,32]{4,3,2,1,0:T(8,128)(2,1)} %param.9) | copy-start | bytes 221188
  7.2 4.3 %copy-start.8 = (s32[16,2]{0,1:T(2,128)S(1)}, s32[16,2]{0,1:T(2,128)}, u32[]{:S(2)}) copy-start(s32[16,2]{0,1:T(2,128)} %param.6) | copy-start | bytes 388
  7.2 4.5 %copy-start.7 = (bf16[16,2]{0,1:T(2,128)(2,1)S(1)}, bf16[16,2]{0,1:T(2,128)(2,1)}, u32[]{:S(2)}) copy-start(bf16[16,2]{0,1:T(2,128)(2,1)} %param.7) | copy-start | bytes 196
  7.2 111.8 %all-gather.2.cloned.1.call-start = ((), (), s32[]{:S(2)}) async-start(), calls=%async_computation | async-start | bytes 9437184 | tf_op jit(solution)/shard_map/all_gather | solution.py:250
  12.0 16.1 %collective-permute-start = (bf16[96,128]{1,0:T(8,128)(2,1)S(1)}, bf16[96,128]{1,0:T(8,128)(2,1)S(1)}, u32[]{:S(2)}, u32[]{:S(2)}) collective-permute-start(bf16[96,128]{1,0:T(8,128)(2,1)S(1)} %pad_maximum_fusion.1), channel_id=1, source_target_pairs={{0,8},{1,9},{2,10},{3,11},{4,12},{5,13},{6,14},{7,15},{8,16},{9,17... | collective-permute-start | bytes 73736 | tf_op jit(solution)/shard_map/ppermute | solution.py:279
  14.6 13.7 %collective-permute-start.4 = (bf16[96,128]{1,0:T(8,128)(2,1)S(1)}, bf16[96,128]{1,0:T(8,128)(2,1)S(1)}, u32[]{:S(2)}, u32[]{:S(2)}) collective-permute-start(bf16[96,128]{1,0:T(8,128)(2,1)S(1)} %pad_maximum_fusion.1), channel_id=1, source_target_pairs={{0,56},{1,57},{2,58},{3,59},{4,60},{5,61},{6,62},{7,63},{8,0},{9,1... | collective-permute-start | bytes 73736 | tf_op jit(solution)/shard_map/ppermute | solution.py:282
  18.6 42.7 %collective-permute-start.10 = (bf16[16,128,256]{2,1,0:T(8,128)(2,1)}, bf16[16,128,256]{2,1,0:T(8,128)(2,1)S(1)}, u32[]{:S(2)}, u32[]{:S(2)}) collective-permute-start(bf16[16,128,256]{2,1,0:T(8,128)(2,1)} %bitcast.1), channel_id=1, source_target_pairs={{0,2},{1,3},{2,4},{3,5},{4,6},{5,7},{6,0},{7,1},{8,10},{9,11},{10,... | collective-permute-start | bytes 3145736 | tf_op jit(solution)/shard_map/ppermute | solution.py:290
  19.9 41.4 %collective-permute-start.11 = (bf16[16,128,256]{2,1,0:T(8,128)(2,1)}, bf16[16,128,256]{2,1,0:T(8,128)(2,1)S(1)}, u32[]{:S(2)}, u32[]{:S(2)}) collective-permute-start(bf16[16,128,256]{2,1,0:T(8,128)(2,1)} %bitcast.2), channel_id=1, source_target_pairs={{0,6},{1,7},{2,0},{3,1},{4,2},{5,3},{6,4},{7,5},{8,14},{9,15},{10,... | collective-permute-start | bytes 3145736 | tf_op jit(solution)/shard_map/ppermute | solution.py:290
  28.2 4.9 %collective-permute-start.1 = (bf16[96,128]{1,0:T(8,128)(2,1)S(1)}, bf16[96,128]{1,0:T(8,128)(2,1)S(1)}, u32[]{:S(2)}, u32[]{:S(2)}) collective-permute-start(bf16[96,128]{1,0:T(8,128)(2,1)S(1)} %collective-permute-done), channel_id=1, source_target_pairs={{0,8},{1,9},{2,10},{3,11},{4,12},{5,13},{6,14},{7,15},{8,16},{9,17... | collective-permute-start | bytes 73736 | tf_op jit(solution)/shard_map/ppermute | solution.py:279
  28.3 4.8 %collective-permute-start.5 = (bf16[96,128]{1,0:T(8,128)(2,1)S(1)}, bf16[96,128]{1,0:T(8,128)(2,1)S(1)}, u32[]{:S(2)}, u32[]{:S(2)}) collective-permute-start(bf16[96,128]{1,0:T(8,128)(2,1)S(1)} %collective-permute-done.4), channel_id=1, source_target_pairs={{0,56},{1,57},{2,58},{3,59},{4,60},{5,61},{6,62},{7,63},{8,0},{9,1... | collective-permute-start | bytes 73736 | tf_op jit(solution)/shard_map/ppermute | solution.py:282
  33.0 4.8 %collective-permute-start.2 = (bf16[96,128]{1,0:T(8,128)(2,1)S(1)}, bf16[96,128]{1,0:T(8,128)(2,1)S(1)}, u32[]{:S(2)}, u32[]{:S(2)}) collective-permute-start(bf16[96,128]{1,0:T(8,128)(2,1)S(1)} %collective-permute-done.1), channel_id=1, source_target_pairs={{0,8},{1,9},{2,10},{3,11},{4,12},{5,13},{6,14},{7,15},{8,16},{9,17... | collective-permute-start | bytes 73736 | tf_op jit(solution)/shard_map/ppermute | solution.py:279
  33.0 9.6 %collective-permute-start.6 = (bf16[96,128]{1,0:T(8,128)(2,1)S(1)}, bf16[96,128]{1,0:T(8,128)(2,1)S(1)}, u32[]{:S(2)}, u32[]{:S(2)}) collective-permute-start(bf16[96,128]{1,0:T(8,128)(2,1)S(1)} %collective-permute-done.5), channel_id=1, source_target_pairs={{0,56},{1,57},{2,58},{3,59},{4,60},{5,61},{6,62},{7,63},{8,0},{9,1... | collective-permute-start | bytes 73736 | tf_op jit(solution)/shard_map/ppermute | solution.py:282
  37.8 4.8 %collective-permute-start.3 = (bf16[96,128]{1,0:T(8,128)(2,1)S(1)}, bf16[96,128]{1,0:T(8,128)(2,1)S(1)}, u32[]{:S(2)}, u32[]{:S(2)}) collective-permute-start(bf16[96,128]{1,0:T(8,128)(2,1)S(1)} %collective-permute-done.2), channel_id=1, source_target_pairs={{0,8},{1,9},{2,10},{3,11},{4,12},{5,13},{6,14},{7,15},{8,16},{9,17... | collective-permute-start | bytes 73736 | tf_op jit(solution)/shard_map/ppermute | solution.py:279
  42.7 10.8 %collective-permute-start.7 = (bf16[8,80,128]{2,1,0:T(8,128)(2,1)S(1)}, bf16[8,80,128]{2,1,0:T(8,128)(2,1)S(1)}, u32[]{:S(2)}, u32[]{:S(2)}) collective-permute-start(bf16[8,80,128]{2,1,0:T(8,128)(2,1)S(1)} %slice.48), channel_id=1, source_target_pairs={{0,2},{1,3},{2,4},{3,5},{4,6},{5,7},{6,0},{7,1},{8,10},{9,11},{10,... | collective-permute-start | bytes 491528 | tf_op jit(solution)/shard_map/ppermute | solution.py:292
  42.8 18.4 %collective-permute-start.8 = (bf16[8,80,128]{2,1,0:T(8,128)(2,1)S(1)}, bf16[8,80,128]{2,1,0:T(8,128)(2,1)S(1)}, u32[]{:S(2)}, u32[]{:S(2)}) collective-permute-start(bf16[8,80,128]{2,1,0:T(8,128)(2,1)S(1)} %slice.48), channel_id=1, source_target_pairs={{0,4},{1,5},{2,6},{3,7},{4,0},{5,1},{6,2},{7,3},{8,12},{9,13},{10,... | collective-permute-start | bytes 491528 | tf_op jit(solution)/shard_map/ppermute | solution.py:292
  47.0 29.0 %collective-permute-start.14 = (bf16[16,128,256]{2,1,0:T(8,128)(2,1)}, bf16[16,128,256]{2,1,0:T(8,128)(2,1)}, u32[]{:S(2)}, u32[]{:S(2)}) collective-permute-start(bf16[16,128,256]{2,1,0:T(8,128)(2,1)} %bitcast.14), channel_id=1, source_target_pairs={{0,3},{1,2},{2,5},{3,4},{4,7},{5,6},{6,1},{7,0},{8,11},{9,10},{10,... | collective-permute-start | bytes 3145736 | tf_op jit(solution)/shard_map/ppermute | solution.py:290
  53.5 7.8 %collective-permute-start.9 = (bf16[8,80,128]{2,1,0:T(8,128)(2,1)S(1)}, bf16[8,80,128]{2,1,0:T(8,128)(2,1)S(1)}, u32[]{:S(2)}, u32[]{:S(2)}) collective-permute-start(bf16[8,80,128]{2,1,0:T(8,128)(2,1)S(1)} %slice.48), channel_id=1, source_target_pairs={{0,6},{1,7},{2,0},{3,1},{4,2},{5,3},{6,4},{7,5},{8,14},{9,15},{10,... | collective-permute-start | bytes 491528 | tf_op jit(solution)/shard_map/ppermute | solution.py:292
  61.1 24.3 %collective-permute-start.15 = (bf16[16,128,256]{2,1,0:T(8,128)(2,1)}, bf16[16,128,256]{2,1,0:T(8,128)(2,1)}, u32[]{:S(2)}, u32[]{:S(2)}) collective-permute-start(bf16[16,128,256]{2,1,0:T(8,128)(2,1)} %bitcast.15), channel_id=1, source_target_pairs={{0,7},{1,6},{2,1},{3,0},{4,3},{5,2},{6,5},{7,4},{8,15},{9,14},{10,... | collective-permute-start | bytes 3145736 | tf_op jit(solution)/shard_map/ppermute | solution.py:290
  61.3 43.1 %copy-start.3 = (bf16[16,128,256]{2,1,0:T(8,128)(2,1)}, bf16[16,128,256]{2,1,0:T(8,128)(2,1)S(1)}, u32[]{:S(2)}) copy-start(bf16[16,128,256]{2,1,0:T(8,128)(2,1)S(1)} %collective-permute-done.10.refs_2_) | copy-start | bytes 3145732
  61.4 33.4 %copy-start.4 = (bf16[16,128,256]{2,1,0:T(8,128)(2,1)}, bf16[16,128,256]{2,1,0:T(8,128)(2,1)S(1)}, u32[]{:S(2)}) copy-start(bf16[16,128,256]{2,1,0:T(8,128)(2,1)S(1)} %collective-permute-done.11.refs_3_) | copy-start | bytes 3145732
  61.4 17.3 %collective-permute-start.12 = (bf16[32,80,128]{2,1,0:T(8,128)(2,1)S(1)}, bf16[32,80,128]{2,1,0:T(8,128)(2,1)S(1)}, u32[]{:S(2)}, u32[]{:S(2)}) collective-permute-start(bf16[32,80,128]{2,1,0:T(8,128)(2,1)S(1)} %bitcast.62), channel_id=1, source_target_pairs={{0,64},{64,128},{128,192},{192,0},{1,65},{65,129},{129,193},{193,1... | collective-permute-start | bytes 1966088 | tf_op jit(solution)/shard_map/ppermute | solution.py:295
  63.3 30.4 %collective-permute-start.13 = (bf16[32,80,128]{2,1,0:T(8,128)(2,1)S(1)}, bf16[32,80,128]{2,1,0:T(8,128)(2,1)}, u32[]{:S(2)}, u32[]{:S(2)}) collective-permute-start(bf16[32,80,128]{2,1,0:T(8,128)(2,1)S(1)} %bitcast.63), channel_id=1, source_target_pairs={{0,128},{64,192},{128,0},{192,64},{1,129},{65,193},{129,1},{193,65... | collective-permute-start | bytes 1966088 | tf_op jit(solution)/shard_map/ppermute | solution.py:295
  69.2 25.6 %collective-permute-start.16 = (bf16[32,80,128]{2,1,0:T(8,128)(2,1)S(1)}, bf16[32,80,128]{2,1,0:T(8,128)(2,1)}, u32[]{:S(2)}, u32[]{:S(2)}) collective-permute-start(bf16[32,80,128]{2,1,0:T(8,128)(2,1)S(1)} %bitcast.64), channel_id=1, source_target_pairs={{0,192},{64,0},{128,64},{192,128},{1,193},{65,1},{129,65},{193,129... | collective-permute-start | bytes 1966088 | tf_op jit(solution)/shard_map/ppermute | solution.py:295
  76.0 22.9 %collective-permute-start.17 = (bf16[32,80,128]{2,1,0:T(8,128)(2,1)S(1)}, bf16[32,80,128]{2,1,0:T(8,128)(2,1)}, u32[]{:S(2)}, u32[]{:S(2)}) collective-permute-start(bf16[32,80,128]{2,1,0:T(8,128)(2,1)S(1)} %bitcast.65), channel_id=1, source_target_pairs={{0,1},{1,0},{2,3},{3,2},{4,5},{5,4},{6,7},{7,6},{8,9},{9,8},{10,11... | collective-permute-start | bytes 1966088 | tf_op jit(solution)/shard_map/ppermute | solution.py:299
  78.7 20.2 %collective-permute-start.18 = (bf16[32,80,128]{2,1,0:T(8,128)(2,1)S(1)}, bf16[32,80,128]{2,1,0:T(8,128)(2,1)}, u32[]{:S(2)}, u32[]{:S(2)}) collective-permute-start(bf16[32,80,128]{2,1,0:T(8,128)(2,1)S(1)} %collective-permute-done.12), channel_id=1, source_target_pairs={{0,1},{1,0},{2,3},{3,2},{4,5},{5,4},{6,7},{7,6},{8,9},{9,8},{10,11... | collective-permute-start | bytes 1966088 | tf_op jit(solution)/shard_map/ppermute | solution.py:299
  85.4 30.2 %collective-permute-start.21 = (bf16[16,128,256]{2,1,0:T(8,128)(2,1)}, bf16[16,128,256]{2,1,0:T(8,128)(2,1)}, u32[]{:S(2)}, u32[]{:S(2)}) collective-permute-start(bf16[16,128,256]{2,1,0:T(8,128)(2,1)} %bitcast.69), channel_id=1, source_target_pairs={{0,1},{1,0},{2,3},{3,2},{4,5},{5,4},{6,7},{7,6},{8,9},{9,8},{10,11... | collective-permute-start | bytes 3145736 | tf_op jit(solution)/shard_map/ppermute | solution.py:290
  93.7 25.3 %collective-permute-start.22 = (bf16[16,128,256]{2,1,0:T(8,128)(2,1)}, bf16[16,128,256]{2,1,0:T(8,128)(2,1)}, u32[]{:S(2)}, u32[]{:S(2)}) collective-permute-start(bf16[16,128,256]{2,1,0:T(8,128)(2,1)} %bitcast.68), channel_id=1, source_target_pairs={{0,4},{1,5},{2,6},{3,7},{4,0},{5,1},{6,2},{7,3},{8,12},{9,13},{10,... | collective-permute-start | bytes 3145736 | tf_op jit(solution)/shard_map/ppermute | solution.py:290
  94.8 12.2 %copy-start.2 = (bf16[16,128,256]{2,1,0:T(8,128)(2,1)S(1)}, bf16[16,128,256]{2,1,0:T(8,128)(2,1)}, u32[]{:S(2)}) copy-start(bf16[16,128,256]{2,1,0:T(8,128)(2,1)} %grad_ref.1) | copy-start | bytes 3145732
  94.8 49.3 %collective-permute-start.29 = (bf16[16,128,256]{2,1,0:T(8,128)(2,1)}, bf16[16,128,256]{2,1,0:T(8,128)(2,1)}, u32[]{:S(2)}, u32[]{:S(2)}) collective-permute-start(bf16[16,128,256]{2,1,0:T(8,128)(2,1)} %bitcast.67), channel_id=1, source_target_pairs={{0,5},{1,4},{2,7},{3,6},{4,1},{5,0},{6,3},{7,2},{8,13},{9,12},{10,... | collective-permute-start | bytes 3145736 | tf_op jit(solution)/shard_map/ppermute | solution.py:290
  98.8 5.5 %collective-permute-start.19 = (bf16[32,80,128]{2,1,0:T(8,128)(2,1)}, bf16[32,80,128]{2,1,0:T(8,128)(2,1)S(1)}, u32[]{:S(2)}, u32[]{:S(2)}) collective-permute-start(bf16[32,80,128]{2,1,0:T(8,128)(2,1)} %collective-permute-done.13), channel_id=1, source_target_pairs={{0,1},{1,0},{2,3},{3,2},{4,5},{5,4},{6,7},{7,6},{8,9},{9,8},{10,11... | collective-permute-start | bytes 1966088 | tf_op jit(solution)/shard_map/ppermute | solution.py:299
  98.9 5.5 %collective-permute-start.20 = (bf16[32,80,128]{2,1,0:T(8,128)(2,1)}, bf16[32,80,128]{2,1,0:T(8,128)(2,1)S(1)}, u32[]{:S(2)}, u32[]{:S(2)}) collective-permute-start(bf16[32,80,128]{2,1,0:T(8,128)(2,1)} %collective-permute-done.16), channel_id=1, source_target_pairs={{0,1},{1,0},{2,3},{3,2},{4,5},{5,4},{6,7},{7,6},{8,9},{9,8},{10,11... | collective-permute-start | bytes 1966088 | tf_op jit(solution)/shard_map/ppermute | solution.py:299
  104.5 2.4 %copy-start = (bf16[256,80,128]{2,1,0:T(8,128)(2,1)}, bf16[256,80,128]{2,1,0:T(8,128)(2,1)S(1)}, u32[]{:S(2)}) copy-start(bf16[256,80,128]{2,1,0:T(8,128)(2,1)S(1)} %constant_dynamic-update-slice_fusion.8.weight_ref) | copy-start | bytes 15728644
  107.0 2.5 %copy-start.1 = (bf16[256,80,128]{2,1,0:T(8,128)(2,1)S(1)}, bf16[256,80,128]{2,1,0:T(8,128)(2,1)}, u32[]{:S(2)}) copy-start(bf16[256,80,128]{2,1,0:T(8,128)(2,1)} %copy-done) | copy-start | bytes 15728644
  126.9 20.5 %copy-start.9 = (bf16[4,96,96]{2,1,0:T(8,128)(2,1)S(1)}, bf16[4,96,96]{2,1,0:T(8,128)(2,1)}, u32[]{:S(2)}) copy-start(bf16[4,96,96]{2,1,0:T(8,128)(2,1)} %get-tuple-element.56) | copy-start | bytes 221188
  126.9 29.1 %copy-start.6 = (bf16[4,96,96]{2,1,0:T(8,128)(2,1)S(1)}, bf16[4,96,96]{2,1,0:T(8,128)(2,1)}, u32[]{:S(2)}) copy-start(bf16[4,96,96]{2,1,0:T(8,128)(2,1)} %get-tuple-element.50) | copy-start | bytes 221188
  126.9 20.5 %collective-permute-start.23 = (bf16[4,96,96]{2,1,0:T(8,128)(2,1)}, bf16[4,96,96]{2,1,0:T(8,128)(2,1)S(1)}, u32[]{:S(2)}, u32[]{:S(2)}) collective-permute-start(bf16[4,96,96]{2,1,0:T(8,128)(2,1)} %get-tuple-element.51), channel_id=1, source_target_pairs={{0,1},{1,0},{2,3},{3,2},{4,5},{5,4},{6,7},{7,6},{8,9},{9,8},{10,11... | collective-permute-start | bytes 221192 | tf_op jit(solution)/shard_map/ppermute | solution.py:334
  130.9 18.4 %collective-permute-start.24 = (bf16[4,96,96]{2,1,0:T(8,128)(2,1)}, bf16[4,96,96]{2,1,0:T(8,128)(2,1)S(1)}, u32[]{:S(2)}, u32[]{:S(2)}) collective-permute-start(bf16[4,96,96]{2,1,0:T(8,128)(2,1)} %get-tuple-element.52), channel_id=1, source_target_pairs={{0,6},{1,7},{2,0},{3,1},{4,2},{5,3},{6,4},{7,5},{8,14},{9,15},{10,... | collective-permute-start | bytes 221192 | tf_op jit(solution)/shard_map/ppermute | solution.py:334
  131.5 19.5 %collective-permute-start.25 = (bf16[4,96,96]{2,1,0:T(8,128)(2,1)}, bf16[4,96,96]{2,1,0:T(8,128)(2,1)S(1)}, u32[]{:S(2)}, u32[]{:S(2)}) collective-permute-start(bf16[4,96,96]{2,1,0:T(8,128)(2,1)} %get-tuple-element.53), channel_id=1, source_target_pairs={{0,2},{1,3},{2,4},{3,5},{4,6},{5,7},{6,0},{7,1},{8,10},{9,11},{10,... | collective-permute-start | bytes 221192 | tf_op jit(solution)/shard_map/ppermute | solution.py:334
  133.0 18.1 %collective-permute-start.26 = (bf16[4,96,96]{2,1,0:T(8,128)(2,1)}, bf16[4,96,96]{2,1,0:T(8,128)(2,1)S(1)}, u32[]{:S(2)}, u32[]{:S(2)}) collective-permute-start(bf16[4,96,96]{2,1,0:T(8,128)(2,1)} %get-tuple-element.54), channel_id=1, source_target_pairs={{0,7},{1,6},{2,1},{3,0},{4,3},{5,2},{6,5},{7,4},{8,15},{9,14},{10,... | collective-permute-start | bytes 221192 | tf_op jit(solution)/shard_map/ppermute | solution.py:334
  144.0 7.0 %collective-permute-start.27 = (bf16[4,96,96]{2,1,0:T(8,128)(2,1)}, bf16[4,96,96]{2,1,0:T(8,128)(2,1)S(1)}, u32[]{:S(2)}, u32[]{:S(2)}) collective-permute-start(bf16[4,96,96]{2,1,0:T(8,128)(2,1)} %get-tuple-element.55), channel_id=1, source_target_pairs={{0,3},{1,2},{2,5},{3,4},{4,7},{5,6},{6,1},{7,0},{8,11},{9,10},{10,... | collective-permute-start | bytes 221192 | tf_op jit(solution)/shard_map/ppermute | solution.py:334
  147.4 5.5 %collective-permute-start.28 = (bf16[4,96,96]{2,1,0:T(8,128)(2,1)S(1)}, bf16[4,96,96]{2,1,0:T(8,128)(2,1)S(1)}, u32[]{:S(2)}, u32[]{:S(2)}) collective-permute-start(bf16[4,96,96]{2,1,0:T(8,128)(2,1)S(1)} %copy-done.9), channel_id=1, source_target_pairs={{0,4},{1,5},{2,6},{3,7},{4,0},{5,1},{6,2},{7,3},{8,12},{9,13},{10,... | collective-permute-start | bytes 221192 | tf_op jit(solution)/shard_map/ppermute | solution.py:334
  149.3 6.7 %collective-permute-start.30 = (bf16[4,96,96]{2,1,0:T(8,128)(2,1)}, bf16[4,96,96]{2,1,0:T(8,128)(2,1)S(1)}, u32[]{:S(2)}, u32[]{:S(2)}) collective-permute-start(bf16[4,96,96]{2,1,0:T(8,128)(2,1)} %shard_map.70), channel_id=1, source_target_pairs={{0,5},{1,4},{2,7},{3,6},{4,1},{5,0},{6,3},{7,2},{8,13},{9,12},{10,... | collective-permute-start | bytes 221192 | tf_op jit(solution)/shard_map/ppermute | solution.py:334
  156.1 7.6 %collective-permute-start.31 = (bf16[4,96,96]{2,1,0:T(8,128)(2,1)S(1)}, bf16[4,96,96]{2,1,0:T(8,128)(2,1)S(1)}, u32[]{:S(2)}, u32[]{:S(2)}) collective-permute-start(bf16[4,96,96]{2,1,0:T(8,128)(2,1)S(1)} %add_convert_fusion), channel_id=1, source_target_pairs={{0,64},{64,128},{128,192},{192,0},{1,65},{65,129},{129,193},{193,1... | collective-permute-start | bytes 221192 | tf_op jit(solution)/shard_map/ppermute | solution.py:340
  156.2 7.5 %collective-permute-start.32 = (bf16[4,96,96]{2,1,0:T(8,128)(2,1)S(1)}, bf16[4,96,96]{2,1,0:T(8,128)(2,1)S(1)}, u32[]{:S(2)}, u32[]{:S(2)}) collective-permute-start(bf16[4,96,96]{2,1,0:T(8,128)(2,1)S(1)} %add_convert_fusion), channel_id=1, source_target_pairs={{0,128},{64,192},{128,0},{192,64},{1,129},{65,193},{129,1},{193,65... | collective-permute-start | bytes 221192 | tf_op jit(solution)/shard_map/ppermute | solution.py:340
  157.3 6.4 %collective-permute-start.33 = (bf16[4,96,96]{2,1,0:T(8,128)(2,1)S(1)}, bf16[4,96,96]{2,1,0:T(8,128)(2,1)S(1)}, u32[]{:S(2)}, u32[]{:S(2)}) collective-permute-start(bf16[4,96,96]{2,1,0:T(8,128)(2,1)S(1)} %add_convert_fusion), channel_id=1, source_target_pairs={{0,192},{64,0},{128,64},{192,128},{1,193},{65,1},{129,65},{193,129... | collective-permute-start | bytes 221192 | tf_op jit(solution)/shard_map/ppermute | solution.py:340
Sparse Core Ops, SparseCore 0:
  9.8 99.5 all-gather.1

commit v5 on v4

--- a/solution.py
+++ b/solution.py
@@ -269,7 +269,9 @@
     note = jnp.pad(note, ((0, 15), (0, CHANNELS - 2 * rows * top)))
     held = jnp.concatenate([piece, note], 0)
     kept, held, *first = lax.optimization_barrier((kept, held, *first))
-    own, *rest = [sent(kept, d, dc) for d, dc in offsets[:2] + offsets[4:]]
+    second = [sent(kept, d, dc) for d, dc in offsets[4:6]]
+    held, *second = lax.optimization_barrier((held, *second))
+    first = [lax.ppermute(part, "ep", ep_perm(0, d, dc)) for part, (d, dc) in zip(first, offsets[2:])]
     experts = [e - y * NC - c + ((y - d) % NY) * NC + (c ^ dc) for d, dc in offsets]
     experts = jnp.stack(experts)
 
@@ -284,14 +286,14 @@
     held = jnp.stack([from_z[d] for d in range(NZ)])
     notes = held[:, PIECE, : 2 * rows * top].astype(jnp.float32)
     held = held[:, :PIECE]
-    held, *rest = lax.optimization_barrier((held, *rest))
-    rest = rest[:1] + first + rest[1:]
-    chunks = [own] + [
-        lax.ppermute(part, "ep", ep_perm(0, d, dc)) for part, (d, dc) in zip(rest, offsets[1:])
-    ]
+    held, kept, *first = lax.optimization_barrier((held, kept, *first))
+    second = lax.optimization_barrier((held, *second))[1:]
+    own, *rest = [sent(kept, d, dc) for d, dc in offsets[:2] + offsets[6:]]
+    sends = zip([rest[0], *second, *rest[1:]], offsets[1:2] + offsets[4:])
+    rest = [lax.ppermute(part, "ep", ep_perm(0, d, dc)) for part, (d, dc) in sends]
+    chunks = [own, rest[0], *first, *rest[1:]]
     held = stack_of(held, [lax.ppermute(held, "ep", ep_perm(0, d, 0)) for d in range(1, NY)])
     held = held.reshape(NY * NZ, PIECE, CHANNELS)
-    held, chunks[2], chunks[3] = lax.optimization_barrier((held, chunks[2], chunks[3]))
     quarters = [held] + [lax.ppermute(held, "rep", rep_perm(d)) for d in range(1, NX)]
     quarters[2], chunks[4], chunks[5] = lax.optimization_barrier(
         (quarters[2], chunks[4], chunks[5])

time: 173 us -> 175 us (1.012); the launches traced: 172 us -> 172 us
  waiting for transfers between devices: 50 us -> 39.6 us
  starting transfers between devices: 51.3 us -> 58.8 us
  local copies, waits for them, and re-layouts: 27.7 us -> 30.5 us
  Pallas kernels: 17.3 us -> 15.3 us
  other arithmetic: 7.88 us -> 9.68 us
    ppermute x7, waiting for transfers between devices: 21.5 us -> 13.7 us  [per_device(): lax.ppermute(part, 'ep', ep_perm(0, d, dc))]
    ppermute x7, starting transfers between devices: 10.8 us -> 16 us  [per_device(): part = lax.ppermute(part, 'ep', ep_perm(0, -d, dc))]
    ppermute x3, waiting for transfers between devices: 0.01 us -> 4.39 us  [per_device(): lax.ppermute(held, 'ep', ep_perm(0, d, 0))]
    ppermute x3, waiting for transfers between devices: 4.39 us -> 1.94 us  [per_device(): lax.ppermute(total, 'rep', rep_perm(d)).astype(jnp.float32)]
    ppermute x4, waiting for transfers between devices: 8.81 us -> 6.5 us  [per_device(): up = lax.ppermute(up, 'ep', ep_perm(1, 0, 0))]
    ppermute x7, starting transfers between devices: 12 us -> 14.2 us  [per_device(): lax.ppermute(part, 'ep', ep_perm(0, d, dc))]
    pallas_call x2, Pallas kernels: 11.2 us -> 9.23 us  [weight_grads(): pl.pallas_call(functools.partial(weight_kernel, chunks), out_shape=[jax.S...]
    ppermute x3, starting transfers between devices: 5.09 us -> 3.28 us  [per_device(): lax.ppermute(held, 'ep', ep_perm(0, d, 0))]
  transfers between devices with their start and end apart: 35 -> 35, of which waited for: 12 -> 13; matrix products, arithmetic and copies ran while one was open for 17% -> 20% of each run, Pallas kernels for 10% -> 9%
where the time goes in v5:
time: 175 us; the launch traced here: 172 us
  starting transfers between devices  58.8 us (34%)
  waiting for transfers between devices  39.6 us (23%)
  local copies, waits for them, and re-layouts  30.5 us (17%)
  between operations  17.5 us (10%)
  Pallas kernels  15.3 us (9%)
  other arithmetic  9.68 us (6%)
    ppermute x7, starting transfers between devices, per_device(): part = lax.ppermute(part, 'ep', ep_perm(0, -d, dc))  16 us
    ppermute x7, starting transfers between devices, per_device(): lax.ppermute(part, 'ep', ep_perm(0, d, dc))  14.2 us
    ppermute x7, waiting for transfers between devices, per_device(): lax.ppermute(part, 'ep', ep_perm(0, d, dc))  13.7 us
    unnamed x42, local copies, waits for them, and re-layouts  11 us
    dynamic_slice x3, local copies, waits for them, and re-layouts, sent(): lax.dynamic_slice(kept, (0, (y + d) % NY, c ^ dc, 0, 0, 0), (NZ, 1, 1, 2,...  10.2 us
    ppermute x3, starting transfers between devices, per_device(): down = lax.ppermute(down, 'ep', ep_perm(-1, 0, 0))  9.6 us
    pallas_call x2, Pallas kernels, weight_grads(): pl.pallas_call(functools.partial(weight_kernel, chunks), out_shape=[jax.S...  9.23 us
    ppermute x3, waiting for transfers between devices, per_device(): lax.ppermute(held, 'rep', rep_perm(d))  8.16 us
  transfers between devices with their start and end apart: 35, of which 13 were waited for; matrix products, arithmetic and copies ran while one was open for 20% of the time, Pallas kernels for 9%

profile of v5, /device:TPU:1, one launch (start us, length us, event | category | flops | bytes accessed | tf_op | source)
XLA Modules:
  0.0 171.5 jit_solution(7673318996454618966)
XLA Ops:
  7.2 0.7 all-gather.2.cloned.1.call-update
  8.0 2.7 %constant_dynamic-slice_fusion.6 = (bf16[8,1,1,2,128,256]{5,4,3,2,1,0:T(8,128)(2,1)S(1)}, bf16[8,1,1,2,128,256]{5,4,3,2,1,0:T(8,128)(2,1)}) fusion(bf16[8,4,2,2,128,256]{5,4,3,2,1,0:T(8,128)(2,1)} %bitcast.58, s32[]{:T(128)S(6)} %select_n.250, s32[]{:T(128)S(6)} %select_n.248, s32[]{:T(128)S(6)} %select_n.247), kind=kLoop, calls=%fused_computation.72 | loop fusion | bytes 4194316 | tf_op jit(solution)/shard_map/dynamic_slice | solution.py:256
  11.6 3.1 %constant_dynamic-slice_fusion.4 = (bf16[8,1,1,2,128,256]{5,4,3,0,2,1:T(8,128)(2,1)}, bf16[8,1,1,2,128,256]{5,4,3,0,2,1:T(8,128)(2,1)}) fusion(s32[]{:T(128)S(6)} %select_n.250, s32[]{:T(128)S(6)} %select_n.252, s32[]{:T(128)S(6)} %select_n.247, bf16[8,4,2,2,128,256]{5,4,3,2,1,0:T(8,128)(2,1)} %bitcast.59), kind=kLoop, calls=%fused_computation.70 | loop fusion | bytes 4194316 | tf_op jit(solution)/shard_map/dynamic_slice | solution.py:256
  14.8 2.5 %collective-permute-start = (bf16[96,128]{1,0:T(8,128)(2,1)S(1)}, bf16[96,128]{1,0:T(8,128)(2,1)S(1)}, u32[]{:S(2)}, u32[]{:S(2)}) collective-permute-start(bf16[96,128]{1,0:T(8,128)(2,1)S(1)} %pad_maximum_fusion.1), channel_id=1, source_target_pairs={{0,8},{1,9},{2,10},{3,11},{4,12},{5,13},{6,14},{7,15},{8,16},{9,17... | collective-permute-start | bytes 73736 | tf_op jit(solution)/shard_map/ppermute | solution.py:281
  17.3 3.9 %collective-permute-start.4 = (bf16[96,128]{1,0:T(8,128)(2,1)S(1)}, bf16[96,128]{1,0:T(8,128)(2,1)S(1)}, u32[]{:S(2)}, u32[]{:S(2)}) collective-permute-start(bf16[96,128]{1,0:T(8,128)(2,1)S(1)} %pad_maximum_fusion.1), channel_id=1, source_target_pairs={{0,56},{1,57},{2,58},{3,59},{4,60},{5,61},{6,62},{7,63},{8,0},{9,1... | collective-permute-start | bytes 73736 | tf_op jit(solution)/shard_map/ppermute | solution.py:284
  21.2 1.3 collective-permute-start.7
  22.5 1.4 collective-permute-start.8
  24.4 0.6 constant_dynamic-update-slice_fusion.7
  25.8 0.6 constant_dynamic-update-slice_fusion.6
  26.4 2.7 %collective-permute-start.5 = (bf16[96,128]{1,0:T(8,128)(2,1)S(1)}, bf16[96,128]{1,0:T(8,128)(2,1)S(1)}, u32[]{:S(2)}, u32[]{:S(2)}) collective-permute-start(bf16[96,128]{1,0:T(8,128)(2,1)S(1)} %collective-permute-done.4), channel_id=1, source_target_pairs={{0,56},{1,57},{2,58},{3,59},{4,60},{5,61},{6,62},{7,63},{8,0},{9,1... | collective-permute-start | bytes 73736 | tf_op jit(solution)/shard_map/ppermute | solution.py:284
  29.0 1.2 collective-permute-done.1
  30.2 0.6 constant_dynamic-update-slice_fusion.5
  30.8 3.0 %collective-permute-start.6 = (bf16[96,128]{1,0:T(8,128)(2,1)S(1)}, bf16[96,128]{1,0:T(8,128)(2,1)S(1)}, u32[]{:S(2)}, u32[]{:S(2)}) collective-permute-start(bf16[96,128]{1,0:T(8,128)(2,1)S(1)} %collective-permute-done.5), channel_id=1, source_target_pairs={{0,56},{1,57},{2,58},{3,59},{4,60},{5,61},{6,62},{7,63},{8,0},{9,1... | collective-permute-start | bytes 73736 | tf_op jit(solution)/shard_map/ppermute | solution.py:284
  33.8 1.2 collective-permute-done.2
  35.0 0.6 constant_dynamic-update-slice_fusion.4
  35.6 4.2 %collective-permute-done.3 = bf16[96,128]{1,0:T(8,128)(2,1)S(1)} collective-permute-done((bf16[96,128]{1,0:T(8,128)(2,1)S(1)}, bf16[96,128]{1,0:T(8,128)(2,1)S(1)}, u32[]{:S(2)}, u32[]{:S(2)}) %collective-permute-start.3) | collective-permute-done | bytes 24608 | tf_op jit(solution)/shard_map/ppermute | solution.py:281
  39.8 0.6 constant_dynamic-update-slice_fusion.3
  40.4 0.6 constant_dynamic-update-slice_fusion.2
  42.2 0.7 slice_convert_fusion
  43.0 0.7 fusion.23
  44.8 1.2 convert_reduce_fusion.5
  46.1 0.9 slice.48
  48.9 2.5 %collective-permute-start.10 = (bf16[8,80,128]{2,1,0:T(8,128)(2,1)S(1)}, bf16[8,80,128]{2,1,0:T(8,128)(2,1)S(1)}, u32[]{:S(2)}, u32[]{:S(2)}) collective-permute-start(bf16[8,80,128]{2,1,0:T(8,128)(2,1)S(1)} %slice.48), channel_id=1, source_target_pairs={{0,4},{1,5},{2,6},{3,7},{4,0},{5,1},{6,2},{7,3},{8,12},{9,13},{10,... | collective-permute-start | bytes 491528 | tf_op jit(solution)/shard_map/ppermute | solution.py:295
  51.4 0.7 collective-permute-start.11
  52.6 3.8 %collective-permute-done.9 = bf16[8,80,128]{2,1,0:T(8,128)(2,1)S(1)} collective-permute-done((bf16[8,80,128]{2,1,0:T(8,128)(2,1)S(1)}, bf16[8,80,128]{2,1,0:T(8,128)(2,1)S(1)}, u32[]{:S(2)}, u32[]{:S(2)}) %collective-permute-start.9) | collective-permute-done | bytes 163872 | tf_op jit(solution)/shard_map/ppermute | solution.py:295
  57.2 3.0 %collective-permute-start.13 = (bf16[32,80,128]{2,1,0:T(8,128)(2,1)S(1)}, bf16[32,80,128]{2,1,0:T(8,128)(2,1)S(1)}, u32[]{:S(2)}, u32[]{:S(2)}) collective-permute-start(bf16[32,80,128]{2,1,0:T(8,128)(2,1)S(1)} %bitcast.63), channel_id=1, source_target_pairs={{0,128},{64,192},{128,0},{192,64},{1,129},{65,193},{129,1},{193,65... | collective-permute-start | bytes 1966088 | tf_op jit(solution)/shard_map/ppermute | solution.py:297
  60.2 0.8 select_reduce_fusion
  61.0 6.3 %collective-permute-start.14 = (bf16[16,128,256]{2,1,0:T(8,128)(2,1)}, bf16[16,128,256]{2,1,0:T(8,128)(2,1)}, u32[]{:S(2)}, u32[]{:S(2)}) collective-permute-start(bf16[16,128,256]{2,1,0:T(8,128)(2,1)} %bitcast.69), channel_id=1, source_target_pairs={{0,3},{1,2},{2,5},{3,4},{4,7},{5,6},{6,1},{7,0},{8,11},{9,10},{10,... | collective-permute-start | bytes 3145736 | tf_op jit(solution)/shard_map/ppermute | solution.py:293
  67.3 1.4 collective-permute-start.15
  69.1 1.3 slice.41
  73.2 0.7 copy.119
  74.0 0.7 copy.121
  74.7 0.8 copy.120
  75.9 0.6 select_reduce_fusion.6.gate_of
  76.5 1.3 select_reduce_fusion.2.gate_of
  77.8 2.4 %collective-permute-start.16 = (bf16[32,80,128]{2,1,0:T(8,128)(2,1)S(1)}, bf16[32,80,128]{2,1,0:T(8,128)(2,1)S(1)}, u32[]{:S(2)}, u32[]{:S(2)}) collective-permute-start(bf16[32,80,128]{2,1,0:T(8,128)(2,1)S(1)} %bitcast.65), channel_id=1, source_target_pairs={{0,192},{64,0},{128,64},{192,128},{1,193},{65,1},{129,65},{193,129... | collective-permute-start | bytes 1966088 | tf_op jit(solution)/shard_map/ppermute | solution.py:297
  80.2 1.1 collective-permute-start.17
  81.4 8.2 %collective-permute-done.12 = bf16[32,80,128]{2,1,0:T(8,128)(2,1)} collective-permute-done((bf16[32,80,128]{2,1,0:T(8,128)(2,1)S(1)}, bf16[32,80,128]{2,1,0:T(8,128)(2,1)}, u32[]{:S(2)}, u32[]{:S(2)}) %collective-permute-start.12) | collective-permute-done | bytes 655392 | tf_op jit(solution)/shard_map/ppermute | solution.py:297
  89.6 0.9 collective-permute-start.18
  90.5 4.3 %constant_dynamic-slice_fusion.1 = (bf16[8,1,1,2,128,256]{5,4,3,0,2,1:T(8,128)(2,1)}, bf16[8,1,1,2,128,256]{5,4,3,0,2,1:T(8,128)(2,1)}, bf16[8,1,1,2,128,256]{5,...) fusion(s32[]{:T(128)S(6)} %select_n.269, s32[]{:T(128)S(6)} %select_n.248, s32[]{:T(128)S(6)} %select_n.252, ...), kind=kLoop, calls=%fused_computation.67 | loop fusion | bytes 8388624 | tf_op jit(solution)/shard_map/dynamic_slice | solution.py:256
  94.9 1.2 collective-permute-start.22
  96.1 0.7 pad_add_fusion.2.plan
  96.8 2.5 %collective-permute-start.29 = (bf16[16,128,256]{2,1,0:T(8,128)(2,1)}, bf16[16,128,256]{2,1,0:T(8,128)(2,1)}, u32[]{:S(2)}, u32[]{:S(2)}) collective-permute-start(bf16[16,128,256]{2,1,0:T(8,128)(2,1)} %bitcast.38), channel_id=1, source_target_pairs={{0,5},{1,4},{2,7},{3,6},{4,1},{5,0},{6,3},{7,2},{8,13},{9,12},{10,... | collective-permute-start | bytes 3145736 | tf_op jit(solution)/shard_map/ppermute | solution.py:293
  99.9 1.2 constant_dynamic-update-slice_fusion.14
  101.6 0.7 collective-permute-done.20
  102.4 2.4 %copy-done = bf16[256,80,128]{2,1,0:T(8,128)(2,1)} copy-done((bf16[256,80,128]{2,1,0:T(8,128)(2,1)}, bf16[256,80,128]{2,1,0:T(8,128)(2,1)S(1)}, u32[]{:S(2)}) %copy-start) | copy-done | bytes 5242904
  104.9 2.5 %copy-done.1 = bf16[256,80,128]{2,1,0:T(8,128)(2,1)S(1)} copy-done((bf16[256,80,128]{2,1,0:T(8,128)(2,1)S(1)}, bf16[256,80,128]{2,1,0:T(8,128)(2,1)}, u32[]{:S(2)}) %copy-start.1) | copy-done | bytes 5242904
  107.3 6.1 %shard_map.68 = bf16[16,128,256]{2,1,0:T(8,128)(2,1)} custom-call(s32[128]{0:T(128)S(1)} %add.346.place_ref, f32[32]{0:T(128)S(1)} %reshape.729.gate_ref, bf16[16,128,256]{2,1,0:T(8,128)(2,1)S(1)} %copy-done.2, bf16[256,80,128]{2,1,0:T(8,128)(2,1)S(1)} %copy-done.1), custom_call_target="tpu_custom_call" | custom-call | flops 1 | bytes 1 | tf_op jit(solution)/shard_map/pallas_call | solution.py:76
  113.5 7.6 %collective-permute-done.22.refs_6_ = bf16[16,128,256]{2,1,0:T(8,128)(2,1)} collective-permute-done((bf16[16,128,256]{2,1,0:T(8,128)(2,1)}, bf16[16,128,256]{2,1,0:T(8,128)(2,1)}, u32[]{:S(2)}, u32[]{:S(2)}) %collective-permute-start.22) | collective-permute-done | bytes 1048608 | tf_op jit(solution)/shard_map/ppermute | solution.py:293
  121.1 5.9 %shard_map.69 = (bf16[4,96,96]{2,1,0:T(8,128)(2,1)}, bf16[4,96,96]{2,1,0:T(8,128)(2,1)}, bf16[4,96,96]{2,1,0:T(8,128)(2,1)}, bf16[4,96,96]{2,1,0:T(8,128)(2,1)},...) custom-call(s32[291]{0:T(512)} %pad_add_fusion.2.plan, ...), custom_call_target="tpu_custom_call" | custom-call | flops 1 | bytes 1 | tf_op jit(solution)/shard_map/pallas_call | solution.py:221
  127.0 2.2 %collective-permute-start.23 = (bf16[4,96,96]{2,1,0:T(8,128)(2,1)}, bf16[4,96,96]{2,1,0:T(8,128)(2,1)S(1)}, u32[]{:S(2)}, u32[]{:S(2)}) collective-permute-start(bf16[4,96,96]{2,1,0:T(8,128)(2,1)} %get-tuple-element.52), channel_id=1, source_target_pairs={{0,1},{1,0},{2,3},{3,2},{4,5},{5,4},{6,7},{7,6},{8,9},{9,8},{10,11... | collective-permute-start | bytes 221192 | tf_op jit(solution)/shard_map/ppermute | solution.py:336
  129.2 5.7 %collective-permute-start.24 = (bf16[4,96,96]{2,1,0:T(8,128)(2,1)}, bf16[4,96,96]{2,1,0:T(8,128)(2,1)S(1)}, u32[]{:S(2)}, u32[]{:S(2)}) collective-permute-start(bf16[4,96,96]{2,1,0:T(8,128)(2,1)} %get-tuple-element.53), channel_id=1, source_target_pairs={{0,6},{1,7},{2,0},{3,1},{4,2},{5,3},{6,4},{7,5},{8,14},{9,15},{10,... | collective-permute-start | bytes 221192 | tf_op jit(solution)/shard_map/ppermute | solution.py:336
  134.9 0.6 pad_add_fusion.3.plan
  135.5 3.4 %collective-permute-start.26 = (bf16[4,96,96]{2,1,0:T(8,128)(2,1)}, bf16[4,96,96]{2,1,0:T(8,128)(2,1)S(1)}, u32[]{:S(2)}, u32[]{:S(2)}) collective-permute-start(bf16[4,96,96]{2,1,0:T(8,128)(2,1)} %get-tuple-element.55), channel_id=1, source_target_pairs={{0,7},{1,6},{2,1},{3,0},{4,3},{5,2},{6,5},{7,4},{8,15},{9,14},{10,... | collective-permute-start | bytes 221192 | tf_op jit(solution)/shard_map/ppermute | solution.py:336
  139.0 6.0 %collective-permute-done.29.refs_0_ = bf16[16,128,256]{2,1,0:T(8,128)(2,1)} collective-permute-done((bf16[16,128,256]{2,1,0:T(8,128)(2,1)}, bf16[16,128,256]{2,1,0:T(8,128)(2,1)}, u32[]{:S(2)}, u32[]{:S(2)}) %collective-permute-start.29) | collective-permute-done | bytes 1048608 | tf_op jit(solution)/shard_map/ppermute | solution.py:293
  145.0 3.3 %shard_map.70 = bf16[4,96,96]{2,1,0:T(8,128)(2,1)} custom-call(s32[51]{0:T(128)} %pad_add_fusion.3.plan, f32[20]{0:T(128)} %select_reduce_fusion.6.gate_of, bf16[128,128,256]{2,1,0:T(8,128)(2,1)} %all-gather.2.cloned.1.call-done.grads, bf16[16,128,256]{2,1,0:T(8,128)(2,1)} %collective-permute-done.29.refs_0_), custom_call_target="tpu_custom_call" | custom-call | flops 1 | bytes 1 | tf_op jit(solution)/shard_map/pallas_call | solution.py:221
  148.4 2.5 %collective-permute-start.28 = (bf16[4,96,96]{2,1,0:T(8,128)(2,1)S(1)}, bf16[4,96,96]{2,1,0:T(8,128)(2,1)S(1)}, u32[]{:S(2)}, u32[]{:S(2)}) collective-permute-start(bf16[4,96,96]{2,1,0:T(8,128)(2,1)S(1)} %copy-done.11), channel_id=1, source_target_pairs={{0,4},{1,5},{2,6},{3,7},{4,0},{5,1},{6,2},{7,3},{8,12},{9,13},{10,... | collective-permute-start | bytes 221192 | tf_op jit(solution)/shard_map/ppermute | solution.py:336
  150.9 2.2 %collective-permute-start.30 = (bf16[4,96,96]{2,1,0:T(8,128)(2,1)}, bf16[4,96,96]{2,1,0:T(8,128)(2,1)S(1)}, u32[]{:S(2)}, u32[]{:S(2)}) collective-permute-start(bf16[4,96,96]{2,1,0:T(8,128)(2,1)} %shard_map.70), channel_id=1, source_target_pairs={{0,5},{1,4},{2,7},{3,6},{4,1},{5,0},{6,3},{7,2},{8,13},{9,12},{10,... | collective-permute-start | bytes 221192 | tf_op jit(solution)/shard_map/ppermute | solution.py:336
  153.4 3.2 %collective-permute-done.30 = bf16[4,96,96]{2,1,0:T(8,128)(2,1)S(1)} collective-permute-done((bf16[4,96,96]{2,1,0:T(8,128)(2,1)}, bf16[4,96,96]{2,1,0:T(8,128)(2,1)S(1)}, u32[]{:S(2)}, u32[]{:S(2)}) %collective-permute-start.30) | collective-permute-done | bytes 73760 | tf_op jit(solution)/shard_map/ppermute | solution.py:336
  156.7 1.2 collective-permute-start.31
  157.9 1.6 collective-permute-start.32
  159.5 2.0 %collective-permute-start.33 = (bf16[4,96,96]{2,1,0:T(8,128)(2,1)S(1)}, bf16[4,96,96]{2,1,0:T(8,128)(2,1)S(1)}, u32[]{:S(2)}, u32[]{:S(2)}) collective-permute-start(bf16[4,96,96]{2,1,0:T(8,128)(2,1)S(1)} %add_convert_fusion), channel_id=1, source_target_pairs={{0,192},{64,0},{128,64},{192,128},{1,193},{65,1},{129,65},{193,129... | collective-permute-start | bytes 221192 | tf_op jit(solution)/shard_map/ppermute | solution.py:342
  161.5 1.5 collective-permute-done.32
  163.8 0.9 copy.124
  (140 shorter events, 11.0 us)
Async XLA Ops:
  7.2 3.5 %copy-start.5 = (bf16[1,9,4,32,32]{4,3,2,1,0:T(8,128)(2,1)S(1)}, bf16[1,9,4,32,32]{4,3,2,1,0:T(8,128)(2,1)}, u32[]{:S(2)}) copy-start(bf16[1,9,4,32,32]{4,3,2,1,0:T(8,128)(2,1)} %param.9) | copy-start | bytes 221188
  7.2 3.9 %copy-start.10 = (s32[16,2]{0,1:T(2,128)S(1)}, s32[16,2]{0,1:T(2,128)}, u32[]{:S(2)}) copy-start(s32[16,2]{0,1:T(2,128)} %param.6) | copy-start | bytes 388
  7.2 4.1 %copy-start.9 = (bf16[16,2]{0,1:T(2,128)(2,1)S(1)}, bf16[16,2]{0,1:T(2,128)(2,1)}, u32[]{:S(2)}) copy-start(bf16[16,2]{0,1:T(2,128)(2,1)} %param.7) | copy-start | bytes 196
  7.2 113.9 %all-gather.2.cloned.1.call-start = ((), (), s32[]{:S(2)}) async-start(), calls=%async_computation | async-start | bytes 9437184 | tf_op jit(solution)/shard_map/all_gather | solution.py:250
  14.8 10.9 %collective-permute-start = (bf16[96,128]{1,0:T(8,128)(2,1)S(1)}, bf16[96,128]{1,0:T(8,128)(2,1)S(1)}, u32[]{:S(2)}, u32[]{:S(2)}) collective-permute-start(bf16[96,128]{1,0:T(8,128)(2,1)S(1)} %pad_maximum_fusion.1), channel_id=1, source_target_pairs={{0,8},{1,9},{2,10},{3,11},{4,12},{5,13},{6,14},{7,15},{8,16},{9,17... | collective-permute-start | bytes 73736 | tf_op jit(solution)/shard_map/ppermute | solution.py:281
  17.3 9.1 %collective-permute-start.4 = (bf16[96,128]{1,0:T(8,128)(2,1)S(1)}, bf16[96,128]{1,0:T(8,128)(2,1)S(1)}, u32[]{:S(2)}, u32[]{:S(2)}) collective-permute-start(bf16[96,128]{1,0:T(8,128)(2,1)S(1)} %pad_maximum_fusion.1), channel_id=1, source_target_pairs={{0,56},{1,57},{2,58},{3,59},{4,60},{5,61},{6,62},{7,63},{8,0},{9,1... | collective-permute-start | bytes 73736 | tf_op jit(solution)/shard_map/ppermute | solution.py:284
  21.2 27.6 %collective-permute-start.7 = (bf16[16,128,256]{2,1,0:T(8,128)(2,1)}, bf16[16,128,256]{2,1,0:T(8,128)(2,1)S(1)}, u32[]{:S(2)}, u32[]{:S(2)}) collective-permute-start(bf16[16,128,256]{2,1,0:T(8,128)(2,1)} %bitcast.1), channel_id=1, source_target_pairs={{0,2},{1,3},{2,4},{3,5},{4,6},{5,7},{6,0},{7,1},{8,10},{9,11},{10,... | collective-permute-start | bytes 3145736 | tf_op jit(solution)/shard_map/ppermute | solution.py:274
  22.5 26.3 %collective-permute-start.8 = (bf16[16,128,256]{2,1,0:T(8,128)(2,1)S(1)}, bf16[16,128,256]{2,1,0:T(8,128)(2,1)S(1)}, u32[]{:S(2)}, u32[]{:S(2)}) collective-permute-start(bf16[16,128,256]{2,1,0:T(8,128)(2,1)S(1)} %bitcast.70), channel_id=1, source_target_pairs={{0,6},{1,7},{2,0},{3,1},{4,2},{5,3},{6,4},{7,5},{8,14},{9,15},{10,... | collective-permute-start | bytes 3145736 | tf_op jit(solution)/shard_map/ppermute | solution.py:274
  25.7 4.5 %collective-permute-start.1 = (bf16[96,128]{1,0:T(8,128)(2,1)S(1)}, bf16[96,128]{1,0:T(8,128)(2,1)S(1)}, u32[]{:S(2)}, u32[]{:S(2)}) collective-permute-start(bf16[96,128]{1,0:T(8,128)(2,1)S(1)} %collective-permute-done), channel_id=1, source_target_pairs={{0,8},{1,9},{2,10},{3,11},{4,12},{5,13},{6,14},{7,15},{8,16},{9,17... | collective-permute-start | bytes 73736 | tf_op jit(solution)/shard_map/ppermute | solution.py:281
  26.4 4.4 %collective-permute-start.5 = (bf16[96,128]{1,0:T(8,128)(2,1)S(1)}, bf16[96,128]{1,0:T(8,128)(2,1)S(1)}, u32[]{:S(2)}, u32[]{:S(2)}) collective-permute-start(bf16[96,128]{1,0:T(8,128)(2,1)S(1)} %collective-permute-done.4), channel_id=1, source_target_pairs={{0,56},{1,57},{2,58},{3,59},{4,60},{5,61},{6,62},{7,63},{8,0},{9,1... | collective-permute-start | bytes 73736 | tf_op jit(solution)/shard_map/ppermute | solution.py:284
  30.2 4.8 %collective-permute-start.2 = (bf16[96,128]{1,0:T(8,128)(2,1)S(1)}, bf16[96,128]{1,0:T(8,128)(2,1)S(1)}, u32[]{:S(2)}, u32[]{:S(2)}) collective-permute-start(bf16[96,128]{1,0:T(8,128)(2,1)S(1)} %collective-permute-done.1), channel_id=1, source_target_pairs={{0,8},{1,9},{2,10},{3,11},{4,12},{5,13},{6,14},{7,15},{8,16},{9,17... | collective-permute-start | bytes 73736 | tf_op jit(solution)/shard_map/ppermute | solution.py:281
  30.8 9.6 %collective-permute-start.6 = (bf16[96,128]{1,0:T(8,128)(2,1)S(1)}, bf16[96,128]{1,0:T(8,128)(2,1)S(1)}, u32[]{:S(2)}, u32[]{:S(2)}) collective-permute-start(bf16[96,128]{1,0:T(8,128)(2,1)S(1)} %collective-permute-done.5), channel_id=1, source_target_pairs={{0,56},{1,57},{2,58},{3,59},{4,60},{5,61},{6,62},{7,63},{8,0},{9,1... | collective-permute-start | bytes 73736 | tf_op jit(solution)/shard_map/ppermute | solution.py:284
  35.0 4.8 %collective-permute-start.3 = (bf16[96,128]{1,0:T(8,128)(2,1)S(1)}, bf16[96,128]{1,0:T(8,128)(2,1)S(1)}, u32[]{:S(2)}, u32[]{:S(2)}) collective-permute-start(bf16[96,128]{1,0:T(8,128)(2,1)S(1)} %collective-permute-done.2), channel_id=1, source_target_pairs={{0,8},{1,9},{2,10},{3,11},{4,12},{5,13},{6,14},{7,15},{8,16},{9,17... | collective-permute-start | bytes 73736 | tf_op jit(solution)/shard_map/ppermute | solution.py:281
  46.1 2.6 %copy-start.12 = (s32[7]{0:T(128)}, s32[7]{0:T(128)S(1)}, u32[]{:S(2)}) copy-start(s32[7]{0:T(128)S(1)} %select_reduce_fusion.9) | copy-start | bytes 88
  47.8 9.3 %copy-start.8 = (pred[7,16]{1,0:T(8,128)(4,1)}, pred[7,16]{1,0:T(8,128)(4,1)S(1)}, u32[]{:S(2)}) copy-start(pred[7,16]{1,0:T(8,128)(4,1)S(1)} %copy.109) | copy-start | bytes 340
  48.2 9.0 %copy-start.7 = (s32[7,16]{1,0:T(8,128)}, s32[7,16]{1,0:T(8,128)S(1)}, u32[]{:S(2)}) copy-start(s32[7,16]{1,0:T(8,128)S(1)} %broadcast_add_fusion) | copy-start | bytes 1348
  48.8 50.5 %copy-start.3 = (bf16[16,128,256]{2,1,0:T(8,128)(2,1)}, bf16[16,128,256]{2,1,0:T(8,128)(2,1)S(1)}, u32[]{:S(2)}) copy-start(bf16[16,128,256]{2,1,0:T(8,128)(2,1)S(1)} %collective-permute-done.7.refs_2_) | copy-start | bytes 3145732
  48.8 47.9 %copy-start.4 = (bf16[16,128,256]{2,1,0:T(8,128)(2,1)}, bf16[16,128,256]{2,1,0:T(8,128)(2,1)S(1)}, u32[]{:S(2)}) copy-start(bf16[16,128,256]{2,1,0:T(8,128)(2,1)S(1)} %collective-permute-done.8.refs_3_) | copy-start | bytes 3145732
  48.8 7.6 %collective-permute-start.9 = (bf16[8,80,128]{2,1,0:T(8,128)(2,1)S(1)}, bf16[8,80,128]{2,1,0:T(8,128)(2,1)S(1)}, u32[]{:S(2)}, u32[]{:S(2)}) collective-permute-start(bf16[8,80,128]{2,1,0:T(8,128)(2,1)S(1)} %slice.48), channel_id=1, source_target_pairs={{0,2},{1,3},{2,4},{3,5},{4,6},{5,7},{6,0},{7,1},{8,10},{9,11},{10,... | collective-permute-start | bytes 491528 | tf_op jit(solution)/shard_map/ppermute | solution.py:295
  48.9 7.5 %collective-permute-start.10 = (bf16[8,80,128]{2,1,0:T(8,128)(2,1)S(1)}, bf16[8,80,128]{2,1,0:T(8,128)(2,1)S(1)}, u32[]{:S(2)}, u32[]{:S(2)}) collective-permute-start(bf16[8,80,128]{2,1,0:T(8,128)(2,1)S(1)} %slice.48), channel_id=1, source_target_pairs={{0,4},{1,5},{2,6},{3,7},{4,0},{5,1},{6,2},{7,3},{8,12},{9,13},{10,... | collective-permute-start | bytes 491528 | tf_op jit(solution)/shard_map/ppermute | solution.py:295
  51.4 5.6 %collective-permute-start.11 = (bf16[8,80,128]{2,1,0:T(8,128)(2,1)S(1)}, bf16[8,80,128]{2,1,0:T(8,128)(2,1)S(1)}, u32[]{:S(2)}, u32[]{:S(2)}) collective-permute-start(bf16[8,80,128]{2,1,0:T(8,128)(2,1)S(1)} %slice.48), channel_id=1, source_target_pairs={{0,6},{1,7},{2,0},{3,1},{4,2},{5,3},{6,4},{7,5},{8,14},{9,15},{10,... | collective-permute-start | bytes 491528 | tf_op jit(solution)/shard_map/ppermute | solution.py:295
  57.2 23.1 %collective-permute-start.13 = (bf16[32,80,128]{2,1,0:T(8,128)(2,1)S(1)}, bf16[32,80,128]{2,1,0:T(8,128)(2,1)S(1)}, u32[]{:S(2)}, u32[]{:S(2)}) collective-permute-start(bf16[32,80,128]{2,1,0:T(8,128)(2,1)S(1)} %bitcast.63), channel_id=1, source_target_pairs={{0,128},{64,192},{128,0},{192,64},{1,129},{65,193},{129,1},{193,65... | collective-permute-start | bytes 1966088 | tf_op jit(solution)/shard_map/ppermute | solution.py:297
  61.0 33.9 %collective-permute-start.14 = (bf16[16,128,256]{2,1,0:T(8,128)(2,1)}, bf16[16,128,256]{2,1,0:T(8,128)(2,1)}, u32[]{:S(2)}, u32[]{:S(2)}) collective-permute-start(bf16[16,128,256]{2,1,0:T(8,128)(2,1)} %bitcast.69), channel_id=1, source_target_pairs={{0,3},{1,2},{2,5},{3,4},{4,7},{5,6},{6,1},{7,0},{8,11},{9,10},{10,... | collective-permute-start | bytes 3145736 | tf_op jit(solution)/shard_map/ppermute | solution.py:293
  67.3 27.6 %collective-permute-start.15 = (bf16[16,128,256]{2,1,0:T(8,128)(2,1)}, bf16[16,128,256]{2,1,0:T(8,128)(2,1)}, u32[]{:S(2)}, u32[]{:S(2)}) collective-permute-start(bf16[16,128,256]{2,1,0:T(8,128)(2,1)} %bitcast.68), channel_id=1, source_target_pairs={{0,7},{1,6},{2,1},{3,0},{4,3},{5,2},{6,5},{7,4},{8,15},{9,14},{10,... | collective-permute-start | bytes 3145736 | tf_op jit(solution)/shard_map/ppermute | solution.py:293
  68.7 20.8 %collective-permute-start.12 = (bf16[32,80,128]{2,1,0:T(8,128)(2,1)S(1)}, bf16[32,80,128]{2,1,0:T(8,128)(2,1)}, u32[]{:S(2)}, u32[]{:S(2)}) collective-permute-start(bf16[32,80,128]{2,1,0:T(8,128)(2,1)S(1)} %bitcast.64), channel_id=1, source_target_pairs={{0,64},{64,128},{128,192},{192,0},{1,65},{65,129},{129,193},{193,1... | collective-permute-start | bytes 1966088 | tf_op jit(solution)/shard_map/ppermute | solution.py:297
  77.8 18.9 %collective-permute-start.16 = (bf16[32,80,128]{2,1,0:T(8,128)(2,1)S(1)}, bf16[32,80,128]{2,1,0:T(8,128)(2,1)S(1)}, u32[]{:S(2)}, u32[]{:S(2)}) collective-permute-start(bf16[32,80,128]{2,1,0:T(8,128)(2,1)S(1)} %bitcast.65), channel_id=1, source_target_pairs={{0,192},{64,0},{128,64},{192,128},{1,193},{65,1},{129,65},{193,129... | collective-permute-start | bytes 1966088 | tf_op jit(solution)/shard_map/ppermute | solution.py:297
  80.2 19.0 %collective-permute-start.17 = (bf16[32,80,128]{2,1,0:T(8,128)(2,1)S(1)}, bf16[32,80,128]{2,1,0:T(8,128)(2,1)S(1)}, u32[]{:S(2)}, u32[]{:S(2)}) collective-permute-start(bf16[32,80,128]{2,1,0:T(8,128)(2,1)S(1)} %bitcast.66), channel_id=1, source_target_pairs={{0,1},{1,0},{2,3},{3,2},{4,5},{5,4},{6,7},{7,6},{8,9},{9,8},{10,11... | collective-permute-start | bytes 1966088 | tf_op jit(solution)/shard_map/ppermute | solution.py:301
  89.6 9.7 %collective-permute-start.18 = (bf16[32,80,128]{2,1,0:T(8,128)(2,1)}, bf16[32,80,128]{2,1,0:T(8,128)(2,1)S(1)}, u32[]{:S(2)}, u32[]{:S(2)}) collective-permute-start(bf16[32,80,128]{2,1,0:T(8,128)(2,1)} %collective-permute-done.12), channel_id=1, source_target_pairs={{0,1},{1,0},{2,3},{3,2},{4,5},{5,4},{6,7},{7,6},{8,9},{9,8},{10,11... | collective-permute-start | bytes 1966088 | tf_op jit(solution)/shard_map/ppermute | solution.py:301
  94.8 18.6 %collective-permute-start.21 = (bf16[16,128,256]{2,1,0:T(8,128)(2,1)}, bf16[16,128,256]{2,1,0:T(8,128)(2,1)}, u32[]{:S(2)}, u32[]{:S(2)}) collective-permute-start(bf16[16,128,256]{2,1,0:T(8,128)(2,1)} %bitcast.33), channel_id=1, source_target_pairs={{0,1},{1,0},{2,3},{3,2},{4,5},{5,4},{6,7},{7,6},{8,9},{9,8},{10,11... | collective-permute-start | bytes 3145736 | tf_op jit(solution)/shard_map/ppermute | solution.py:293
  94.9 26.2 %collective-permute-start.22 = (bf16[16,128,256]{2,1,0:T(8,128)(2,1)}, bf16[16,128,256]{2,1,0:T(8,128)(2,1)}, u32[]{:S(2)}, u32[]{:S(2)}) collective-permute-start(bf16[16,128,256]{2,1,0:T(8,128)(2,1)} %bitcast.34), channel_id=1, source_target_pairs={{0,4},{1,5},{2,6},{3,7},{4,0},{5,1},{6,2},{7,3},{8,12},{9,13},{10,... | collective-permute-start | bytes 3145736 | tf_op jit(solution)/shard_map/ppermute | solution.py:293
  96.8 8.1 %copy-start.2 = (bf16[16,128,256]{2,1,0:T(8,128)(2,1)S(1)}, bf16[16,128,256]{2,1,0:T(8,128)(2,1)}, u32[]{:S(2)}) copy-start(bf16[16,128,256]{2,1,0:T(8,128)(2,1)} %grad_ref.1) | copy-start | bytes 3145732
  96.8 48.2 %collective-permute-start.29 = (bf16[16,128,256]{2,1,0:T(8,128)(2,1)}, bf16[16,128,256]{2,1,0:T(8,128)(2,1)}, u32[]{:S(2)}, u32[]{:S(2)}) collective-permute-start(bf16[16,128,256]{2,1,0:T(8,128)(2,1)} %bitcast.38), channel_id=1, source_target_pairs={{0,5},{1,4},{2,7},{3,6},{4,1},{5,0},{6,3},{7,2},{8,13},{9,12},{10,... | collective-permute-start | bytes 3145736 | tf_op jit(solution)/shard_map/ppermute | solution.py:293
  99.2 2.2 %collective-permute-start.19 = (bf16[32,80,128]{2,1,0:T(8,128)(2,1)S(1)}, bf16[32,80,128]{2,1,0:T(8,128)(2,1)S(1)}, u32[]{:S(2)}, u32[]{:S(2)}) collective-permute-start(bf16[32,80,128]{2,1,0:T(8,128)(2,1)S(1)} %collective-permute-done.13), channel_id=1, source_target_pairs={{0,1},{1,0},{2,3},{3,2},{4,5},{5,4},{6,7},{7,6},{8,9},{9,8},{10,11... | collective-permute-start | bytes 1966088 | tf_op jit(solution)/shard_map/ppermute | solution.py:301
  99.3 3.0 %collective-permute-start.20 = (bf16[32,80,128]{2,1,0:T(8,128)(2,1)S(1)}, bf16[32,80,128]{2,1,0:T(8,128)(2,1)S(1)}, u32[]{:S(2)}, u32[]{:S(2)}) collective-permute-start(bf16[32,80,128]{2,1,0:T(8,128)(2,1)S(1)} %collective-permute-done.16), channel_id=1, source_target_pairs={{0,1},{1,0},{2,3},{3,2},{4,5},{5,4},{6,7},{7,6},{8,9},{9,8},{10,11... | collective-permute-start | bytes 1966088 | tf_op jit(solution)/shard_map/ppermute | solution.py:301
  102.4 2.4 %copy-start = (bf16[256,80,128]{2,1,0:T(8,128)(2,1)}, bf16[256,80,128]{2,1,0:T(8,128)(2,1)S(1)}, u32[]{:S(2)}) copy-start(bf16[256,80,128]{2,1,0:T(8,128)(2,1)S(1)} %constant_dynamic-update-slice_fusion.8.weight_ref) | copy-start | bytes 15728644
  104.9 2.5 %copy-start.1 = (bf16[256,80,128]{2,1,0:T(8,128)(2,1)S(1)}, bf16[256,80,128]{2,1,0:T(8,128)(2,1)}, u32[]{:S(2)}) copy-start(bf16[256,80,128]{2,1,0:T(8,128)(2,1)} %copy-done) | copy-start | bytes 15728644
  127.0 21.3 %copy-start.11 = (bf16[4,96,96]{2,1,0:T(8,128)(2,1)S(1)}, bf16[4,96,96]{2,1,0:T(8,128)(2,1)}, u32[]{:S(2)}) copy-start(bf16[4,96,96]{2,1,0:T(8,128)(2,1)} %get-tuple-element.57) | copy-start | bytes 221188
  127.0 29.6 %copy-start.6 = (bf16[4,96,96]{2,1,0:T(8,128)(2,1)S(1)}, bf16[4,96,96]{2,1,0:T(8,128)(2,1)}, u32[]{:S(2)}) copy-start(bf16[4,96,96]{2,1,0:T(8,128)(2,1)} %get-tuple-element.51) | copy-start | bytes 221188
  127.0 21.3 %collective-permute-start.23 = (bf16[4,96,96]{2,1,0:T(8,128)(2,1)}, bf16[4,96,96]{2,1,0:T(8,128)(2,1)S(1)}, u32[]{:S(2)}, u32[]{:S(2)}) collective-permute-start(bf16[4,96,96]{2,1,0:T(8,128)(2,1)} %get-tuple-element.52), channel_id=1, source_target_pairs={{0,1},{1,0},{2,3},{3,2},{4,5},{5,4},{6,7},{7,6},{8,9},{9,8},{10,11... | collective-permute-start | bytes 221192 | tf_op jit(solution)/shard_map/ppermute | solution.py:336
  129.2 21.7 %collective-permute-start.24 = (bf16[4,96,96]{2,1,0:T(8,128)(2,1)}, bf16[4,96,96]{2,1,0:T(8,128)(2,1)S(1)}, u32[]{:S(2)}, u32[]{:S(2)}) collective-permute-start(bf16[4,96,96]{2,1,0:T(8,128)(2,1)} %get-tuple-element.53), channel_id=1, source_target_pairs={{0,6},{1,7},{2,0},{3,1},{4,2},{5,3},{6,4},{7,5},{8,14},{9,15},{10,... | collective-permute-start | bytes 221192 | tf_op jit(solution)/shard_map/ppermute | solution.py:336
  135.5 17.5 %collective-permute-start.25 = (bf16[4,96,96]{2,1,0:T(8,128)(2,1)}, bf16[4,96,96]{2,1,0:T(8,128)(2,1)S(1)}, u32[]{:S(2)}, u32[]{:S(2)}) collective-permute-start(bf16[4,96,96]{2,1,0:T(8,128)(2,1)} %get-tuple-element.54), channel_id=1, source_target_pairs={{0,2},{1,3},{2,4},{3,5},{4,6},{5,7},{6,0},{7,1},{8,10},{9,11},{10,... | collective-permute-start | bytes 221192 | tf_op jit(solution)/shard_map/ppermute | solution.py:336
  135.5 17.5 %collective-permute-start.26 = (bf16[4,96,96]{2,1,0:T(8,128)(2,1)}, bf16[4,96,96]{2,1,0:T(8,128)(2,1)S(1)}, u32[]{:S(2)}, u32[]{:S(2)}) collective-permute-start(bf16[4,96,96]{2,1,0:T(8,128)(2,1)} %get-tuple-element.55), channel_id=1, source_target_pairs={{0,7},{1,6},{2,1},{3,0},{4,3},{5,2},{6,5},{7,4},{8,15},{9,14},{10,... | collective-permute-start | bytes 221192 | tf_op jit(solution)/shard_map/ppermute | solution.py:336
  145.0 8.1 %collective-permute-start.27 = (bf16[4,96,96]{2,1,0:T(8,128)(2,1)}, bf16[4,96,96]{2,1,0:T(8,128)(2,1)S(1)}, u32[]{:S(2)}, u32[]{:S(2)}) collective-permute-start(bf16[4,96,96]{2,1,0:T(8,128)(2,1)} %get-tuple-element.56), channel_id=1, source_target_pairs={{0,3},{1,2},{2,5},{3,4},{4,7},{5,6},{6,1},{7,0},{8,11},{9,10},{10,... | collective-permute-start | bytes 221192 | tf_op jit(solution)/shard_map/ppermute | solution.py:336
  148.4 5.1 %collective-permute-start.28 = (bf16[4,96,96]{2,1,0:T(8,128)(2,1)S(1)}, bf16[4,96,96]{2,1,0:T(8,128)(2,1)S(1)}, u32[]{:S(2)}, u32[]{:S(2)}) collective-permute-start(bf16[4,96,96]{2,1,0:T(8,128)(2,1)S(1)} %copy-done.11), channel_id=1, source_target_pairs={{0,4},{1,5},{2,6},{3,7},{4,0},{5,1},{6,2},{7,3},{8,12},{9,13},{10,... | collective-permute-start | bytes 221192 | tf_op jit(solution)/shard_map/ppermute | solution.py:336
  150.9 5.8 %collective-permute-start.30 = (bf16[4,96,96]{2,1,0:T(8,128)(2,1)}, bf16[4,96,96]{2,1,0:T(8,128)(2,1)S(1)}, u32[]{:S(2)}, u32[]{:S(2)}) collective-permute-start(bf16[4,96,96]{2,1,0:T(8,128)(2,1)} %shard_map.70), channel_id=1, source_target_pairs={{0,5},{1,4},{2,7},{3,6},{4,1},{5,0},{6,3},{7,2},{8,13},{9,12},{10,... | collective-permute-start | bytes 221192 | tf_op jit(solution)/shard_map/ppermute | solution.py:336
  156.7 4.8 %collective-permute-start.31 = (bf16[4,96,96]{2,1,0:T(8,128)(2,1)S(1)}, bf16[4,96,96]{2,1,0:T(8,128)(2,1)S(1)}, u32[]{:S(2)}, u32[]{:S(2)}) collective-permute-start(bf16[4,96,96]{2,1,0:T(8,128)(2,1)S(1)} %add_convert_fusion), channel_id=1, source_target_pairs={{0,64},{64,128},{128,192},{192,0},{1,65},{65,129},{129,193},{193,1... | collective-permute-start | bytes 221192 | tf_op jit(solution)/shard_map/ppermute | solution.py:342
  157.9 5.1 %collective-permute-start.32 = (bf16[4,96,96]{2,1,0:T(8,128)(2,1)S(1)}, bf16[4,96,96]{2,1,0:T(8,128)(2,1)S(1)}, u32[]{:S(2)}, u32[]{:S(2)}) collective-permute-start(bf16[4,96,96]{2,1,0:T(8,128)(2,1)S(1)} %add_convert_fusion), channel_id=1, source_target_pairs={{0,128},{64,192},{128,0},{192,64},{1,129},{65,193},{129,1},{193,65... | collective-permute-start | bytes 221192 | tf_op jit(solution)/shard_map/ppermute | solution.py:342
  159.5 3.9 %collective-permute-start.33 = (bf16[4,96,96]{2,1,0:T(8,128)(2,1)S(1)}, bf16[4,96,96]{2,1,0:T(8,128)(2,1)S(1)}, u32[]{:S(2)}, u32[]{:S(2)}) collective-permute-start(bf16[4,96,96]{2,1,0:T(8,128)(2,1)S(1)} %add_convert_fusion), channel_id=1, source_target_pairs={{0,192},{64,0},{128,64},{192,128},{1,193},{65,1},{129,65},{193,129... | collective-permute-start | bytes 221192 | tf_op jit(solution)/shard_map/ppermute | solution.py:342
Sparse Core Ops, SparseCore 0:
  9.8 99.4 all-gather.1

commit v6 on v4

--- a/solution.py
+++ b/solution.py
@@ -298,6 +298,7 @@
     )
     quarters += [lax.ppermute(quarter, "ep", ep_perm(0, 0, 1)) for quarter in quarters]
     held = jnp.concatenate(quarters, 0)
+    held, chunks[6] = lax.optimization_barrier((held, chunks[6]))
     held = held.reshape(NC * NX * NY * NZ, PIECE, CHANNELS)
 
     from_z = (z - jnp.arange(NZ, dtype=jnp.int32)) % NZ

time: 173 us -> 167 us (0.965)
  local copies, waits for them, and re-layouts: 27.7 us -> 22.9 us
  waiting for transfers between devices: 50 us -> 46.5 us
    unnamed x36 -> x32, local copies, waits for them, and re-layouts: 10 us -> 5.19 us
    ppermute x7, waiting for transfers between devices: 21.5 us -> 18.6 us  [per_device(): lax.ppermute(part, 'ep', ep_perm(0, d, dc))]
    ppermute x3, starting transfers between devices: 3.19 us -> 5.16 us  [per_device(): lax.ppermute(total, 'rep', rep_perm(d)).astype(jnp.float32)]
  transfers between devices with their start and end apart: 35 -> 35, of which waited for: 12 -> 12; matrix products, arithmetic and copies ran while one was open for 17% -> 18% of each run, Pallas kernels for 10% -> 11%
where the time goes in v6:
time: 167 us; the launch traced here: 166 us
  starting transfers between devices  52.2 us (31%)
  waiting for transfers between devices  46.5 us (28%)
  local copies, waits for them, and re-layouts  22.9 us (14%)
  Pallas kernels  18.6 us (11%)
  between operations  18 us (11%)
  other arithmetic  7.82 us (5%)
    ppermute x7, waiting for transfers between devices, per_device(): lax.ppermute(part, 'ep', ep_perm(0, d, dc))  18.6 us
    pallas_call x2, Pallas kernels, weight_grads(): pl.pallas_call(functools.partial(weight_kernel, chunks), out_shape=[jax.S...  12.5 us
    ppermute x7, starting transfers between devices, per_device(): lax.ppermute(part, 'ep', ep_perm(0, d, dc))  10.9 us
    ppermute x7, starting transfers between devices, per_device(): part = lax.ppermute(part, 'ep', ep_perm(0, -d, dc))  10.9 us
    ppermute x3, starting transfers between devices, per_device(): down = lax.ppermute(down, 'ep', ep_perm(-1, 0, 0))  9.5 us
    ppermute x4, waiting for transfers between devices, per_device(): up = lax.ppermute(up, 'ep', ep_perm(1, 0, 0))  8.81 us
    dynamic_slice x2, local copies, waits for them, and re-layouts, sent(): lax.dynamic_slice(kept, (0, (y + d) % NY, c ^ dc, 0, 0, 0), (NZ, 1, 1, 2,...  8.66 us
    ppermute x3, waiting for transfers between devices, per_device(): lax.ppermute(held, 'rep', rep_perm(d))  8.63 us
  transfers between devices with their start and end apart: 35, of which 12 were waited for; matrix products, arithmetic and copies ran while one was open for 18% of the time, Pallas kernels for 11%

profile of v6, /device:TPU:1, one launch (start us, length us, event | category | flops | bytes accessed | tf_op | source)
XLA Modules:
  0.0 166.0 jit_solution(13903882768406418516)
XLA Ops:
  7.2 0.7 all-gather.2.cloned.1.call-update
  8.0 3.1 %constant_dynamic-slice_fusion.6 = (bf16[8,1,1,2,128,256]{5,4,3,2,1,0:T(8,128)(2,1)}, bf16[8,1,1,2,128,256]{5,4,3,2,1,0:T(8,128)(2,1)}) fusion(bf16[8,4,2,2,128,256]{5,4,3,2,1,0:T(8,128)(2,1)} %bitcast.58, s32[]{:T(128)S(6)} %select_n.250, s32[]{:T(128)S(6)} %select_n.248, s32[]{:T(128)S(6)} %select_n.247), kind=kLoop, calls=%fused_computation.72 | loop fusion | bytes 4194316 | tf_op jit(solution)/shard_map/dynamic_slice | solution.py:256
  12.0 2.5 %collective-permute-start = (bf16[96,128]{1,0:T(8,128)(2,1)S(1)}, bf16[96,128]{1,0:T(8,128)(2,1)S(1)}, u32[]{:S(2)}, u32[]{:S(2)}) collective-permute-start(bf16[96,128]{1,0:T(8,128)(2,1)S(1)} %pad_maximum_fusion.1), channel_id=1, source_target_pairs={{0,8},{1,9},{2,10},{3,11},{4,12},{5,13},{6,14},{7,15},{8,16},{9,17... | collective-permute-start | bytes 73736 | tf_op jit(solution)/shard_map/ppermute | solution.py:279
  14.6 4.0 %collective-permute-start.4 = (bf16[96,128]{1,0:T(8,128)(2,1)S(1)}, bf16[96,128]{1,0:T(8,128)(2,1)S(1)}, u32[]{:S(2)}, u32[]{:S(2)}) collective-permute-start(bf16[96,128]{1,0:T(8,128)(2,1)S(1)} %pad_maximum_fusion.1), channel_id=1, source_target_pairs={{0,56},{1,57},{2,58},{3,59},{4,60},{5,61},{6,62},{7,63},{8,0},{9,1... | collective-permute-start | bytes 73736 | tf_op jit(solution)/shard_map/ppermute | solution.py:282
  18.6 1.3 collective-permute-start.10
  19.9 1.4 collective-permute-start.11
  21.8 5.6 %constant_dynamic-slice_fusion = (bf16[8,1,1,2,128,256]{5,4,3,0,2,1:T(8,128)(2,1)}, bf16[8,1,1,2,128,256]{5,4,3,0,2,1:T(8,128)(2,1)}, bf16[8,1,1,2,128,256]{5,4,...) fusion(s32[]{:T(128)S(6)} %select_n.253, ...), kind=kLoop, calls=%fused_computation.66 | loop fusion | bytes 12582936 | tf_op jit(solution)/shard_map/dynamic_slice | solution.py:256
  28.3 2.7 %collective-permute-start.5 = (bf16[96,128]{1,0:T(8,128)(2,1)S(1)}, bf16[96,128]{1,0:T(8,128)(2,1)S(1)}, u32[]{:S(2)}, u32[]{:S(2)}) collective-permute-start(bf16[96,128]{1,0:T(8,128)(2,1)S(1)} %collective-permute-done.4), channel_id=1, source_target_pairs={{0,56},{1,57},{2,58},{3,59},{4,60},{5,61},{6,62},{7,63},{8,0},{9,1... | collective-permute-start | bytes 73736 | tf_op jit(solution)/shard_map/ppermute | solution.py:282
  31.0 2.0 %collective-permute-done.1 = bf16[96,128]{1,0:T(8,128)(2,1)S(1)} collective-permute-done((bf16[96,128]{1,0:T(8,128)(2,1)S(1)}, bf16[96,128]{1,0:T(8,128)(2,1)S(1)}, u32[]{:S(2)}, u32[]{:S(2)}) %collective-permute-start.1) | collective-permute-done | bytes 24608 | tf_op jit(solution)/shard_map/ppermute | solution.py:279
  33.0 2.7 %collective-permute-start.6 = (bf16[96,128]{1,0:T(8,128)(2,1)S(1)}, bf16[96,128]{1,0:T(8,128)(2,1)S(1)}, u32[]{:S(2)}, u32[]{:S(2)}) collective-permute-start(bf16[96,128]{1,0:T(8,128)(2,1)S(1)} %collective-permute-done.5), channel_id=1, source_target_pairs={{0,56},{1,57},{2,58},{3,59},{4,60},{5,61},{6,62},{7,63},{8,0},{9,1... | collective-permute-start | bytes 73736 | tf_op jit(solution)/shard_map/ppermute | solution.py:282
  35.8 2.0 %collective-permute-done.2 = bf16[96,128]{1,0:T(8,128)(2,1)S(1)} collective-permute-done((bf16[96,128]{1,0:T(8,128)(2,1)S(1)}, bf16[96,128]{1,0:T(8,128)(2,1)S(1)}, u32[]{:S(2)}, u32[]{:S(2)}) %collective-permute-start.2) | collective-permute-done | bytes 24608 | tf_op jit(solution)/shard_map/ppermute | solution.py:279
  37.8 4.8 %collective-permute-done.3 = bf16[96,128]{1,0:T(8,128)(2,1)S(1)} collective-permute-done((bf16[96,128]{1,0:T(8,128)(2,1)S(1)}, bf16[96,128]{1,0:T(8,128)(2,1)S(1)}, u32[]{:S(2)}, u32[]{:S(2)}) %collective-permute-start.3) | collective-permute-done | bytes 24608 | tf_op jit(solution)/shard_map/ppermute | solution.py:279
  42.7 2.6 %collective-permute-start.8 = (bf16[8,80,128]{2,1,0:T(8,128)(2,1)S(1)}, bf16[8,80,128]{2,1,0:T(8,128)(2,1)S(1)}, u32[]{:S(2)}, u32[]{:S(2)}) collective-permute-start(bf16[8,80,128]{2,1,0:T(8,128)(2,1)S(1)} %slice.48), channel_id=1, source_target_pairs={{0,4},{1,5},{2,6},{3,7},{4,0},{5,1},{6,2},{7,3},{8,12},{9,13},{10,... | collective-permute-start | bytes 491528 | tf_op jit(solution)/shard_map/ppermute | solution.py:292
  45.6 0.4 convert_reduce_fusion
  46.0 0.4 select_reduce_fusion.1
  46.9 4.8 %collective-permute-start.14 = (bf16[16,128,256]{2,1,0:T(8,128)(2,1)}, bf16[16,128,256]{2,1,0:T(8,128)(2,1)}, u32[]{:S(2)}, u32[]{:S(2)}) collective-permute-start(bf16[16,128,256]{2,1,0:T(8,128)(2,1)} %bitcast.14), channel_id=1, source_target_pairs={{0,3},{1,2},{2,5},{3,4},{4,7},{5,6},{6,1},{7,0},{8,11},{9,10},{10,... | collective-permute-start | bytes 3145736 | tf_op jit(solution)/shard_map/ppermute | solution.py:290
  51.9 1.2 convert_reduce_fusion.5
  53.4 2.4 %collective-permute-start.9 = (bf16[8,80,128]{2,1,0:T(8,128)(2,1)S(1)}, bf16[8,80,128]{2,1,0:T(8,128)(2,1)S(1)}, u32[]{:S(2)}, u32[]{:S(2)}) collective-permute-start(bf16[8,80,128]{2,1,0:T(8,128)(2,1)S(1)} %slice.48), channel_id=1, source_target_pairs={{0,6},{1,7},{2,0},{3,1},{4,2},{5,3},{6,4},{7,5},{8,14},{9,15},{10,... | collective-permute-start | bytes 491528 | tf_op jit(solution)/shard_map/ppermute | solution.py:292
  55.9 0.6 slice.41
  59.1 0.6 slice.53
  60.4 0.7 copy.118
  61.7 1.3 collective-permute-start.12
  63.1 0.5 fusion.16
  63.6 2.5 %collective-permute-start.13 = (bf16[32,80,128]{2,1,0:T(8,128)(2,1)S(1)}, bf16[32,80,128]{2,1,0:T(8,128)(2,1)}, u32[]{:S(2)}, u32[]{:S(2)}) collective-permute-start(bf16[32,80,128]{2,1,0:T(8,128)(2,1)S(1)} %bitcast.63), channel_id=1, source_target_pairs={{0,128},{64,192},{128,0},{192,64},{1,129},{65,193},{129,1},{193,65... | collective-permute-start | bytes 1966088 | tf_op jit(solution)/shard_map/ppermute | solution.py:295
  66.3 0.7 copy.123
  67.1 0.7 copy.120
  68.0 0.7 copy.122
  68.7 0.7 copy.121
  69.5 1.2 collective-permute-start.16
  70.6 5.3 %collective-permute-done.14.refs_4_ = bf16[16,128,256]{2,1,0:T(8,128)(2,1)} collective-permute-done((bf16[16,128,256]{2,1,0:T(8,128)(2,1)}, bf16[16,128,256]{2,1,0:T(8,128)(2,1)}, u32[]{:S(2)}, u32[]{:S(2)}) %collective-permute-start.14) | collective-permute-done | bytes 1048608 | tf_op jit(solution)/shard_map/ppermute | solution.py:290
  75.9 1.4 collective-permute-start.17
  77.4 1.6 collective-permute-done.12
  79.0 1.1 collective-permute-start.18
  80.4 0.6 select_reduce_fusion.6.gate_of
  81.1 1.4 select_reduce_fusion.2.gate_of
  82.5 3.2 %collective-permute-done.15.refs_5_ = bf16[16,128,256]{2,1,0:T(8,128)(2,1)} collective-permute-done((bf16[16,128,256]{2,1,0:T(8,128)(2,1)}, bf16[16,128,256]{2,1,0:T(8,128)(2,1)}, u32[]{:S(2)}, u32[]{:S(2)}) %collective-permute-start.15) | collective-permute-done | bytes 1048608 | tf_op jit(solution)/shard_map/ppermute | solution.py:290
  85.7 1.3 collective-permute-start.21
  87.0 7.1 %collective-permute-done.13 = bf16[32,80,128]{2,1,0:T(8,128)(2,1)} collective-permute-done((bf16[32,80,128]{2,1,0:T(8,128)(2,1)S(1)}, bf16[32,80,128]{2,1,0:T(8,128)(2,1)}, u32[]{:S(2)}, u32[]{:S(2)}) %collective-permute-start.13) | collective-permute-done | bytes 655392 | tf_op jit(solution)/shard_map/ppermute | solution.py:295
  94.0 1.2 collective-permute-start.22
  95.2 0.7 pad_add_fusion.2.plan
  96.0 0.8 collective-permute-start.29
  96.8 0.5 collective-permute-start.19
  97.6 1.2 constant_dynamic-update-slice_fusion.13
  98.7 1.2 constant_dynamic-update-slice_fusion.12
  99.9 1.2 constant_dynamic-update-slice_fusion.11
  101.1 1.2 constant_dynamic-update-slice_fusion.10
  102.5 10.1 %collective-permute-done.21.refs_6_ = bf16[16,128,256]{2,1,0:T(8,128)(2,1)} collective-permute-done((bf16[16,128,256]{2,1,0:T(8,128)(2,1)}, bf16[16,128,256]{2,1,0:T(8,128)(2,1)}, u32[]{:S(2)}, u32[]{:S(2)}) %collective-permute-start.21) | collective-permute-done | bytes 1048608 | tf_op jit(solution)/shard_map/ppermute | solution.py:290
  112.6 6.1 %shard_map.68 = bf16[16,128,256]{2,1,0:T(8,128)(2,1)} custom-call(s32[128]{0:T(128)S(1)} %add.346.place_ref, f32[32]{0:T(128)S(1)} %reshape.729.gate_ref, bf16[16,128,256]{2,1,0:T(8,128)(2,1)S(1)} %copy-done, bf16[256,80,128]{2,1,0:T(8,128)(2,1)S(1)} %constant_dynamic-update-slice_fusion.8.weight_ref), custom_call_target="tpu_custom_call" | custom-call | flops 1 | bytes 1 | tf_op jit(solution)/shard_map/pallas_call | solution.py:76
  118.8 9.2 %shard_map.69 = (bf16[4,96,96]{2,1,0:T(8,128)(2,1)}, bf16[4,96,96]{2,1,0:T(8,128)(2,1)}, bf16[4,96,96]{2,1,0:T(8,128)(2,1)}, bf16[4,96,96]{2,1,0:T(8,128)(2,1)},...) custom-call(s32[291]{0:T(512)} %pad_add_fusion.2.plan, ...), custom_call_target="tpu_custom_call" | custom-call | flops 1 | bytes 1 | tf_op jit(solution)/shard_map/pallas_call | solution.py:221
  128.1 3.3 %collective-permute-start.24 = (bf16[4,96,96]{2,1,0:T(8,128)(2,1)}, bf16[4,96,96]{2,1,0:T(8,128)(2,1)S(1)}, u32[]{:S(2)}, u32[]{:S(2)}) collective-permute-start(bf16[4,96,96]{2,1,0:T(8,128)(2,1)} %get-tuple-element.56), channel_id=1, source_target_pairs={{0,6},{1,7},{2,0},{3,1},{4,2},{5,3},{6,4},{7,5},{8,14},{9,15},{10,... | collective-permute-start | bytes 221192 | tf_op jit(solution)/shard_map/ppermute | solution.py:335
  131.4 0.7 pad_add_fusion.3.plan
  132.0 3.4 %collective-permute-start.26 = (bf16[4,96,96]{2,1,0:T(8,128)(2,1)}, bf16[4,96,96]{2,1,0:T(8,128)(2,1)S(1)}, u32[]{:S(2)}, u32[]{:S(2)}) collective-permute-start(bf16[4,96,96]{2,1,0:T(8,128)(2,1)} %get-tuple-element.58), channel_id=1, source_target_pairs={{0,7},{1,6},{2,1},{3,0},{4,3},{5,2},{6,5},{7,4},{8,15},{9,14},{10,... | collective-permute-start | bytes 221192 | tf_op jit(solution)/shard_map/ppermute | solution.py:335
  135.4 0.5 collective-permute-start.27
  135.9 3.3 %shard_map.70 = bf16[4,96,96]{2,1,0:T(8,128)(2,1)} custom-call(s32[51]{0:T(128)} %pad_add_fusion.3.plan, f32[20]{0:T(128)} %select_reduce_fusion.6.gate_of, bf16[128,128,256]{2,1,0:T(8,128)(2,1)} %all-gather.2.cloned.1.call-done.grads, bf16[16,128,256]{2,1,0:T(8,128)(2,1)} %collective-permute-done.29.refs_0_), custom_call_target="tpu_custom_call" | custom-call | flops 1 | bytes 1 | tf_op jit(solution)/shard_map/pallas_call | solution.py:221
  139.2 3.7 %collective-permute-start.28 = (bf16[4,96,96]{2,1,0:T(8,128)(2,1)S(1)}, bf16[4,96,96]{2,1,0:T(8,128)(2,1)S(1)}, u32[]{:S(2)}, u32[]{:S(2)}) collective-permute-start(bf16[4,96,96]{2,1,0:T(8,128)(2,1)S(1)} %copy-done.7), channel_id=1, source_target_pairs={{0,4},{1,5},{2,6},{3,7},{4,0},{5,1},{6,2},{7,3},{8,12},{9,13},{10,... | collective-permute-start | bytes 221192 | tf_op jit(solution)/shard_map/ppermute | solution.py:335
  142.9 3.3 %collective-permute-done.28 = bf16[4,96,96]{2,1,0:T(8,128)(2,1)S(1)} collective-permute-done((bf16[4,96,96]{2,1,0:T(8,128)(2,1)S(1)}, bf16[4,96,96]{2,1,0:T(8,128)(2,1)S(1)}, u32[]{:S(2)}, u32[]{:S(2)}) %collective-permute-start.28) | collective-permute-done | bytes 73760 | tf_op jit(solution)/shard_map/ppermute | solution.py:335
  146.2 3.0 %collective-permute-done.30 = bf16[4,96,96]{2,1,0:T(8,128)(2,1)S(1)} collective-permute-done((bf16[4,96,96]{2,1,0:T(8,128)(2,1)}, bf16[4,96,96]{2,1,0:T(8,128)(2,1)S(1)}, u32[]{:S(2)}, u32[]{:S(2)}) %collective-permute-start.30) | collective-permute-done | bytes 73760 | tf_op jit(solution)/shard_map/ppermute | solution.py:335
  149.3 1.3 collective-permute-start.31
  150.6 2.6 %collective-permute-start.32 = (bf16[4,96,96]{2,1,0:T(8,128)(2,1)S(1)}, bf16[4,96,96]{2,1,0:T(8,128)(2,1)S(1)}, u32[]{:S(2)}, u32[]{:S(2)}) collective-permute-start(bf16[4,96,96]{2,1,0:T(8,128)(2,1)S(1)} %add_convert_fusion), channel_id=1, source_target_pairs={{0,128},{64,192},{128,0},{192,64},{1,129},{65,193},{129,1},{193,65... | collective-permute-start | bytes 221192 | tf_op jit(solution)/shard_map/ppermute | solution.py:341
  153.2 1.2 collective-permute-start.33
  154.5 0.3 collective-permute-done.31
  154.8 3.1 %collective-permute-done.32 = bf16[4,96,96]{2,1,0:T(8,128)(2,1)S(1)} collective-permute-done((bf16[4,96,96]{2,1,0:T(8,128)(2,1)S(1)}, bf16[4,96,96]{2,1,0:T(8,128)(2,1)S(1)}, u32[]{:S(2)}, u32[]{:S(2)}) %collective-permute-start.32) | collective-permute-done | bytes 73760 | tf_op jit(solution)/shard_map/ppermute | solution.py:341
  157.9 0.3 reshape.727
  158.2 0.9 copy.124
  (129 shorter events, 6.1 us)
Async XLA Ops:
  7.2 3.9 %copy-start.3 = (bf16[1,9,4,32,32]{4,3,2,1,0:T(8,128)(2,1)S(1)}, bf16[1,9,4,32,32]{4,3,2,1,0:T(8,128)(2,1)}, u32[]{:S(2)}) copy-start(bf16[1,9,4,32,32]{4,3,2,1,0:T(8,128)(2,1)} %param.9) | copy-start | bytes 221188
  7.2 4.3 %copy-start.6 = (s32[16,2]{0,1:T(2,128)S(1)}, s32[16,2]{0,1:T(2,128)}, u32[]{:S(2)}) copy-start(s32[16,2]{0,1:T(2,128)} %param.6) | copy-start | bytes 388
  7.2 4.5 %copy-start.5 = (bf16[16,2]{0,1:T(2,128)(2,1)S(1)}, bf16[16,2]{0,1:T(2,128)(2,1)}, u32[]{:S(2)}) copy-start(bf16[16,2]{0,1:T(2,128)(2,1)} %param.7) | copy-start | bytes 196
  7.2 111.6 %all-gather.2.cloned.1.call-start = ((), (), s32[]{:S(2)}) async-start(), calls=%async_computation | async-start | bytes 9437184 | tf_op jit(solution)/shard_map/all_gather | solution.py:250
  12.0 16.1 %collective-permute-start = (bf16[96,128]{1,0:T(8,128)(2,1)S(1)}, bf16[96,128]{1,0:T(8,128)(2,1)S(1)}, u32[]{:S(2)}, u32[]{:S(2)}) collective-permute-start(bf16[96,128]{1,0:T(8,128)(2,1)S(1)} %pad_maximum_fusion.1), channel_id=1, source_target_pairs={{0,8},{1,9},{2,10},{3,11},{4,12},{5,13},{6,14},{7,15},{8,16},{9,17... | collective-permute-start | bytes 73736 | tf_op jit(solution)/shard_map/ppermute | solution.py:279
  14.6 13.7 %collective-permute-start.4 = (bf16[96,128]{1,0:T(8,128)(2,1)S(1)}, bf16[96,128]{1,0:T(8,128)(2,1)S(1)}, u32[]{:S(2)}, u32[]{:S(2)}) collective-permute-start(bf16[96,128]{1,0:T(8,128)(2,1)S(1)} %pad_maximum_fusion.1), channel_id=1, source_target_pairs={{0,56},{1,57},{2,58},{3,59},{4,60},{5,61},{6,62},{7,63},{8,0},{9,1... | collective-permute-start | bytes 73736 | tf_op jit(solution)/shard_map/ppermute | solution.py:282
  18.6 43.0 %collective-permute-start.10 = (bf16[16,128,256]{2,1,0:T(8,128)(2,1)}, bf16[16,128,256]{2,1,0:T(8,128)(2,1)S(1)}, u32[]{:S(2)}, u32[]{:S(2)}) collective-permute-start(bf16[16,128,256]{2,1,0:T(8,128)(2,1)} %bitcast.1), channel_id=1, source_target_pairs={{0,2},{1,3},{2,4},{3,5},{4,6},{5,7},{6,0},{7,1},{8,10},{9,11},{10,... | collective-permute-start | bytes 3145736 | tf_op jit(solution)/shard_map/ppermute | solution.py:290
  19.9 41.8 %collective-permute-start.11 = (bf16[16,128,256]{2,1,0:T(8,128)(2,1)}, bf16[16,128,256]{2,1,0:T(8,128)(2,1)S(1)}, u32[]{:S(2)}, u32[]{:S(2)}) collective-permute-start(bf16[16,128,256]{2,1,0:T(8,128)(2,1)} %bitcast.2), channel_id=1, source_target_pairs={{0,6},{1,7},{2,0},{3,1},{4,2},{5,3},{6,4},{7,5},{8,14},{9,15},{10,... | collective-permute-start | bytes 3145736 | tf_op jit(solution)/shard_map/ppermute | solution.py:290
  28.1 4.9 %collective-permute-start.1 = (bf16[96,128]{1,0:T(8,128)(2,1)S(1)}, bf16[96,128]{1,0:T(8,128)(2,1)S(1)}, u32[]{:S(2)}, u32[]{:S(2)}) collective-permute-start(bf16[96,128]{1,0:T(8,128)(2,1)S(1)} %collective-permute-done), channel_id=1, source_target_pairs={{0,8},{1,9},{2,10},{3,11},{4,12},{5,13},{6,14},{7,15},{8,16},{9,17... | collective-permute-start | bytes 73736 | tf_op jit(solution)/shard_map/ppermute | solution.py:279
  28.3 4.8 %collective-permute-start.5 = (bf16[96,128]{1,0:T(8,128)(2,1)S(1)}, bf16[96,128]{1,0:T(8,128)(2,1)S(1)}, u32[]{:S(2)}, u32[]{:S(2)}) collective-permute-start(bf16[96,128]{1,0:T(8,128)(2,1)S(1)} %collective-permute-done.4), channel_id=1, source_target_pairs={{0,56},{1,57},{2,58},{3,59},{4,60},{5,61},{6,62},{7,63},{8,0},{9,1... | collective-permute-start | bytes 73736 | tf_op jit(solution)/shard_map/ppermute | solution.py:282
  33.0 4.8 %collective-permute-start.2 = (bf16[96,128]{1,0:T(8,128)(2,1)S(1)}, bf16[96,128]{1,0:T(8,128)(2,1)S(1)}, u32[]{:S(2)}, u32[]{:S(2)}) collective-permute-start(bf16[96,128]{1,0:T(8,128)(2,1)S(1)} %collective-permute-done.1), channel_id=1, source_target_pairs={{0,8},{1,9},{2,10},{3,11},{4,12},{5,13},{6,14},{7,15},{8,16},{9,17... | collective-permute-start | bytes 73736 | tf_op jit(solution)/shard_map/ppermute | solution.py:279
  33.0 9.6 %collective-permute-start.6 = (bf16[96,128]{1,0:T(8,128)(2,1)S(1)}, bf16[96,128]{1,0:T(8,128)(2,1)S(1)}, u32[]{:S(2)}, u32[]{:S(2)}) collective-permute-start(bf16[96,128]{1,0:T(8,128)(2,1)S(1)} %collective-permute-done.5), channel_id=1, source_target_pairs={{0,56},{1,57},{2,58},{3,59},{4,60},{5,61},{6,62},{7,63},{8,0},{9,1... | collective-permute-start | bytes 73736 | tf_op jit(solution)/shard_map/ppermute | solution.py:282
  37.8 4.8 %collective-permute-start.3 = (bf16[96,128]{1,0:T(8,128)(2,1)S(1)}, bf16[96,128]{1,0:T(8,128)(2,1)S(1)}, u32[]{:S(2)}, u32[]{:S(2)}) collective-permute-start(bf16[96,128]{1,0:T(8,128)(2,1)S(1)} %collective-permute-done.2), channel_id=1, source_target_pairs={{0,8},{1,9},{2,10},{3,11},{4,12},{5,13},{6,14},{7,15},{8,16},{9,17... | collective-permute-start | bytes 73736 | tf_op jit(solution)/shard_map/ppermute | solution.py:279
  42.6 10.8 %collective-permute-start.7 = (bf16[8,80,128]{2,1,0:T(8,128)(2,1)S(1)}, bf16[8,80,128]{2,1,0:T(8,128)(2,1)S(1)}, u32[]{:S(2)}, u32[]{:S(2)}) collective-permute-start(bf16[8,80,128]{2,1,0:T(8,128)(2,1)S(1)} %slice.48), channel_id=1, source_target_pairs={{0,2},{1,3},{2,4},{3,5},{4,6},{5,7},{6,0},{7,1},{8,10},{9,11},{10,... | collective-permute-start | bytes 491528 | tf_op jit(solution)/shard_map/ppermute | solution.py:292
  42.7 18.7 %collective-permute-start.8 = (bf16[8,80,128]{2,1,0:T(8,128)(2,1)S(1)}, bf16[8,80,128]{2,1,0:T(8,128)(2,1)S(1)}, u32[]{:S(2)}, u32[]{:S(2)}) collective-permute-start(bf16[8,80,128]{2,1,0:T(8,128)(2,1)S(1)} %slice.48), channel_id=1, source_target_pairs={{0,4},{1,5},{2,6},{3,7},{4,0},{5,1},{6,2},{7,3},{8,12},{9,13},{10,... | collective-permute-start | bytes 491528 | tf_op jit(solution)/shard_map/ppermute | solution.py:292
  46.9 29.0 %collective-permute-start.14 = (bf16[16,128,256]{2,1,0:T(8,128)(2,1)}, bf16[16,128,256]{2,1,0:T(8,128)(2,1)}, u32[]{:S(2)}, u32[]{:S(2)}) collective-permute-start(bf16[16,128,256]{2,1,0:T(8,128)(2,1)} %bitcast.14), channel_id=1, source_target_pairs={{0,3},{1,2},{2,5},{3,4},{4,7},{5,6},{6,1},{7,0},{8,11},{9,10},{10,... | collective-permute-start | bytes 3145736 | tf_op jit(solution)/shard_map/ppermute | solution.py:290
  53.4 8.1 %collective-permute-start.9 = (bf16[8,80,128]{2,1,0:T(8,128)(2,1)S(1)}, bf16[8,80,128]{2,1,0:T(8,128)(2,1)S(1)}, u32[]{:S(2)}, u32[]{:S(2)}) collective-permute-start(bf16[8,80,128]{2,1,0:T(8,128)(2,1)S(1)} %slice.48), channel_id=1, source_target_pairs={{0,6},{1,7},{2,0},{3,1},{4,2},{5,3},{6,4},{7,5},{8,14},{9,15},{10,... | collective-permute-start | bytes 491528 | tf_op jit(solution)/shard_map/ppermute | solution.py:292
  61.4 24.3 %collective-permute-start.15 = (bf16[16,128,256]{2,1,0:T(8,128)(2,1)}, bf16[16,128,256]{2,1,0:T(8,128)(2,1)}, u32[]{:S(2)}, u32[]{:S(2)}) collective-permute-start(bf16[16,128,256]{2,1,0:T(8,128)(2,1)} %bitcast.15), channel_id=1, source_target_pairs={{0,7},{1,6},{2,1},{3,0},{4,3},{5,2},{6,5},{7,4},{8,15},{9,14},{10,... | collective-permute-start | bytes 3145736 | tf_op jit(solution)/shard_map/ppermute | solution.py:290
  61.6 40.9 %copy-start.1 = (bf16[16,128,256]{2,1,0:T(8,128)(2,1)}, bf16[16,128,256]{2,1,0:T(8,128)(2,1)S(1)}, u32[]{:S(2)}) copy-start(bf16[16,128,256]{2,1,0:T(8,128)(2,1)S(1)} %collective-permute-done.10.refs_2_) | copy-start | bytes 3145732
  61.6 40.9 %copy-start.2 = (bf16[16,128,256]{2,1,0:T(8,128)(2,1)}, bf16[16,128,256]{2,1,0:T(8,128)(2,1)S(1)}, u32[]{:S(2)}) copy-start(bf16[16,128,256]{2,1,0:T(8,128)(2,1)S(1)} %collective-permute-done.11.refs_3_) | copy-start | bytes 3145732
  61.7 17.3 %collective-permute-start.12 = (bf16[32,80,128]{2,1,0:T(8,128)(2,1)S(1)}, bf16[32,80,128]{2,1,0:T(8,128)(2,1)S(1)}, u32[]{:S(2)}, u32[]{:S(2)}) collective-permute-start(bf16[32,80,128]{2,1,0:T(8,128)(2,1)S(1)} %bitcast.62), channel_id=1, source_target_pairs={{0,64},{64,128},{128,192},{192,0},{1,65},{65,129},{129,193},{193,1... | collective-permute-start | bytes 1966088 | tf_op jit(solution)/shard_map/ppermute | solution.py:295
  63.6 30.4 %collective-permute-start.13 = (bf16[32,80,128]{2,1,0:T(8,128)(2,1)S(1)}, bf16[32,80,128]{2,1,0:T(8,128)(2,1)}, u32[]{:S(2)}, u32[]{:S(2)}) collective-permute-start(bf16[32,80,128]{2,1,0:T(8,128)(2,1)S(1)} %bitcast.63), channel_id=1, source_target_pairs={{0,128},{64,192},{128,0},{192,64},{1,129},{65,193},{129,1},{193,65... | collective-permute-start | bytes 1966088 | tf_op jit(solution)/shard_map/ppermute | solution.py:295
  69.5 26.5 %collective-permute-start.16 = (bf16[32,80,128]{2,1,0:T(8,128)(2,1)S(1)}, bf16[32,80,128]{2,1,0:T(8,128)(2,1)}, u32[]{:S(2)}, u32[]{:S(2)}) collective-permute-start(bf16[32,80,128]{2,1,0:T(8,128)(2,1)S(1)} %bitcast.64), channel_id=1, source_target_pairs={{0,192},{64,0},{128,64},{192,128},{1,193},{65,1},{129,65},{193,129... | collective-permute-start | bytes 1966088 | tf_op jit(solution)/shard_map/ppermute | solution.py:295
  75.9 20.9 %collective-permute-start.17 = (bf16[32,80,128]{2,1,0:T(8,128)(2,1)S(1)}, bf16[32,80,128]{2,1,0:T(8,128)(2,1)}, u32[]{:S(2)}, u32[]{:S(2)}) collective-permute-start(bf16[32,80,128]{2,1,0:T(8,128)(2,1)S(1)} %bitcast.65), channel_id=1, source_target_pairs={{0,1},{1,0},{2,3},{3,2},{4,5},{5,4},{6,7},{7,6},{8,9},{9,8},{10,11... | collective-permute-start | bytes 1966088 | tf_op jit(solution)/shard_map/ppermute | solution.py:299
  79.0 18.4 %collective-permute-start.18 = (bf16[32,80,128]{2,1,0:T(8,128)(2,1)S(1)}, bf16[32,80,128]{2,1,0:T(8,128)(2,1)}, u32[]{:S(2)}, u32[]{:S(2)}) collective-permute-start(bf16[32,80,128]{2,1,0:T(8,128)(2,1)S(1)} %collective-permute-done.12), channel_id=1, source_target_pairs={{0,1},{1,0},{2,3},{3,2},{4,5},{5,4},{6,7},{7,6},{8,9},{9,8},{10,11... | collective-permute-start | bytes 1966088 | tf_op jit(solution)/shard_map/ppermute | solution.py:299
  85.7 26.9 %collective-permute-start.21 = (bf16[16,128,256]{2,1,0:T(8,128)(2,1)}, bf16[16,128,256]{2,1,0:T(8,128)(2,1)}, u32[]{:S(2)}, u32[]{:S(2)}) collective-permute-start(bf16[16,128,256]{2,1,0:T(8,128)(2,1)} %bitcast.69), channel_id=1, source_target_pairs={{0,4},{1,5},{2,6},{3,7},{4,0},{5,1},{6,2},{7,3},{8,12},{9,13},{10,... | collective-permute-start | bytes 3145736 | tf_op jit(solution)/shard_map/ppermute | solution.py:290
  94.0 24.7 %collective-permute-start.22 = (bf16[16,128,256]{2,1,0:T(8,128)(2,1)}, bf16[16,128,256]{2,1,0:T(8,128)(2,1)}, u32[]{:S(2)}, u32[]{:S(2)}) collective-permute-start(bf16[16,128,256]{2,1,0:T(8,128)(2,1)} %bitcast.68), channel_id=1, source_target_pairs={{0,1},{1,0},{2,3},{3,2},{4,5},{5,4},{6,7},{7,6},{8,9},{9,8},{10,11... | collective-permute-start | bytes 3145736 | tf_op jit(solution)/shard_map/ppermute | solution.py:290
  96.0 16.7 %copy-start = (bf16[16,128,256]{2,1,0:T(8,128)(2,1)S(1)}, bf16[16,128,256]{2,1,0:T(8,128)(2,1)}, u32[]{:S(2)}) copy-start(bf16[16,128,256]{2,1,0:T(8,128)(2,1)} %grad_ref.1) | copy-start | bytes 3145732
  96.0 39.5 %collective-permute-start.29 = (bf16[16,128,256]{2,1,0:T(8,128)(2,1)}, bf16[16,128,256]{2,1,0:T(8,128)(2,1)}, u32[]{:S(2)}, u32[]{:S(2)}) collective-permute-start(bf16[16,128,256]{2,1,0:T(8,128)(2,1)} %bitcast.67), channel_id=1, source_target_pairs={{0,5},{1,4},{2,7},{3,6},{4,1},{5,0},{6,3},{7,2},{8,13},{9,12},{10,... | collective-permute-start | bytes 3145736 | tf_op jit(solution)/shard_map/ppermute | solution.py:290
  96.8 5.5 %collective-permute-start.19 = (bf16[32,80,128]{2,1,0:T(8,128)(2,1)}, bf16[32,80,128]{2,1,0:T(8,128)(2,1)S(1)}, u32[]{:S(2)}, u32[]{:S(2)}) collective-permute-start(bf16[32,80,128]{2,1,0:T(8,128)(2,1)} %collective-permute-done.13), channel_id=1, source_target_pairs={{0,1},{1,0},{2,3},{3,2},{4,5},{5,4},{6,7},{7,6},{8,9},{9,8},{10,11... | collective-permute-start | bytes 1966088 | tf_op jit(solution)/shard_map/ppermute | solution.py:299
  97.4 5.0 %collective-permute-start.20 = (bf16[32,80,128]{2,1,0:T(8,128)(2,1)}, bf16[32,80,128]{2,1,0:T(8,128)(2,1)S(1)}, u32[]{:S(2)}, u32[]{:S(2)}) collective-permute-start(bf16[32,80,128]{2,1,0:T(8,128)(2,1)} %collective-permute-done.16), channel_id=1, source_target_pairs={{0,1},{1,0},{2,3},{3,2},{4,5},{5,4},{6,7},{7,6},{8,9},{9,8},{10,11... | collective-permute-start | bytes 1966088 | tf_op jit(solution)/shard_map/ppermute | solution.py:299
  128.0 11.3 %copy-start.7 = (bf16[4,96,96]{2,1,0:T(8,128)(2,1)S(1)}, bf16[4,96,96]{2,1,0:T(8,128)(2,1)}, u32[]{:S(2)}) copy-start(bf16[4,96,96]{2,1,0:T(8,128)(2,1)} %get-tuple-element.60) | copy-start | bytes 221188
  128.0 21.2 %copy-start.4 = (bf16[4,96,96]{2,1,0:T(8,128)(2,1)S(1)}, bf16[4,96,96]{2,1,0:T(8,128)(2,1)}, u32[]{:S(2)}) copy-start(bf16[4,96,96]{2,1,0:T(8,128)(2,1)} %get-tuple-element.54) | copy-start | bytes 221188
  128.0 11.2 %collective-permute-start.23 = (bf16[4,96,96]{2,1,0:T(8,128)(2,1)}, bf16[4,96,96]{2,1,0:T(8,128)(2,1)S(1)}, u32[]{:S(2)}, u32[]{:S(2)}) collective-permute-start(bf16[4,96,96]{2,1,0:T(8,128)(2,1)} %get-tuple-element.55), channel_id=1, source_target_pairs={{0,1},{1,0},{2,3},{3,2},{4,5},{5,4},{6,7},{7,6},{8,9},{9,8},{10,11... | collective-permute-start | bytes 221192 | tf_op jit(solution)/shard_map/ppermute | solution.py:335
  128.1 14.8 %collective-permute-start.24 = (bf16[4,96,96]{2,1,0:T(8,128)(2,1)}, bf16[4,96,96]{2,1,0:T(8,128)(2,1)S(1)}, u32[]{:S(2)}, u32[]{:S(2)}) collective-permute-start(bf16[4,96,96]{2,1,0:T(8,128)(2,1)} %get-tuple-element.56), channel_id=1, source_target_pairs={{0,6},{1,7},{2,0},{3,1},{4,2},{5,3},{6,4},{7,5},{8,14},{9,15},{10,... | collective-permute-start | bytes 221192 | tf_op jit(solution)/shard_map/ppermute | solution.py:335
  132.0 10.9 %collective-permute-start.25 = (bf16[4,96,96]{2,1,0:T(8,128)(2,1)}, bf16[4,96,96]{2,1,0:T(8,128)(2,1)S(1)}, u32[]{:S(2)}, u32[]{:S(2)}) collective-permute-start(bf16[4,96,96]{2,1,0:T(8,128)(2,1)} %get-tuple-element.57), channel_id=1, source_target_pairs={{0,2},{1,3},{2,4},{3,5},{4,6},{5,7},{6,0},{7,1},{8,10},{9,11},{10,... | collective-permute-start | bytes 221192 | tf_op jit(solution)/shard_map/ppermute | solution.py:335
  132.0 10.9 %collective-permute-start.26 = (bf16[4,96,96]{2,1,0:T(8,128)(2,1)}, bf16[4,96,96]{2,1,0:T(8,128)(2,1)S(1)}, u32[]{:S(2)}, u32[]{:S(2)}) collective-permute-start(bf16[4,96,96]{2,1,0:T(8,128)(2,1)} %get-tuple-element.58), channel_id=1, source_target_pairs={{0,7},{1,6},{2,1},{3,0},{4,3},{5,2},{6,5},{7,4},{8,15},{9,14},{10,... | collective-permute-start | bytes 221192 | tf_op jit(solution)/shard_map/ppermute | solution.py:335
  135.4 7.5 %collective-permute-start.27 = (bf16[4,96,96]{2,1,0:T(8,128)(2,1)}, bf16[4,96,96]{2,1,0:T(8,128)(2,1)S(1)}, u32[]{:S(2)}, u32[]{:S(2)}) collective-permute-start(bf16[4,96,96]{2,1,0:T(8,128)(2,1)} %get-tuple-element.59), channel_id=1, source_target_pairs={{0,3},{1,2},{2,5},{3,4},{4,7},{5,6},{6,1},{7,0},{8,11},{9,10},{10,... | collective-permute-start | bytes 221192 | tf_op jit(solution)/shard_map/ppermute | solution.py:335
  139.2 7.0 %collective-permute-start.28 = (bf16[4,96,96]{2,1,0:T(8,128)(2,1)S(1)}, bf16[4,96,96]{2,1,0:T(8,128)(2,1)S(1)}, u32[]{:S(2)}, u32[]{:S(2)}) collective-permute-start(bf16[4,96,96]{2,1,0:T(8,128)(2,1)S(1)} %copy-done.7), channel_id=1, source_target_pairs={{0,4},{1,5},{2,6},{3,7},{4,0},{5,1},{6,2},{7,3},{8,12},{9,13},{10,... | collective-permute-start | bytes 221192 | tf_op jit(solution)/shard_map/ppermute | solution.py:335
  142.9 6.3 %collective-permute-start.30 = (bf16[4,96,96]{2,1,0:T(8,128)(2,1)}, bf16[4,96,96]{2,1,0:T(8,128)(2,1)S(1)}, u32[]{:S(2)}, u32[]{:S(2)}) collective-permute-start(bf16[4,96,96]{2,1,0:T(8,128)(2,1)} %shard_map.70), channel_id=1, source_target_pairs={{0,5},{1,4},{2,7},{3,6},{4,1},{5,0},{6,3},{7,2},{8,13},{9,12},{10,... | collective-permute-start | bytes 221192 | tf_op jit(solution)/shard_map/ppermute | solution.py:335
  149.3 5.5 %collective-permute-start.31 = (bf16[4,96,96]{2,1,0:T(8,128)(2,1)S(1)}, bf16[4,96,96]{2,1,0:T(8,128)(2,1)S(1)}, u32[]{:S(2)}, u32[]{:S(2)}) collective-permute-start(bf16[4,96,96]{2,1,0:T(8,128)(2,1)S(1)} %add_convert_fusion), channel_id=1, source_target_pairs={{0,64},{64,128},{128,192},{192,0},{1,65},{65,129},{129,193},{193,1... | collective-permute-start | bytes 221192 | tf_op jit(solution)/shard_map/ppermute | solution.py:341
  150.6 7.3 %collective-permute-start.32 = (bf16[4,96,96]{2,1,0:T(8,128)(2,1)S(1)}, bf16[4,96,96]{2,1,0:T(8,128)(2,1)S(1)}, u32[]{:S(2)}, u32[]{:S(2)}) collective-permute-start(bf16[4,96,96]{2,1,0:T(8,128)(2,1)S(1)} %add_convert_fusion), channel_id=1, source_target_pairs={{0,128},{64,192},{128,0},{192,64},{1,129},{65,193},{129,1},{193,65... | collective-permute-start | bytes 221192 | tf_op jit(solution)/shard_map/ppermute | solution.py:341
  153.2 4.6 %collective-permute-start.33 = (bf16[4,96,96]{2,1,0:T(8,128)(2,1)S(1)}, bf16[4,96,96]{2,1,0:T(8,128)(2,1)S(1)}, u32[]{:S(2)}, u32[]{:S(2)}) collective-permute-start(bf16[4,96,96]{2,1,0:T(8,128)(2,1)S(1)} %add_convert_fusion), channel_id=1, source_target_pairs={{0,192},{64,0},{128,64},{192,128},{1,193},{65,1},{129,65},{193,129... | collective-permute-start | bytes 221192 | tf_op jit(solution)/shard_map/ppermute | solution.py:341
Sparse Core Ops, SparseCore 0:
  9.8 99.5 all-gather.1

commit v7 on v6

--- a/solution.py
+++ b/solution.py
@@ -293,8 +293,8 @@
     held = held.reshape(NY * NZ, PIECE, CHANNELS)
     held, chunks[2], chunks[3] = lax.optimization_barrier((held, chunks[2], chunks[3]))
     quarters = [held] + [lax.ppermute(held, "rep", rep_perm(d)) for d in range(1, NX)]
-    quarters[2], chunks[4], chunks[5] = lax.optimization_barrier(
-        (quarters[2], chunks[4], chunks[5])
+    quarters[1], chunks[4], chunks[5] = lax.optimization_barrier(
+        (quarters[1], chunks[4], chunks[5])
     )
     quarters += [lax.ppermute(quarter, "ep", ep_perm(0, 0, 1)) for quarter in quarters]
     held = jnp.concatenate(quarters, 0)

time: 167 us -> 174 us (1.042)
  starting transfers between devices: 52.2 us -> 56.3 us
  waiting for transfers between devices: 46.5 us -> 49.2 us
    ppermute x3, waiting for transfers between devices: 0.01 us -> 19.3 us  [per_device(): lax.ppermute(held, 'ep', ep_perm(0, d, 0))]
    ppermute x7, waiting for transfers between devices: 18.6 us -> 0.32 us  [per_device(): lax.ppermute(part, 'ep', ep_perm(0, d, dc))]
    ppermute x7, starting transfers between devices: 10.9 us -> 16.2 us  [per_device(): lax.ppermute(part, 'ep', ep_perm(0, d, dc))]
    ppermute x3, waiting for transfers between devices: 8.63 us -> 11.8 us  [per_device(): lax.ppermute(held, 'rep', rep_perm(d))]
    ppermute x4, starting transfers between devices: 3.09 us -> 6.16 us  [per_device(): lax.ppermute(quarter, 'ep', ep_perm(0, 0, 1))]
    ppermute x7, starting transfers between devices: 10.9 us -> 8.3 us  [per_device(): part = lax.ppermute(part, 'ep', ep_perm(0, -d, dc))]
    ppermute x7, waiting for transfers between devices: 6.26 us -> 4.48 us  [per_device(): part = lax.ppermute(part, 'ep', ep_perm(0, -d, dc))]
  transfers between devices with their start and end apart: 35 -> 35, of which waited for: 12 -> 11; matrix products, arithmetic and copies ran while one was open for 18% -> 17% of each run, Pallas kernels for 11% -> 10%
where the time goes in v7:
time: 174 us; the launch traced here: 172 us
  starting transfers between devices  56.3 us (32%)
  waiting for transfers between devices  49.2 us (28%)
  local copies, waits for them, and re-layouts  22.8 us (13%)
  between operations  18 us (10%)
  Pallas kernels  17.8 us (10%)
  other arithmetic  7.82 us (4%)
    ppermute x3, waiting for transfers between devices, per_device(): lax.ppermute(held, 'ep', ep_perm(0, d, 0))  19.3 us
    ppermute x7, starting transfers between devices, per_device(): lax.ppermute(part, 'ep', ep_perm(0, d, dc))  16.2 us
    ppermute x3, waiting for transfers between devices, per_device(): lax.ppermute(held, 'rep', rep_perm(d))  11.8 us
    pallas_call x2, Pallas kernels, weight_grads(): pl.pallas_call(functools.partial(weight_kernel, chunks), out_shape=[jax.S...  11.7 us
    ppermute x3, starting transfers between devices, per_device(): down = lax.ppermute(down, 'ep', ep_perm(-1, 0, 0))  9.5 us
    ppermute x4, waiting for transfers between devices, per_device(): up = lax.ppermute(up, 'ep', ep_perm(1, 0, 0))  8.81 us
    dynamic_slice x2, local copies, waits for them, and re-layouts, sent(): lax.dynamic_slice(kept, (0, (y + d) % NY, c ^ dc, 0, 0, 0), (NZ, 1, 1, 2,...  8.66 us
    ppermute x7, starting transfers between devices, per_device(): part = lax.ppermute(part, 'ep', ep_perm(0, -d, dc))  8.3 us
  transfers between devices with their start and end apart: 35, of which 11 were waited for; matrix products, arithmetic and copies ran while one was open for 17% of the time, Pallas kernels for 10%

profile of v7, /device:TPU:1, one launch (start us, length us, event | category | flops | bytes accessed | tf_op | source)
XLA Modules:
  0.0 172.0 jit_solution(11622699044882536789)
XLA Ops:
  7.2 0.7 all-gather.2.cloned.1.call-update
  8.0 3.1 %constant_dynamic-slice_fusion.6 = (bf16[8,1,1,2,128,256]{5,4,3,2,1,0:T(8,128)(2,1)}, bf16[8,1,1,2,128,256]{5,4,3,2,1,0:T(8,128)(2,1)}) fusion(bf16[8,4,2,2,128,256]{5,4,3,2,1,0:T(8,128)(2,1)} %bitcast.58, s32[]{:T(128)S(6)} %select_n.250, s32[]{:T(128)S(6)} %select_n.248, s32[]{:T(128)S(6)} %select_n.247), kind=kLoop, calls=%fused_computation.72 | loop fusion | bytes 4194316 | tf_op jit(solution)/shard_map/dynamic_slice | solution.py:256
  12.0 2.5 %collective-permute-start = (bf16[96,128]{1,0:T(8,128)(2,1)S(1)}, bf16[96,128]{1,0:T(8,128)(2,1)S(1)}, u32[]{:S(2)}, u32[]{:S(2)}) collective-permute-start(bf16[96,128]{1,0:T(8,128)(2,1)S(1)} %pad_maximum_fusion.1), channel_id=1, source_target_pairs={{0,8},{1,9},{2,10},{3,11},{4,12},{5,13},{6,14},{7,15},{8,16},{9,17... | collective-permute-start | bytes 73736 | tf_op jit(solution)/shard_map/ppermute | solution.py:279
  14.6 4.0 %collective-permute-start.4 = (bf16[96,128]{1,0:T(8,128)(2,1)S(1)}, bf16[96,128]{1,0:T(8,128)(2,1)S(1)}, u32[]{:S(2)}, u32[]{:S(2)}) collective-permute-start(bf16[96,128]{1,0:T(8,128)(2,1)S(1)} %pad_maximum_fusion.1), channel_id=1, source_target_pairs={{0,56},{1,57},{2,58},{3,59},{4,60},{5,61},{6,62},{7,63},{8,0},{9,1... | collective-permute-start | bytes 73736 | tf_op jit(solution)/shard_map/ppermute | solution.py:282
  18.6 1.3 collective-permute-start.10
  19.9 1.4 collective-permute-start.11
  21.8 5.6 %constant_dynamic-slice_fusion = (bf16[8,1,1,2,128,256]{5,4,3,0,2,1:T(8,128)(2,1)}, bf16[8,1,1,2,128,256]{5,4,3,0,2,1:T(8,128)(2,1)}, bf16[8,1,1,2,128,256]{5,4,...) fusion(s32[]{:T(128)S(6)} %select_n.253, ...), kind=kLoop, calls=%fused_computation.66 | loop fusion | bytes 12582936 | tf_op jit(solution)/shard_map/dynamic_slice | solution.py:256
  28.3 2.7 %collective-permute-start.5 = (bf16[96,128]{1,0:T(8,128)(2,1)S(1)}, bf16[96,128]{1,0:T(8,128)(2,1)S(1)}, u32[]{:S(2)}, u32[]{:S(2)}) collective-permute-start(bf16[96,128]{1,0:T(8,128)(2,1)S(1)} %collective-permute-done.4), channel_id=1, source_target_pairs={{0,56},{1,57},{2,58},{3,59},{4,60},{5,61},{6,62},{7,63},{8,0},{9,1... | collective-permute-start | bytes 73736 | tf_op jit(solution)/shard_map/ppermute | solution.py:282
  31.0 2.0 %collective-permute-done.1 = bf16[96,128]{1,0:T(8,128)(2,1)S(1)} collective-permute-done((bf16[96,128]{1,0:T(8,128)(2,1)S(1)}, bf16[96,128]{1,0:T(8,128)(2,1)S(1)}, u32[]{:S(2)}, u32[]{:S(2)}) %collective-permute-start.1) | collective-permute-done | bytes 24608 | tf_op jit(solution)/shard_map/ppermute | solution.py:279
  33.0 2.7 %collective-permute-start.6 = (bf16[96,128]{1,0:T(8,128)(2,1)S(1)}, bf16[96,128]{1,0:T(8,128)(2,1)S(1)}, u32[]{:S(2)}, u32[]{:S(2)}) collective-permute-start(bf16[96,128]{1,0:T(8,128)(2,1)S(1)} %collective-permute-done.5), channel_id=1, source_target_pairs={{0,56},{1,57},{2,58},{3,59},{4,60},{5,61},{6,62},{7,63},{8,0},{9,1... | collective-permute-start | bytes 73736 | tf_op jit(solution)/shard_map/ppermute | solution.py:282
  35.8 2.0 %collective-permute-done.2 = bf16[96,128]{1,0:T(8,128)(2,1)S(1)} collective-permute-done((bf16[96,128]{1,0:T(8,128)(2,1)S(1)}, bf16[96,128]{1,0:T(8,128)(2,1)S(1)}, u32[]{:S(2)}, u32[]{:S(2)}) %collective-permute-start.2) | collective-permute-done | bytes 24608 | tf_op jit(solution)/shard_map/ppermute | solution.py:279
  37.8 4.8 %collective-permute-done.3 = bf16[96,128]{1,0:T(8,128)(2,1)S(1)} collective-permute-done((bf16[96,128]{1,0:T(8,128)(2,1)S(1)}, bf16[96,128]{1,0:T(8,128)(2,1)S(1)}, u32[]{:S(2)}, u32[]{:S(2)}) %collective-permute-start.3) | collective-permute-done | bytes 24608 | tf_op jit(solution)/shard_map/ppermute | solution.py:279
  42.7 2.6 %collective-permute-start.8 = (bf16[8,80,128]{2,1,0:T(8,128)(2,1)S(1)}, bf16[8,80,128]{2,1,0:T(8,128)(2,1)S(1)}, u32[]{:S(2)}, u32[]{:S(2)}) collective-permute-start(bf16[8,80,128]{2,1,0:T(8,128)(2,1)S(1)} %slice.48), channel_id=1, source_target_pairs={{0,4},{1,5},{2,6},{3,7},{4,0},{5,1},{6,2},{7,3},{8,12},{9,13},{10,... | collective-permute-start | bytes 491528 | tf_op jit(solution)/shard_map/ppermute | solution.py:292
  45.6 0.4 convert_reduce_fusion
  46.0 0.4 select_reduce_fusion.1
  46.9 4.8 %collective-permute-start.13 = (bf16[16,128,256]{2,1,0:T(8,128)(2,1)}, bf16[16,128,256]{2,1,0:T(8,128)(2,1)}, u32[]{:S(2)}, u32[]{:S(2)}) collective-permute-start(bf16[16,128,256]{2,1,0:T(8,128)(2,1)} %bitcast.14), channel_id=1, source_target_pairs={{0,3},{1,2},{2,5},{3,4},{4,7},{5,6},{6,1},{7,0},{8,11},{9,10},{10,... | collective-permute-start | bytes 3145736 | tf_op jit(solution)/shard_map/ppermute | solution.py:290
  51.9 1.2 convert_reduce_fusion.5
  53.3 0.7 collective-permute-start.14
  54.1 1.7 collective-permute-start.9
  55.9 0.6 slice.41
  59.1 0.6 slice.53
  60.4 0.7 copy.118
  61.4 19.3 %collective-permute-done.9 = bf16[8,80,128]{2,1,0:T(8,128)(2,1)S(1)} collective-permute-done((bf16[8,80,128]{2,1,0:T(8,128)(2,1)S(1)}, bf16[8,80,128]{2,1,0:T(8,128)(2,1)S(1)}, u32[]{:S(2)}, u32[]{:S(2)}) %collective-permute-start.9) | collective-permute-done | bytes 163872 | tf_op jit(solution)/shard_map/ppermute | solution.py:292
  80.9 1.3 collective-permute-start.12
  82.3 0.5 fusion.16
  82.9 2.5 %collective-permute-start.15 = (bf16[32,80,128]{2,1,0:T(8,128)(2,1)S(1)}, bf16[32,80,128]{2,1,0:T(8,128)(2,1)}, u32[]{:S(2)}, u32[]{:S(2)}) collective-permute-start(bf16[32,80,128]{2,1,0:T(8,128)(2,1)S(1)} %bitcast.63), channel_id=1, source_target_pairs={{0,128},{64,192},{128,0},{192,64},{1,129},{65,193},{129,1},{193,65... | collective-permute-start | bytes 1966088 | tf_op jit(solution)/shard_map/ppermute | solution.py:295
  85.5 0.7 copy.123
  86.4 0.7 copy.120
  87.2 0.7 copy.122
  87.9 0.7 copy.121
  88.7 1.2 collective-permute-start.16
  89.9 2.3 %collective-permute-start.17 = (bf16[32,80,128]{2,1,0:T(8,128)(2,1)S(1)}, bf16[32,80,128]{2,1,0:T(8,128)(2,1)}, u32[]{:S(2)}, u32[]{:S(2)}) collective-permute-start(bf16[32,80,128]{2,1,0:T(8,128)(2,1)S(1)} %bitcast.65), channel_id=1, source_target_pairs={{0,1},{1,0},{2,3},{3,2},{4,5},{5,4},{6,7},{7,6},{8,9},{9,8},{10,11... | collective-permute-start | bytes 1966088 | tf_op jit(solution)/shard_map/ppermute | solution.py:299
  92.3 2.4 %collective-permute-start.21 = (bf16[16,128,256]{2,1,0:T(8,128)(2,1)}, bf16[16,128,256]{2,1,0:T(8,128)(2,1)}, u32[]{:S(2)}, u32[]{:S(2)}) collective-permute-start(bf16[16,128,256]{2,1,0:T(8,128)(2,1)} %bitcast.69), channel_id=1, source_target_pairs={{0,4},{1,5},{2,6},{3,7},{4,0},{5,1},{6,2},{7,3},{8,12},{9,13},{10,... | collective-permute-start | bytes 3145736 | tf_op jit(solution)/shard_map/ppermute | solution.py:290
  94.7 2.4 %collective-permute-done.12 = bf16[32,80,128]{2,1,0:T(8,128)(2,1)S(1)} collective-permute-done((bf16[32,80,128]{2,1,0:T(8,128)(2,1)S(1)}, bf16[32,80,128]{2,1,0:T(8,128)(2,1)S(1)}, u32[]{:S(2)}, u32[]{:S(2)}) %collective-permute-start.12) | collective-permute-done | bytes 655392 | tf_op jit(solution)/shard_map/ppermute | solution.py:295
  97.1 3.2 %collective-permute-start.18 = (bf16[32,80,128]{2,1,0:T(8,128)(2,1)S(1)}, bf16[32,80,128]{2,1,0:T(8,128)(2,1)}, u32[]{:S(2)}, u32[]{:S(2)}) collective-permute-start(bf16[32,80,128]{2,1,0:T(8,128)(2,1)S(1)} %collective-permute-done.12), channel_id=1, source_target_pairs={{0,1},{1,0},{2,3},{3,2},{4,5},{5,4},{6,7},{7,6},{8,9},{9,8},{10,11... | collective-permute-start | bytes 1966088 | tf_op jit(solution)/shard_map/ppermute | solution.py:299
  100.7 0.6 select_reduce_fusion.6.gate_of
  101.3 1.4 select_reduce_fusion.2.gate_of
  102.7 9.4 %collective-permute-done.15 = bf16[32,80,128]{2,1,0:T(8,128)(2,1)} collective-permute-done((bf16[32,80,128]{2,1,0:T(8,128)(2,1)S(1)}, bf16[32,80,128]{2,1,0:T(8,128)(2,1)}, u32[]{:S(2)}, u32[]{:S(2)}) %collective-permute-start.15) | collective-permute-done | bytes 655392 | tf_op jit(solution)/shard_map/ppermute | solution.py:295
  112.1 2.4 %collective-permute-start.22 = (bf16[16,128,256]{2,1,0:T(8,128)(2,1)}, bf16[16,128,256]{2,1,0:T(8,128)(2,1)}, u32[]{:S(2)}, u32[]{:S(2)}) collective-permute-start(bf16[16,128,256]{2,1,0:T(8,128)(2,1)} %bitcast.68), channel_id=1, source_target_pairs={{0,1},{1,0},{2,3},{3,2},{4,5},{5,4},{6,7},{7,6},{8,9},{9,8},{10,11... | collective-permute-start | bytes 3145736 | tf_op jit(solution)/shard_map/ppermute | solution.py:290
  114.5 0.7 pad_add_fusion.2.plan
  115.2 3.1 %collective-permute-start.29 = (bf16[16,128,256]{2,1,0:T(8,128)(2,1)}, bf16[16,128,256]{2,1,0:T(8,128)(2,1)}, u32[]{:S(2)}, u32[]{:S(2)}) collective-permute-start(bf16[16,128,256]{2,1,0:T(8,128)(2,1)} %bitcast.67), channel_id=1, source_target_pairs={{0,5},{1,4},{2,7},{3,6},{4,1},{5,0},{6,3},{7,2},{8,13},{9,12},{10,... | collective-permute-start | bytes 3145736 | tf_op jit(solution)/shard_map/ppermute | solution.py:290
  118.4 0.5 collective-permute-start.19
  119.1 1.2 constant_dynamic-update-slice_fusion.13
  120.3 1.2 constant_dynamic-update-slice_fusion.12
  121.5 1.2 constant_dynamic-update-slice_fusion.11
  122.7 1.2 constant_dynamic-update-slice_fusion.10
  124.1 6.1 %shard_map.68 = bf16[16,128,256]{2,1,0:T(8,128)(2,1)} custom-call(s32[128]{0:T(128)S(1)} %add.346.place_ref, f32[32]{0:T(128)S(1)} %reshape.729.gate_ref, bf16[16,128,256]{2,1,0:T(8,128)(2,1)S(1)} %copy-done, bf16[256,80,128]{2,1,0:T(8,128)(2,1)S(1)} %constant_dynamic-update-slice_fusion.8.weight_ref), custom_call_target="tpu_custom_call" | custom-call | flops 1 | bytes 1 | tf_op jit(solution)/shard_map/pallas_call | solution.py:76
  130.2 7.8 %shard_map.69 = (bf16[4,96,96]{2,1,0:T(8,128)(2,1)}, bf16[4,96,96]{2,1,0:T(8,128)(2,1)}, bf16[4,96,96]{2,1,0:T(8,128)(2,1)}, bf16[4,96,96]{2,1,0:T(8,128)(2,1)},...) custom-call(s32[291]{0:T(512)} %pad_add_fusion.2.plan, ...), custom_call_target="tpu_custom_call" | custom-call | flops 1 | bytes 1 | tf_op jit(solution)/shard_map/pallas_call | solution.py:221
  138.5 0.7 pad_add_fusion.3.plan
  139.2 1.4 collective-permute-start.25
  140.6 1.6 collective-permute-start.26
  142.5 1.1 collective-permute-start.27
  143.7 3.9 %shard_map.70 = bf16[4,96,96]{2,1,0:T(8,128)(2,1)} custom-call(s32[51]{0:T(128)} %pad_add_fusion.3.plan, f32[20]{0:T(128)} %select_reduce_fusion.6.gate_of, bf16[128,128,256]{2,1,0:T(8,128)(2,1)} %all-gather.2.cloned.1.call-done.grads, bf16[16,128,256]{2,1,0:T(8,128)(2,1)} %collective-permute-done.29.refs_0_), custom_call_target="tpu_custom_call" | custom-call | flops 1 | bytes 1 | tf_op jit(solution)/shard_map/pallas_call | solution.py:221
  147.5 1.1 collective-permute-start.28
  148.7 2.6 %collective-permute-start.30 = (bf16[4,96,96]{2,1,0:T(8,128)(2,1)}, bf16[4,96,96]{2,1,0:T(8,128)(2,1)S(1)}, u32[]{:S(2)}, u32[]{:S(2)}) collective-permute-start(bf16[4,96,96]{2,1,0:T(8,128)(2,1)} %shard_map.70), channel_id=1, source_target_pairs={{0,5},{1,4},{2,7},{3,6},{4,1},{5,0},{6,3},{7,2},{8,13},{9,12},{10,... | collective-permute-start | bytes 221192 | tf_op jit(solution)/shard_map/ppermute | solution.py:335
  151.3 1.7 collective-permute-done.28
  153.0 2.8 %collective-permute-done.30 = bf16[4,96,96]{2,1,0:T(8,128)(2,1)S(1)} collective-permute-done((bf16[4,96,96]{2,1,0:T(8,128)(2,1)}, bf16[4,96,96]{2,1,0:T(8,128)(2,1)S(1)}, u32[]{:S(2)}, u32[]{:S(2)}) %collective-permute-start.30) | collective-permute-done | bytes 73760 | tf_op jit(solution)/shard_map/ppermute | solution.py:335
  155.9 1.7 collective-permute-start.31
  157.6 1.7 collective-permute-start.32
  159.3 0.8 collective-permute-start.33
  160.1 1.3 collective-permute-done.31
  161.4 2.5 %collective-permute-done.32 = bf16[4,96,96]{2,1,0:T(8,128)(2,1)S(1)} collective-permute-done((bf16[4,96,96]{2,1,0:T(8,128)(2,1)S(1)}, bf16[4,96,96]{2,1,0:T(8,128)(2,1)S(1)}, u32[]{:S(2)}, u32[]{:S(2)}) %collective-permute-start.32) | collective-permute-done | bytes 73760 | tf_op jit(solution)/shard_map/ppermute | solution.py:341
  164.0 0.3 reshape.727
  164.3 0.9 copy.124
  (129 shorter events, 6.6 us)
Async XLA Ops:
  7.2 3.9 %copy-start.3 = (bf16[1,9,4,32,32]{4,3,2,1,0:T(8,128)(2,1)S(1)}, bf16[1,9,4,32,32]{4,3,2,1,0:T(8,128)(2,1)}, u32[]{:S(2)}) copy-start(bf16[1,9,4,32,32]{4,3,2,1,0:T(8,128)(2,1)} %param.9) | copy-start | bytes 221188
  7.2 4.3 %copy-start.6 = (s32[16,2]{0,1:T(2,128)S(1)}, s32[16,2]{0,1:T(2,128)}, u32[]{:S(2)}) copy-start(s32[16,2]{0,1:T(2,128)} %param.6) | copy-start | bytes 388
  7.2 4.5 %copy-start.5 = (bf16[16,2]{0,1:T(2,128)(2,1)S(1)}, bf16[16,2]{0,1:T(2,128)(2,1)}, u32[]{:S(2)}) copy-start(bf16[16,2]{0,1:T(2,128)(2,1)} %param.7) | copy-start | bytes 196
  7.2 123.0 %all-gather.2.cloned.1.call-start = ((), (), s32[]{:S(2)}) async-start(), calls=%async_computation | async-start | bytes 9437184 | tf_op jit(solution)/shard_map/all_gather | solution.py:250
  12.0 16.1 %collective-permute-start = (bf16[96,128]{1,0:T(8,128)(2,1)S(1)}, bf16[96,128]{1,0:T(8,128)(2,1)S(1)}, u32[]{:S(2)}, u32[]{:S(2)}) collective-permute-start(bf16[96,128]{1,0:T(8,128)(2,1)S(1)} %pad_maximum_fusion.1), channel_id=1, source_target_pairs={{0,8},{1,9},{2,10},{3,11},{4,12},{5,13},{6,14},{7,15},{8,16},{9,17... | collective-permute-start | bytes 73736 | tf_op jit(solution)/shard_map/ppermute | solution.py:279
  14.6 13.7 %collective-permute-start.4 = (bf16[96,128]{1,0:T(8,128)(2,1)S(1)}, bf16[96,128]{1,0:T(8,128)(2,1)S(1)}, u32[]{:S(2)}, u32[]{:S(2)}) collective-permute-start(bf16[96,128]{1,0:T(8,128)(2,1)S(1)} %pad_maximum_fusion.1), channel_id=1, source_target_pairs={{0,56},{1,57},{2,58},{3,59},{4,60},{5,61},{6,62},{7,63},{8,0},{9,1... | collective-permute-start | bytes 73736 | tf_op jit(solution)/shard_map/ppermute | solution.py:282
  18.6 62.3 %collective-permute-start.10 = (bf16[16,128,256]{2,1,0:T(8,128)(2,1)}, bf16[16,128,256]{2,1,0:T(8,128)(2,1)S(1)}, u32[]{:S(2)}, u32[]{:S(2)}) collective-permute-start(bf16[16,128,256]{2,1,0:T(8,128)(2,1)} %bitcast.1), channel_id=1, source_target_pairs={{0,2},{1,3},{2,4},{3,5},{4,6},{5,7},{6,0},{7,1},{8,10},{9,11},{10,... | collective-permute-start | bytes 3145736 | tf_op jit(solution)/shard_map/ppermute | solution.py:290
  19.9 61.0 %collective-permute-start.11 = (bf16[16,128,256]{2,1,0:T(8,128)(2,1)}, bf16[16,128,256]{2,1,0:T(8,128)(2,1)S(1)}, u32[]{:S(2)}, u32[]{:S(2)}) collective-permute-start(bf16[16,128,256]{2,1,0:T(8,128)(2,1)} %bitcast.2), channel_id=1, source_target_pairs={{0,6},{1,7},{2,0},{3,1},{4,2},{5,3},{6,4},{7,5},{8,14},{9,15},{10,... | collective-permute-start | bytes 3145736 | tf_op jit(solution)/shard_map/ppermute | solution.py:290
  28.1 4.9 %collective-permute-start.1 = (bf16[96,128]{1,0:T(8,128)(2,1)S(1)}, bf16[96,128]{1,0:T(8,128)(2,1)S(1)}, u32[]{:S(2)}, u32[]{:S(2)}) collective-permute-start(bf16[96,128]{1,0:T(8,128)(2,1)S(1)} %collective-permute-done), channel_id=1, source_target_pairs={{0,8},{1,9},{2,10},{3,11},{4,12},{5,13},{6,14},{7,15},{8,16},{9,17... | collective-permute-start | bytes 73736 | tf_op jit(solution)/shard_map/ppermute | solution.py:279
  28.3 4.8 %collective-permute-start.5 = (bf16[96,128]{1,0:T(8,128)(2,1)S(1)}, bf16[96,128]{1,0:T(8,128)(2,1)S(1)}, u32[]{:S(2)}, u32[]{:S(2)}) collective-permute-start(bf16[96,128]{1,0:T(8,128)(2,1)S(1)} %collective-permute-done.4), channel_id=1, source_target_pairs={{0,56},{1,57},{2,58},{3,59},{4,60},{5,61},{6,62},{7,63},{8,0},{9,1... | collective-permute-start | bytes 73736 | tf_op jit(solution)/shard_map/ppermute | solution.py:282
  33.0 4.8 %collective-permute-start.2 = (bf16[96,128]{1,0:T(8,128)(2,1)S(1)}, bf16[96,128]{1,0:T(8,128)(2,1)S(1)}, u32[]{:S(2)}, u32[]{:S(2)}) collective-permute-start(bf16[96,128]{1,0:T(8,128)(2,1)S(1)} %collective-permute-done.1), channel_id=1, source_target_pairs={{0,8},{1,9},{2,10},{3,11},{4,12},{5,13},{6,14},{7,15},{8,16},{9,17... | collective-permute-start | bytes 73736 | tf_op jit(solution)/shard_map/ppermute | solution.py:279
  33.0 9.6 %collective-permute-start.6 = (bf16[96,128]{1,0:T(8,128)(2,1)S(1)}, bf16[96,128]{1,0:T(8,128)(2,1)S(1)}, u32[]{:S(2)}, u32[]{:S(2)}) collective-permute-start(bf16[96,128]{1,0:T(8,128)(2,1)S(1)} %collective-permute-done.5), channel_id=1, source_target_pairs={{0,56},{1,57},{2,58},{3,59},{4,60},{5,61},{6,62},{7,63},{8,0},{9,1... | collective-permute-start | bytes 73736 | tf_op jit(solution)/shard_map/ppermute | solution.py:282
  37.8 4.8 %collective-permute-start.3 = (bf16[96,128]{1,0:T(8,128)(2,1)S(1)}, bf16[96,128]{1,0:T(8,128)(2,1)S(1)}, u32[]{:S(2)}, u32[]{:S(2)}) collective-permute-start(bf16[96,128]{1,0:T(8,128)(2,1)S(1)} %collective-permute-done.2), channel_id=1, source_target_pairs={{0,8},{1,9},{2,10},{3,11},{4,12},{5,13},{6,14},{7,15},{8,16},{9,17... | collective-permute-start | bytes 73736 | tf_op jit(solution)/shard_map/ppermute | solution.py:279
  42.6 10.6 %collective-permute-start.7 = (bf16[8,80,128]{2,1,0:T(8,128)(2,1)S(1)}, bf16[8,80,128]{2,1,0:T(8,128)(2,1)S(1)}, u32[]{:S(2)}, u32[]{:S(2)}) collective-permute-start(bf16[8,80,128]{2,1,0:T(8,128)(2,1)S(1)} %slice.48), channel_id=1, source_target_pairs={{0,2},{1,3},{2,4},{3,5},{4,6},{5,7},{6,0},{7,1},{8,10},{9,11},{10,... | collective-permute-start | bytes 491528 | tf_op jit(solution)/shard_map/ppermute | solution.py:292
  42.7 11.4 %collective-permute-start.8 = (bf16[8,80,128]{2,1,0:T(8,128)(2,1)S(1)}, bf16[8,80,128]{2,1,0:T(8,128)(2,1)S(1)}, u32[]{:S(2)}, u32[]{:S(2)}) collective-permute-start(bf16[8,80,128]{2,1,0:T(8,128)(2,1)S(1)} %slice.48), channel_id=1, source_target_pairs={{0,4},{1,5},{2,6},{3,7},{4,0},{5,1},{6,2},{7,3},{8,12},{9,13},{10,... | collective-permute-start | bytes 491528 | tf_op jit(solution)/shard_map/ppermute | solution.py:292
  46.9 43.0 %collective-permute-start.13 = (bf16[16,128,256]{2,1,0:T(8,128)(2,1)}, bf16[16,128,256]{2,1,0:T(8,128)(2,1)}, u32[]{:S(2)}, u32[]{:S(2)}) collective-permute-start(bf16[16,128,256]{2,1,0:T(8,128)(2,1)} %bitcast.14), channel_id=1, source_target_pairs={{0,3},{1,2},{2,5},{3,4},{4,7},{5,6},{6,1},{7,0},{8,11},{9,10},{10,... | collective-permute-start | bytes 3145736 | tf_op jit(solution)/shard_map/ppermute | solution.py:290
  53.3 39.0 %collective-permute-start.14 = (bf16[16,128,256]{2,1,0:T(8,128)(2,1)}, bf16[16,128,256]{2,1,0:T(8,128)(2,1)}, u32[]{:S(2)}, u32[]{:S(2)}) collective-permute-start(bf16[16,128,256]{2,1,0:T(8,128)(2,1)} %bitcast.15), channel_id=1, source_target_pairs={{0,7},{1,6},{2,1},{3,0},{4,3},{5,2},{6,5},{7,4},{8,15},{9,14},{10,... | collective-permute-start | bytes 3145736 | tf_op jit(solution)/shard_map/ppermute | solution.py:290
  54.1 26.7 %collective-permute-start.9 = (bf16[8,80,128]{2,1,0:T(8,128)(2,1)S(1)}, bf16[8,80,128]{2,1,0:T(8,128)(2,1)S(1)}, u32[]{:S(2)}, u32[]{:S(2)}) collective-permute-start(bf16[8,80,128]{2,1,0:T(8,128)(2,1)S(1)} %slice.48), channel_id=1, source_target_pairs={{0,6},{1,7},{2,0},{3,1},{4,2},{5,3},{6,4},{7,5},{8,14},{9,15},{10,... | collective-permute-start | bytes 491528 | tf_op jit(solution)/shard_map/ppermute | solution.py:292
  80.9 43.2 %copy-start.1 = (bf16[16,128,256]{2,1,0:T(8,128)(2,1)}, bf16[16,128,256]{2,1,0:T(8,128)(2,1)S(1)}, u32[]{:S(2)}) copy-start(bf16[16,128,256]{2,1,0:T(8,128)(2,1)S(1)} %collective-permute-done.10.refs_2_) | copy-start | bytes 3145732
  80.9 43.2 %copy-start.2 = (bf16[16,128,256]{2,1,0:T(8,128)(2,1)}, bf16[16,128,256]{2,1,0:T(8,128)(2,1)S(1)}, u32[]{:S(2)}) copy-start(bf16[16,128,256]{2,1,0:T(8,128)(2,1)S(1)} %collective-permute-done.11.refs_3_) | copy-start | bytes 3145732
  80.9 16.2 %collective-permute-start.12 = (bf16[32,80,128]{2,1,0:T(8,128)(2,1)S(1)}, bf16[32,80,128]{2,1,0:T(8,128)(2,1)S(1)}, u32[]{:S(2)}, u32[]{:S(2)}) collective-permute-start(bf16[32,80,128]{2,1,0:T(8,128)(2,1)S(1)} %bitcast.62), channel_id=1, source_target_pairs={{0,64},{64,128},{128,192},{192,0},{1,65},{65,129},{129,193},{193,1... | collective-permute-start | bytes 1966088 | tf_op jit(solution)/shard_map/ppermute | solution.py:295
  82.9 29.2 %collective-permute-start.15 = (bf16[32,80,128]{2,1,0:T(8,128)(2,1)S(1)}, bf16[32,80,128]{2,1,0:T(8,128)(2,1)}, u32[]{:S(2)}, u32[]{:S(2)}) collective-permute-start(bf16[32,80,128]{2,1,0:T(8,128)(2,1)S(1)} %bitcast.63), channel_id=1, source_target_pairs={{0,128},{64,192},{128,0},{192,64},{1,129},{65,193},{129,1},{193,65... | collective-permute-start | bytes 1966088 | tf_op jit(solution)/shard_map/ppermute | solution.py:295
  88.7 26.5 %collective-permute-start.16 = (bf16[32,80,128]{2,1,0:T(8,128)(2,1)S(1)}, bf16[32,80,128]{2,1,0:T(8,128)(2,1)}, u32[]{:S(2)}, u32[]{:S(2)}) collective-permute-start(bf16[32,80,128]{2,1,0:T(8,128)(2,1)S(1)} %bitcast.64), channel_id=1, source_target_pairs={{0,192},{64,0},{128,64},{192,128},{1,193},{65,1},{129,65},{193,129... | collective-permute-start | bytes 1966088 | tf_op jit(solution)/shard_map/ppermute | solution.py:295
  89.9 28.5 %collective-permute-start.17 = (bf16[32,80,128]{2,1,0:T(8,128)(2,1)S(1)}, bf16[32,80,128]{2,1,0:T(8,128)(2,1)}, u32[]{:S(2)}, u32[]{:S(2)}) collective-permute-start(bf16[32,80,128]{2,1,0:T(8,128)(2,1)S(1)} %bitcast.65), channel_id=1, source_target_pairs={{0,1},{1,0},{2,3},{3,2},{4,5},{5,4},{6,7},{7,6},{8,9},{9,8},{10,11... | collective-permute-start | bytes 1966088 | tf_op jit(solution)/shard_map/ppermute | solution.py:299
  92.3 31.8 %collective-permute-start.21 = (bf16[16,128,256]{2,1,0:T(8,128)(2,1)}, bf16[16,128,256]{2,1,0:T(8,128)(2,1)}, u32[]{:S(2)}, u32[]{:S(2)}) collective-permute-start(bf16[16,128,256]{2,1,0:T(8,128)(2,1)} %bitcast.69), channel_id=1, source_target_pairs={{0,4},{1,5},{2,6},{3,7},{4,0},{5,1},{6,2},{7,3},{8,12},{9,13},{10,... | collective-permute-start | bytes 3145736 | tf_op jit(solution)/shard_map/ppermute | solution.py:290
  97.1 21.9 %collective-permute-start.18 = (bf16[32,80,128]{2,1,0:T(8,128)(2,1)S(1)}, bf16[32,80,128]{2,1,0:T(8,128)(2,1)}, u32[]{:S(2)}, u32[]{:S(2)}) collective-permute-start(bf16[32,80,128]{2,1,0:T(8,128)(2,1)S(1)} %collective-permute-done.12), channel_id=1, source_target_pairs={{0,1},{1,0},{2,3},{3,2},{4,5},{5,4},{6,7},{7,6},{8,9},{9,8},{10,11... | collective-permute-start | bytes 1966088 | tf_op jit(solution)/shard_map/ppermute | solution.py:299
  112.1 18.1 %collective-permute-start.22 = (bf16[16,128,256]{2,1,0:T(8,128)(2,1)}, bf16[16,128,256]{2,1,0:T(8,128)(2,1)}, u32[]{:S(2)}, u32[]{:S(2)}) collective-permute-start(bf16[16,128,256]{2,1,0:T(8,128)(2,1)} %bitcast.68), channel_id=1, source_target_pairs={{0,1},{1,0},{2,3},{3,2},{4,5},{5,4},{6,7},{7,6},{8,9},{9,8},{10,11... | collective-permute-start | bytes 3145736 | tf_op jit(solution)/shard_map/ppermute | solution.py:290
  115.2 8.9 %copy-start = (bf16[16,128,256]{2,1,0:T(8,128)(2,1)S(1)}, bf16[16,128,256]{2,1,0:T(8,128)(2,1)}, u32[]{:S(2)}) copy-start(bf16[16,128,256]{2,1,0:T(8,128)(2,1)} %grad_ref.1) | copy-start | bytes 3145732
  115.2 27.3 %collective-permute-start.29 = (bf16[16,128,256]{2,1,0:T(8,128)(2,1)}, bf16[16,128,256]{2,1,0:T(8,128)(2,1)}, u32[]{:S(2)}, u32[]{:S(2)}) collective-permute-start(bf16[16,128,256]{2,1,0:T(8,128)(2,1)} %bitcast.67), channel_id=1, source_target_pairs={{0,5},{1,4},{2,7},{3,6},{4,1},{5,0},{6,3},{7,2},{8,13},{9,12},{10,... | collective-permute-start | bytes 3145736 | tf_op jit(solution)/shard_map/ppermute | solution.py:290
  118.4 5.5 %collective-permute-start.19 = (bf16[32,80,128]{2,1,0:T(8,128)(2,1)}, bf16[32,80,128]{2,1,0:T(8,128)(2,1)S(1)}, u32[]{:S(2)}, u32[]{:S(2)}) collective-permute-start(bf16[32,80,128]{2,1,0:T(8,128)(2,1)} %collective-permute-done.15), channel_id=1, source_target_pairs={{0,1},{1,0},{2,3},{3,2},{4,5},{5,4},{6,7},{7,6},{8,9},{9,8},{10,11... | collective-permute-start | bytes 1966088 | tf_op jit(solution)/shard_map/ppermute | solution.py:299
  118.9 5.0 %collective-permute-start.20 = (bf16[32,80,128]{2,1,0:T(8,128)(2,1)}, bf16[32,80,128]{2,1,0:T(8,128)(2,1)S(1)}, u32[]{:S(2)}, u32[]{:S(2)}) collective-permute-start(bf16[32,80,128]{2,1,0:T(8,128)(2,1)} %collective-permute-done.16), channel_id=1, source_target_pairs={{0,1},{1,0},{2,3},{3,2},{4,5},{5,4},{6,7},{7,6},{8,9},{9,8},{10,11... | collective-permute-start | bytes 1966088 | tf_op jit(solution)/shard_map/ppermute | solution.py:299
  138.1 9.5 %copy-start.7 = (bf16[4,96,96]{2,1,0:T(8,128)(2,1)S(1)}, bf16[4,96,96]{2,1,0:T(8,128)(2,1)}, u32[]{:S(2)}) copy-start(bf16[4,96,96]{2,1,0:T(8,128)(2,1)} %get-tuple-element.60) | copy-start | bytes 221188
  138.1 17.7 %copy-start.4 = (bf16[4,96,96]{2,1,0:T(8,128)(2,1)S(1)}, bf16[4,96,96]{2,1,0:T(8,128)(2,1)}, u32[]{:S(2)}) copy-start(bf16[4,96,96]{2,1,0:T(8,128)(2,1)} %get-tuple-element.54) | copy-start | bytes 221188
  138.1 9.4 %collective-permute-start.23 = (bf16[4,96,96]{2,1,0:T(8,128)(2,1)}, bf16[4,96,96]{2,1,0:T(8,128)(2,1)S(1)}, u32[]{:S(2)}, u32[]{:S(2)}) collective-permute-start(bf16[4,96,96]{2,1,0:T(8,128)(2,1)} %get-tuple-element.55), channel_id=1, source_target_pairs={{0,1},{1,0},{2,3},{3,2},{4,5},{5,4},{6,7},{7,6},{8,9},{9,8},{10,11... | collective-permute-start | bytes 221192 | tf_op jit(solution)/shard_map/ppermute | solution.py:335
  138.2 10.5 %collective-permute-start.24 = (bf16[4,96,96]{2,1,0:T(8,128)(2,1)}, bf16[4,96,96]{2,1,0:T(8,128)(2,1)S(1)}, u32[]{:S(2)}, u32[]{:S(2)}) collective-permute-start(bf16[4,96,96]{2,1,0:T(8,128)(2,1)} %get-tuple-element.56), channel_id=1, source_target_pairs={{0,6},{1,7},{2,0},{3,1},{4,2},{5,3},{6,4},{7,5},{8,14},{9,15},{10,... | collective-permute-start | bytes 221192 | tf_op jit(solution)/shard_map/ppermute | solution.py:335
  139.2 12.1 %collective-permute-start.25 = (bf16[4,96,96]{2,1,0:T(8,128)(2,1)}, bf16[4,96,96]{2,1,0:T(8,128)(2,1)S(1)}, u32[]{:S(2)}, u32[]{:S(2)}) collective-permute-start(bf16[4,96,96]{2,1,0:T(8,128)(2,1)} %get-tuple-element.57), channel_id=1, source_target_pairs={{0,2},{1,3},{2,4},{3,5},{4,6},{5,7},{6,0},{7,1},{8,10},{9,11},{10,... | collective-permute-start | bytes 221192 | tf_op jit(solution)/shard_map/ppermute | solution.py:335
  140.6 10.7 %collective-permute-start.26 = (bf16[4,96,96]{2,1,0:T(8,128)(2,1)}, bf16[4,96,96]{2,1,0:T(8,128)(2,1)S(1)}, u32[]{:S(2)}, u32[]{:S(2)}) collective-permute-start(bf16[4,96,96]{2,1,0:T(8,128)(2,1)} %get-tuple-element.58), channel_id=1, source_target_pairs={{0,7},{1,6},{2,1},{3,0},{4,3},{5,2},{6,5},{7,4},{8,15},{9,14},{10,... | collective-permute-start | bytes 221192 | tf_op jit(solution)/shard_map/ppermute | solution.py:335
  142.5 8.8 %collective-permute-start.27 = (bf16[4,96,96]{2,1,0:T(8,128)(2,1)}, bf16[4,96,96]{2,1,0:T(8,128)(2,1)S(1)}, u32[]{:S(2)}, u32[]{:S(2)}) collective-permute-start(bf16[4,96,96]{2,1,0:T(8,128)(2,1)} %get-tuple-element.59), channel_id=1, source_target_pairs={{0,3},{1,2},{2,5},{3,4},{4,7},{5,6},{6,1},{7,0},{8,11},{9,10},{10,... | collective-permute-start | bytes 221192 | tf_op jit(solution)/shard_map/ppermute | solution.py:335
  147.5 5.4 %collective-permute-start.28 = (bf16[4,96,96]{2,1,0:T(8,128)(2,1)S(1)}, bf16[4,96,96]{2,1,0:T(8,128)(2,1)S(1)}, u32[]{:S(2)}, u32[]{:S(2)}) collective-permute-start(bf16[4,96,96]{2,1,0:T(8,128)(2,1)S(1)} %copy-done.7), channel_id=1, source_target_pairs={{0,4},{1,5},{2,6},{3,7},{4,0},{5,1},{6,2},{7,3},{8,12},{9,13},{10,... | collective-permute-start | bytes 221192 | tf_op jit(solution)/shard_map/ppermute | solution.py:335
  148.7 7.1 %collective-permute-start.30 = (bf16[4,96,96]{2,1,0:T(8,128)(2,1)}, bf16[4,96,96]{2,1,0:T(8,128)(2,1)S(1)}, u32[]{:S(2)}, u32[]{:S(2)}) collective-permute-start(bf16[4,96,96]{2,1,0:T(8,128)(2,1)} %shard_map.70), channel_id=1, source_target_pairs={{0,5},{1,4},{2,7},{3,6},{4,1},{5,0},{6,3},{7,2},{8,13},{9,12},{10,... | collective-permute-start | bytes 221192 | tf_op jit(solution)/shard_map/ppermute | solution.py:335
  155.9 5.5 %collective-permute-start.31 = (bf16[4,96,96]{2,1,0:T(8,128)(2,1)S(1)}, bf16[4,96,96]{2,1,0:T(8,128)(2,1)S(1)}, u32[]{:S(2)}, u32[]{:S(2)}) collective-permute-start(bf16[4,96,96]{2,1,0:T(8,128)(2,1)S(1)} %add_convert_fusion), channel_id=1, source_target_pairs={{0,64},{64,128},{128,192},{192,0},{1,65},{65,129},{129,193},{193,1... | collective-permute-start | bytes 221192 | tf_op jit(solution)/shard_map/ppermute | solution.py:341
  157.6 6.3 %collective-permute-start.32 = (bf16[4,96,96]{2,1,0:T(8,128)(2,1)S(1)}, bf16[4,96,96]{2,1,0:T(8,128)(2,1)S(1)}, u32[]{:S(2)}, u32[]{:S(2)}) collective-permute-start(bf16[4,96,96]{2,1,0:T(8,128)(2,1)S(1)} %add_convert_fusion), channel_id=1, source_target_pairs={{0,128},{64,192},{128,0},{192,64},{1,129},{65,193},{129,1},{193,65... | collective-permute-start | bytes 221192 | tf_op jit(solution)/shard_map/ppermute | solution.py:341
  159.3 4.6 %collective-permute-start.33 = (bf16[4,96,96]{2,1,0:T(8,128)(2,1)S(1)}, bf16[4,96,96]{2,1,0:T(8,128)(2,1)S(1)}, u32[]{:S(2)}, u32[]{:S(2)}) collective-permute-start(bf16[4,96,96]{2,1,0:T(8,128)(2,1)S(1)} %add_convert_fusion), channel_id=1, source_target_pairs={{0,192},{64,0},{128,64},{192,128},{1,193},{65,1},{129,65},{193,129... | collective-permute-start | bytes 221192 | tf_op jit(solution)/shard_map/ppermute | solution.py:341
Sparse Core Ops, SparseCore 0:
  9.8 99.5 all-gather.1
